TPU v7x, 32 devices: a whole 2x2x4 slice. The times are simulated.
32 devices in a mesh: seq: 16 (over z, y, core), tp: 2 (over x).
Axes of the slice: x: 2, y: 2, z: 4, core: 2. Of those that a mesh axis runs over, the one named last changes fastest.
Arguments:
- tokens: bfloat16 [8192, 2880], P(('seq', 'tp')), may hold values from -24 to 24
- w_query: bfloat16 [2880, 4096], P('seq', 'tp')
- w_kv: bfloat16 [2880, 1024], P('seq', 'tp')
- w_out: bfloat16 [2880, 4096], P('seq', 'tp'), may hold values from -0.5 to 0.5
- sinks: float32 [64], P('tp'), may hold values from 1 to 6
Outputs:
- attn_out: bfloat16 [8192, 2880], P(('seq', 'tp'))
All inputs are finite; a program needn't handle non-finite values.
Results may differ from a plain program's by a relative error of at most 0.015.
Values may be sent and summed in bfloat16 or wider, within the bound.
No kernel may reach another device: no remote copies, remote signals or barrier semaphores. Data moves between devices by JAX's collectives and lax.ppermute only.
A program may use at most 128 MiB of HBM per device.

v0:
```python
import math

import jax
import jax.numpy as jnp
from jax import lax
from jax.sharding import PartitionSpec as P

HEAD_WIDTH = 64
WINDOW_KEYS = 128


rope_base = 150000.0


def from_behind(value, axis, by):
    devices = lax.axis_size(axis)
    pairs = [(i, i + by) for i in range(devices) if 0 <= i + by < devices]
    return lax.ppermute(value, axis, pairs)


def rotary(vectors, places):
    half_dim = vectors.shape[-1] // 2
    frequency = jnp.exp(
        jnp.arange(half_dim, dtype=jnp.float32) * (-2.0 * math.log(rope_base) / vectors.shape[-1])
    )
    angles = places.astype(jnp.float32)[:, None, None] * frequency[None, None, :]
    cosine = jnp.cos(angles)
    sine = jnp.sin(angles)
    lower_half = vectors[..., :half_dim]
    upper_half = vectors[..., half_dim:]
    return jnp.concatenate(
        [lower_half * cosine - upper_half * sine, upper_half * cosine + lower_half * sine], axis=-1
    )


def attend(query_rows, key_value_rows, sink_scores, query_pos, key_pos):
    key_part = key_value_rows[:, :, 0, :]
    value_part = key_value_rows[:, :, 1, :]
    scores = jnp.einsum(
        "qhgd,khd->hgqk", query_rows, key_part, preferred_element_type=jnp.float32
    ) * HEAD_WIDTH ** (-0.5)
    allowed = (
        (key_pos[None, :] <= query_pos[:, None])
        & (key_pos[None, :] > query_pos[:, None] - WINDOW_KEYS)
        & (key_pos[None, :] >= 0)
    )
    scores = jnp.where(allowed[None, None], scores, -jnp.inf)
    row_max = jnp.maximum(jnp.max(scores, axis=-1), sink_scores[:, :, None])
    exponent = jnp.exp(scores - row_max[..., None])
    denominator = jnp.sum(exponent, axis=-1) + jnp.exp(sink_scores[:, :, None] - row_max)
    weights = exponent.astype(jnp.bfloat16)
    mixture = jnp.einsum("hgqk,khd->qhgd", weights, value_part, preferred_element_type=jnp.float32)
    return (mixture / jnp.transpose(denominator, (2, 0, 1))[..., None]).astype(jnp.bfloat16)


def finish(kv_sum, places, kv_heads):
    split_key_value = kv_sum.reshape(kv_sum.shape[0], kv_heads, 2, HEAD_WIDTH)
    key_part = rotary(split_key_value[:, :, 0, :], places)
    return jnp.stack([key_part, split_key_value[:, :, 1, :]], axis=2).astype(jnp.bfloat16)


def body(tokens, w_query, w_kv, w_out, sinks):
    token_rows = lax.all_gather(tokens, "tp", axis=0, tiled=True)
    row_count = token_rows.shape[0]
    kv_width = w_kv.shape[1]
    kv_heads = kv_width // (2 * HEAD_WIDTH)
    q_width = w_query.shape[1]
    head_groups = q_width // HEAD_WIDTH // kv_heads
    start_pos = lax.axis_index("seq") * row_count
    query_pos = start_pos + jnp.arange(row_count, dtype=jnp.int32)
    key_pos = start_pos - WINDOW_KEYS + jnp.arange(row_count + WINDOW_KEYS, dtype=jnp.int32)
    query_sum = jnp.dot(
        token_rows,
        lax.all_gather(w_query, "seq", axis=0, tiled=True),
        preferred_element_type=jnp.float32,
    )
    kv_sum = jnp.dot(
        token_rows,
        lax.all_gather(w_kv, "seq", axis=0, tiled=True),
        preferred_element_type=jnp.float32,
    )
    query_rows = rotary(
        query_sum.reshape(row_count, kv_heads * head_groups, HEAD_WIDTH), query_pos
    ).astype(jnp.bfloat16)
    query_rows = query_rows.reshape(row_count, kv_heads, head_groups, HEAD_WIDTH)
    local_kv = finish(kv_sum, query_pos, kv_heads).reshape(row_count, kv_width)
    kv_tail = from_behind(local_kv[row_count - WINDOW_KEYS :], "seq", 1)
    key_value_rows = jnp.concatenate([kv_tail, local_kv], axis=0).reshape(
        row_count + WINDOW_KEYS, kv_heads, 2, HEAD_WIDTH
    )
    attended = attend(
        query_rows, key_value_rows, sinks.reshape(kv_heads, head_groups), query_pos, key_pos
    ).reshape(row_count, q_width)
    out_terms = lax.dot_general(
        attended,
        lax.all_gather(w_out, "seq", axis=0, tiled=True),
        (((1,), (1,)), ((), ())),
        preferred_element_type=jnp.float32,
    )
    result = lax.psum_scatter(out_terms.astype(jnp.bfloat16), "tp", scatter_dimension=0, tiled=True)
    return result


def solution(mesh):
    in_specs = (P(("seq", "tp"), None), P("seq", "tp"), P("seq", "tp"), P("seq", "tp"), P("tp"))
    out_specs = P(("seq", "tp"), None)
    return jax.shard_map(body, mesh=mesh, in_specs=in_specs, out_specs=out_specs, check_vma=False)
```

profile of v0, /device:TPU:0, one launch (start us, length us, event | category | flops | bytes accessed | tf_op | source)
XLA Modules:
  0.0 367.4 jit_solution(17835974666562924480)
XLA Ops:
  6.5 0.7 all-gather.10.cloned.1.call-update
  7.3 0.0 all-gather.8.cloned.1.call-start
  7.3 0.7 all-gather.8.cloned.1.call-update
  8.0 0.0 all-gather.12.cloned.1.call-start
  8.1 0.7 all-gather.12.cloned.1.call-update
  8.7 0.0 all-gather.14.cloned.1.call-start
  8.8 0.5 all-gather.14.cloned.1.call-update
  9.3 0.0 reduce-scatter.2.cloned.1.call-start
  9.4 0.7 max.16
  10.2 0.3 multiply_cosine_fusion
  10.5 46.6 %all-gather.10.cloned.1.call-done = bf16[16,180,512]{2,1,0:T(8,128)(2,1)} async-done(((bf16[1,180,512]{2,1,0:T(8,128)(2,1)}), bf16[16,180,512]{2,1,0:T(8,128)(2,1)}) %all-gather.10.cloned.1.call-update) | async-done | bytes 2949136 | tf_op jit(solution)/shard_map/all_gather | solution.py:79
  57.0 2.8 reshape.183
  59.8 40.1 %all-gather.8.cloned.1.call-done = bf16[512,2880]{0,1:T(8,128)(2,1)} async-done(((bf16[256,2880]{0,1:T(8,128)(2,1)}), bf16[512,2880]{0,1:T(8,128)(2,1)}) %all-gather.8.cloned.1.call-update) | async-done | bytes 2949136 | tf_op jit(solution)/shard_map/all_gather | solution.py:63
  100.0 3.7 fusion.18
  103.7 0.1 subtract_convert_fusion.1
  103.9 1.7 collective-permute-start
  105.6 0.4 and_and_fusion
  106.0 0.6 collective-permute-done
  106.6 0.1 maximum_maximum_fusion
  106.7 93.2 %all-gather.12.cloned.1.call-done = bf16[16,180,2048]{2,1,0:T(8,128)(2,1)} async-done(((bf16[1,180,2048]{2,1,0:T(8,128)(2,1)}), bf16[16,180,2048]{2,1,0:T(8,128)(2,1)}) %all-gather.12.cloned.1.call-update) | async-done | bytes 11796496 | tf_op jit(solution)/shard_map/all_gather | solution.py:74
  199.8 11.9 %reshape.185 = bf16[2880,2048]{1,0:T(8,128)(2,1)} reshape(bf16[16,180,2048]{2,1,0:T(8,128)(2,1)} %all-gather.12.cloned.1.call-done) | data formatting | bytes 23592960
  211.7 10.5 %fusion.19 = f32[512,2048]{0,1:T(8,128)S(1)} fusion(bf16[512,2880]{0,1:T(8,128)(2,1)} %all-gather.8.cloned.1.call-done, bf16[2880,2048]{1,0:T(8,128)(2,1)} %reshape.185), kind=kOutput, calls=%fused_computation.40 | convolution fusion | flops 6039797760 | bytes 18939904 | tf_op jit(solution)/shard_map/dot_general | solution.py:72
  222.2 0.7 subtract_convert_fusion
  222.9 16.4 %fusion.2 = (f32[4,8,512]{2,1,0:T(8,128)S(1)}, f32[4,640,512,8]{2,1,3,0:T(8,128)}) fusion(pred[512,640]{0,1:T(8,128)(4,1)S(1)} %and_and_fusion, bf16[512,4,8,32]{0,3,2,1:T(8,128)(2,1)S(1)} %bitcast.52, bf16[512,4,8,32]{0,3,2,1:T(8,128)(2,1)S(1)} %bitcast.51, bf16[640,4,2,64]{0,3,1,2:T(8,128)(2,1)S(1)} %maximum_maximum_fusion), kind=kOutput, calls=%fused_computation.4 | convolution fusion | flops 1377812480 | bytes 44761088 | tf_op jit(solution)/shard_map/qhgd,khd->hgqk/dot_general | solution.py:39
  239.4 0.1 broadcast_maximum_fusion
  239.4 19.3 %fusion = f32[4,8,512]{2,1,0:T(8,128)S(1)} fusion(f32[4,640,512,8]{2,1,3,0:T(8,128)} %get-tuple-element.12, f32[4,8,512]{2,1,0:T(8,128)S(1)} %broadcast_maximum_fusion, pred[512,640]{0,1:T(8,128)(4,1)S(1)} %and_and_fusion), kind=kLoop, calls=%fused_computation.2 | loop fusion | flops 41926656 | bytes 42401792 | tf_op jit(solution)/shard_map/reduce_sum | solution.py:50
  258.8 0.1 add_bitcast_fusion
  258.9 18.3 %fusion.6 = bf16[512,4,8,64]{0,3,2,1:T(8,128)(2,1)S(1)} fusion(f32[4,640,512,8]{2,1,3,0:T(8,128)} %get-tuple-element.12, f32[4,8,512]{2,1,0:T(8,128)S(1)} %broadcast_maximum_fusion, pred[512,640]{0,1:T(8,128)(4,1)S(1)} %and_and_fusion, f32[512,4,8]{0,2,1:T(8,128)S(1)} %add_bitcast_fusion, bf16[640,4,2,64]{0,3,1,2:T(8,128)(2,1)S(1)} %maximum_maximum_fusion), kind=kOutput, calls=%fused_computation.9 | convolution fusion | flops 1386217472 | bytes 44826624 | tf_op jit(solution)/shard_map/hgqk,khd->qhgd/dot_general | solution.py:52
  277.2 20.6 %all-gather.14.cloned.1.call-done = bf16[16,180,2048]{2,1,0:T(8,128)(2,1)} async-done(((bf16[1,180,2048]{2,1,0:T(8,128)(2,1)}), bf16[16,180,2048]{2,1,0:T(8,128)(2,1)}) %all-gather.14.cloned.1.call-update) | async-done | bytes 11796496 | tf_op jit(solution)/shard_map/all_gather | solution.py:96
  297.7 11.6 %reshape.187 = bf16[2880,2048]{1,0:T(8,128)(2,1)} reshape(bf16[16,180,2048]{2,1,0:T(8,128)(2,1)} %all-gather.14.cloned.1.call-done) | data formatting | bytes 23592960
  309.3 12.0 %convolution_convert_fusion = bf16[512,2880]{0,1:T(8,128)(2,1)} fusion(bf16[2880,2048]{1,0:T(8,128)(2,1)} %reshape.187, bf16[512,2048]{0,1:T(8,128)(2,1)S(1)} %bitcast.62), kind=kOutput, calls=%fused_computation.7 | convolution fusion | flops 6041272320 | bytes 16842752 | tf_op jit(solution)/shard_map/dot_general | solution.py:94
  321.4 39.5 %reduce-scatter.2.cloned.1.call-done = bf16[256,2880]{0,1:T(8,128)(2,1)} async-done(((bf16[512,2880]{0,1:T(8,128)(2,1)}), bf16[256,2880]{0,1:T(8,128)(2,1)}) %reduce-scatter.2.cloned.1.call-update) | async-done | bytes 1474576 | tf_op jit(solution)/shard_map/reduce_scatter | solution.py:100
  (11 shorter events, 0.1 us)
Async XLA Ops:
  6.5 50.5 %all-gather.10.cloned.1.call-start = ((), (), s32[]{:S(2)}) async-start(), calls=%async_computation.3 | async-start | bytes 3203072 | tf_op jit(solution)/shard_map/all_gather | solution.py:79
  7.3 92.7 %all-gather.8.cloned.1.call-start = ((), (), s32[]{:S(2)}) async-start(), calls=%async_computation.1 | async-start | bytes 4423680 | tf_op jit(solution)/shard_map/all_gather | solution.py:63
  8.0 191.8 %all-gather.12.cloned.1.call-start = ((), (), s32[]{:S(2)}) async-start(), calls=%async_computation.4 | async-start | bytes 12812288 | tf_op jit(solution)/shard_map/all_gather | solution.py:74
  8.7 289.0 %all-gather.14.cloned.1.call-start = ((), (), s32[]{:S(2)}) async-start(), calls=%async_computation.5 | async-start | bytes 12812288 | tf_op jit(solution)/shard_map/all_gather | solution.py:96
  9.3 351.6 %reduce-scatter.2.cloned.1.call-start = ((), (), s32[]{:S(2)}) async-start(), calls=%async_computation.2 | async-start | bytes 4423680 | tf_op jit(solution)/shard_map/reduce_scatter | solution.py:100
  103.9 2.7 collective-permute-start
Sparse Core Ops, SparseCore 0:
  9.6 47.3 all-gather.9
  58.6 41.3 all-gather.7
  102.3 97.5 all-gather.11
  202.0 95.6 all-gather.13
  321.5 39.3 reduce-scatter.1
where the time goes:
time: 368 us; the launch traced here: 367 us
  waiting for transfers between devices  243 us (66%)
  matrix products  60.9 us (17%)
  local copies, waits for them, and re-layouts  27 us (7%)
  other arithmetic  21.1 us (6%)
  between operations  13.3 us (4%)
    all_gather x1, waiting for transfers between devices, body(): lax.all_gather(w_query, 'seq', axis=0, tiled=True)  93.2 us
    all_gather x1, waiting for transfers between devices, body(): lax.all_gather(w_kv, 'seq', axis=0, tiled=True)  46.6 us
    all_gather x1, waiting for transfers between devices, body(): token_rows = lax.all_gather(tokens, 'tp', axis=0, tiled=True)  40.1 us
    reduce_scatter x1, waiting for transfers between devices, body(): lax.psum_scatter(out_terms.astype(jnp.bfloat16), 'tp', scatter_dimension=...  39.5 us
    unnamed x3, local copies, waits for them, and re-layouts  26.3 us
    all_gather x1, waiting for transfers between devices, body(): lax.all_gather(w_out, 'seq', axis=0, tiled=True)  20.6 us
    reduce_sum x1, other arithmetic, attend(): jnp.sum(exponent, axis=-1) + jnp.exp(sink_scores[:, :, None] - row_max)  19.3 us
    dot_general x1, matrix products, attend(): jnp.einsum('hgqk,khd->qhgd', weights, value_part, preferred_element_type=...  18.3 us
  transfers between devices with their start and end apart: 6, of which 6 were waited for; matrix products, arithmetic and copies ran while one was open for 23% of the time, Pallas kernels for 0%

commit v1 on v0

--- a/solution.py
+++ b/solution.py
@@ -1,29 +1,265 @@
+import functools
 import math
 
 import jax
 import jax.numpy as jnp
 from jax import lax
+from jax.experimental import pallas as pl
+from jax.experimental.pallas import tpu as pltpu
 from jax.sharding import PartitionSpec as P
 
 HEAD_WIDTH = 64
 WINDOW_KEYS = 128
-
+SLICES = 4
 
 rope_base = 150000.0
-
-
-def from_behind(value, axis, by):
+vmem_bytes = 48 * 1024 * 1024
+
+
+def shift(value, axis, by):
     devices = lax.axis_size(axis)
     pairs = [(i, i + by) for i in range(devices) if 0 <= i + by < devices]
     return lax.ppermute(value, axis, pairs)
 
 
+def angles_of(places):
+    half_dim = HEAD_WIDTH // 2
+    frequency = jnp.exp(
+        jnp.arange(half_dim, dtype=jnp.float32) * (-2.0 * math.log(rope_base) / HEAD_WIDTH)
+    )
+    return places.astype(jnp.float32)[None, :] * frequency[:, None]
+
+
+def project_kernel(zs, tok, w0, w1, w2, w3, cosine, sine, kv_out, q_out, *, depth):
+    total = None
+    for k, w in enumerate((w0, w1, w2, w3)):
+        rows = pl.ds(pl.multiple_of(zs[k] * depth, 16), depth)
+        term = lax.dot_general(
+            w[...], tok[0, rows, :], (((1,), (0,)), ((), ())), preferred_element_type=jnp.float32
+        )
+        total = term if total is None else total + term
+    cos, sin = cosine[...], sine[...]
+    half = HEAD_WIDTH // 2
+
+    def rotated(at):
+        lower, upper = total[at : at + half], total[at + half : at + 2 * half]
+        return jnp.concatenate([lower * cos - upper * sin, upper * cos + lower * sin], axis=0)
+
+    kv_out[0:HEAD_WIDTH] = rotated(0).astype(jnp.bfloat16)
+    kv_out[HEAD_WIDTH : 2 * HEAD_WIDTH] = total[HEAD_WIDTH : 2 * HEAD_WIDTH].astype(jnp.bfloat16)
+    for h in range(q_out.shape[0] // HEAD_WIDTH):
+        q_out[h * HEAD_WIDTH : (h + 1) * HEAD_WIDTH] = rotated((h + 2) * HEAD_WIDTH).astype(jnp.bfloat16)
+
+
+def project(zs, tok, weights, cosine, sine):
+    blocks, features, block = tok.shape
+    width, depth = weights[0].shape
+    kv_width = 2 * HEAD_WIDTH
+    whole = pl.BlockSpec((width, depth), lambda j, zs: (0, 0))
+    angle = pl.BlockSpec((HEAD_WIDTH // 2, block), lambda j, zs: (0, j))
+    return pl.pallas_call(
+        functools.partial(project_kernel, depth=depth),
+        grid_spec=pltpu.PrefetchScalarGridSpec(
+            num_scalar_prefetch=1,
+            grid=(blocks,),
+            in_specs=[pl.BlockSpec((1, features, block), lambda j, zs: (j, 0, 0))]
+            + [whole] * 4
+            + [angle, angle],
+            out_specs=[
+                pl.BlockSpec((kv_width, block), lambda j, zs: (0, j)),
+                pl.BlockSpec((width - kv_width, block), lambda j, zs: (0, j)),
+            ],
+        ),
+        out_shape=[
+            jax.ShapeDtypeStruct((kv_width, blocks * block), jnp.bfloat16),
+            jax.ShapeDtypeStruct((width - kv_width, blocks * block), jnp.bfloat16),
+        ],
+        compiler_params=pltpu.CompilerParams(vmem_limit_bytes=vmem_bytes),
+        cost_estimate=pl.CostEstimate(
+            flops=2 * width * features * blocks * block,
+            bytes_accessed=2 * features * (blocks * block + width),
+            transcendentals=0,
+        ),
+        name="project",
+    )(zs, tok, *weights, cosine, sine)
+
+
+def attend_kernel(first, sinks, q, kv_before, kv_own, out):
+    window = WINDOW_KEYS
+    keys = jnp.concatenate([kv_before[:HEAD_WIDTH], kv_own[:HEAD_WIDTH]], axis=1)
+    values = jnp.concatenate([kv_before[HEAD_WIDTH:], kv_own[HEAD_WIDTH:]], axis=1)
+    keys = jnp.transpose(keys)
+    row = lax.broadcasted_iota(jnp.int32, (2 * window, window), 0)
+    lane = lax.broadcasted_iota(jnp.int32, (2 * window, window), 1)
+    start = jnp.where(first[0] + pl.program_id(0) == 0, window, 0)
+    allowed = (row > lane) & (row <= lane + window) & (row >= start)
+    bias = jnp.where(allowed, 0.0, -jnp.inf)
+    bias = jnp.concatenate([bias, bias], axis=1)
+    log2e = math.log2(math.e)
+    heads = q.shape[0] // HEAD_WIDTH
+    left = lax.broadcasted_iota(jnp.int32, (1, 2 * window), 1) < window
+    for h in range(0, heads, 2):
+        at = h * HEAD_WIDTH
+        pair = jnp.concatenate([q[at : at + HEAD_WIDTH], q[at + HEAD_WIDTH : at + 2 * HEAD_WIDTH]], axis=1)
+        scores = jnp.dot(keys, pair, preferred_element_type=jnp.float32)
+        scores = scores * (HEAD_WIDTH**-0.5 * log2e) + bias
+        sink = jnp.where(left, sinks[h], sinks[h + 1]) * log2e
+        top = jnp.maximum(jnp.max(scores, axis=0, keepdims=True), sink)
+        exponent = jnp.exp2(scores - top)
+        denominator = jnp.sum(exponent, axis=0, keepdims=True) + jnp.exp2(sink - top)
+        mixture = jnp.dot(values, exponent.astype(jnp.bfloat16), preferred_element_type=jnp.float32)
+        result = (mixture * (1.0 / denominator)).astype(jnp.bfloat16)
+        out[at : at + HEAD_WIDTH] = result[:, :window]
+        out[at + HEAD_WIDTH : at + 2 * HEAD_WIDTH] = result[:, window:]
+
+
+def attend(first, sinks, q, kv):
+    width, tokens = q.shape
+    window = WINDOW_KEYS
+    kv_width = 2 * HEAD_WIDTH
+    return pl.pallas_call(
+        attend_kernel,
+        grid_spec=pltpu.PrefetchScalarGridSpec(
+            num_scalar_prefetch=2,
+            grid=(tokens // window,),
+            in_specs=[
+                pl.BlockSpec((width, window), lambda i, *_: (0, i)),
+                pl.BlockSpec((kv_width, window), lambda i, *_: (0, i)),
+                pl.BlockSpec((kv_width, window), lambda i, *_: (0, i + 1)),
+            ],
+            out_specs=pl.BlockSpec((width, window), lambda i, *_: (0, i)),
+        ),
+        out_shape=jax.ShapeDtypeStruct((width, tokens), jnp.bfloat16),
+        compiler_params=pltpu.CompilerParams(vmem_limit_bytes=vmem_bytes),
+        cost_estimate=pl.CostEstimate(
+            flops=8 * width * tokens * window, bytes_accessed=4 * width * tokens, transcendentals=0
+        ),
+        name="attend",
+    )(first, sinks, q, kv, kv)
+
+
+def output_kernel(order, w, attended, out):
+    out[0] = jnp.dot(w[...], attended[...], preferred_element_type=jnp.float32).astype(jnp.bfloat16)
+
+
+def output_terms(order, w, attended):
+    depth, width = w.shape
+    blocks = order.shape[0]
+    block = attended.shape[1] // blocks
+    return pl.pallas_call(
+        output_kernel,
+        grid_spec=pltpu.PrefetchScalarGridSpec(
+            num_scalar_prefetch=1,
+            grid=(blocks,),
+            in_specs=[
+                pl.BlockSpec((depth, width), lambda r, order: (0, 0)),
+                pl.BlockSpec((width, block), lambda r, order: (0, order[r])),
+            ],
+            out_specs=pl.BlockSpec((1, depth, block), lambda r, order: (r, 0, 0)),
+        ),
+        out_shape=jax.ShapeDtypeStruct((blocks, depth, block), jnp.bfloat16),
+        compiler_params=pltpu.CompilerParams(vmem_limit_bytes=vmem_bytes),
+        cost_estimate=pl.CostEstimate(
+            flops=2 * width * depth * blocks * block,
+            bytes_accessed=2 * (depth * width + (depth + width) * blocks * block),
+            transcendentals=0,
+        ),
+        name="output_terms",
+    )(order, w, attended)
+
+
+def slab_body(tokens, w_query, w_kv, w_out, sinks):
+    devices = lax.axis_size("seq")
+    slabs = devices // SLICES
+    tp = lax.axis_size("tp")
+    place = lax.axis_index("seq")
+    slab, part = place // SLICES, place % SLICES
+    side = lax.axis_index("tp")
+    block = tokens.shape[0]
+    blocks = SLICES * tp
+    both = ("seq", "tp")
+
+    def swap(value, flip_seq, flip_tp):
+        pairs = [
+            (s * tp + t, (s ^ flip_seq) * tp + (t ^ flip_tp)) for s in range(devices) for t in range(tp)
+        ]
+        return lax.ppermute(value, both, pairs)
+
+    def turn(value):
+        pairs = [(s, (s + SLICES) % devices) for s in range(devices)]
+        return lax.ppermute(value, "seq", pairs)
+
+    groups = [
+        [s * tp + t for s in range(z * SLICES, (z + 1) * SLICES) for t in range(tp)] for z in range(slabs)
+    ]
+    slab_tokens = lax.all_gather(
+        tokens.T, both, axis=0, tiled=False, axis_index_groups=groups
+    )
+
+    def of_head(weight, head):
+        width = weight.shape[1] // SLICES
+        return lax.dynamic_slice_in_dim(weight, head * width, width, 1)
+
+    def of_slab(make):
+        pieces = jnp.stack(
+            [make(part)] + [swap(make(part ^ flip), flip, 0) for flip in range(1, SLICES)]
+        )
+        rows, width = pieces.shape[1:]
+        pieces = pieces.reshape(2, 2, rows, width)
+        pieces = jnp.where(part % 2 == 1, pieces[:, ::-1], pieces)
+        pieces = jnp.where(part // 2 == 1, pieces[::-1], pieces)
+        return pieces.reshape(SLICES * rows, width)
+
+    def round_slabs(own):
+        held = [own]
+        for _ in range(slabs - 1):
+            held.append(turn(held[-1]))
+        return held
+
+    own_in = of_slab(lambda head: jnp.concatenate([of_head(w_kv, head), of_head(w_query, head)], axis=1))
+    own_out = of_slab(lambda head: of_head(w_out, head))
+    weights_in = round_slabs(own_in)
+    weights_out = round_slabs(own_out)
+
+    first = slab * (blocks * block)
+    places = first + jnp.arange(blocks * block, dtype=jnp.int32)
+    angles = angles_of(places)
+    slabs_held = (slab - jnp.arange(slabs, dtype=jnp.int32)) % slabs
+    kv, q = project(slabs_held, slab_tokens, [w.T for w in weights_in], jnp.cos(angles), jnp.sin(angles))
+    kv_tail = shift(kv[:, -WINDOW_KEYS:], "seq", SLICES)
+    head_sinks = lax.dynamic_slice_in_dim(sinks, part * (sinks.shape[0] // SLICES), sinks.shape[0] // SLICES, 0)
+    attended = attend(first[None], head_sinks, q, jnp.concatenate([kv_tail, kv], axis=1))
+
+    core, row = part % 2, part // 2
+    order = jnp.stack(
+        [
+            (row ^ r) * 2 * tp + (core ^ c) * tp + (side ^ t)
+            for c in range(2)
+            for r in range(2)
+            for t in range(tp)
+        ]
+    ).astype(jnp.int32)
+    half = blocks // 2
+    result = jnp.zeros((tokens.shape[1], block), jnp.bfloat16)
+    for k in range(slabs):
+        terms = output_terms(order, weights_out[k], attended)
+        from_core = swap(terms[half:], 1, 0)
+        sums = terms[:half].astype(jnp.float32) + from_core.astype(jnp.float32)
+        sent = sums.astype(jnp.bfloat16)
+        total = sums[0]
+        total += swap(sent[1], 0, 1).astype(jnp.float32)
+        total += swap(sent[2], 2, 0).astype(jnp.float32)
+        total += swap(sent[3], 2, 1).astype(jnp.float32)
+        depth = total.shape[0]
+        result = lax.dynamic_update_slice_in_dim(
+            result, total.astype(jnp.bfloat16), slabs_held[k] * depth, 0
+        )
+    return result.T
+
+
 def rotary(vectors, places):
     half_dim = vectors.shape[-1] // 2
-    frequency = jnp.exp(
-        jnp.arange(half_dim, dtype=jnp.float32) * (-2.0 * math.log(rope_base) / vectors.shape[-1])
-    )
-    angles = places.astype(jnp.float32)[:, None, None] * frequency[None, None, :]
+    angles = angles_of(places).T[:, None, :]
     cosine = jnp.cos(angles)
     sine = jnp.sin(angles)
     lower_half = vectors[..., :half_dim]
@@ -33,7 +269,7 @@
     )
 
 
-def attend(query_rows, key_value_rows, sink_scores, query_pos, key_pos):
+def attend_rows(query_rows, key_value_rows, sink_scores, query_pos, key_pos):
     key_part = key_value_rows[:, :, 0, :]
     value_part = key_value_rows[:, :, 1, :]
     scores = jnp.einsum(
@@ -59,7 +295,7 @@
     return jnp.stack([key_part, split_key_value[:, :, 1, :]], axis=2).astype(jnp.bfloat16)
 
 
-def body(tokens, w_query, w_kv, w_out, sinks):
+def row_body(tokens, w_query, w_kv, w_out, sinks):
     token_rows = lax.all_gather(tokens, "tp", axis=0, tiled=True)
     row_count = token_rows.shape[0]
     kv_width = w_kv.shape[1]
@@ -84,11 +320,11 @@
     ).astype(jnp.bfloat16)
     query_rows = query_rows.reshape(row_count, kv_heads, head_groups, HEAD_WIDTH)
     local_kv = finish(kv_sum, query_pos, kv_heads).reshape(row_count, kv_width)
-    kv_tail = from_behind(local_kv[row_count - WINDOW_KEYS :], "seq", 1)
+    kv_tail = shift(local_kv[row_count - WINDOW_KEYS :], "seq", 1)
     key_value_rows = jnp.concatenate([kv_tail, local_kv], axis=0).reshape(
         row_count + WINDOW_KEYS, kv_heads, 2, HEAD_WIDTH
     )
-    attended = attend(
+    attended = attend_rows(
         query_rows, key_value_rows, sinks.reshape(kv_heads, head_groups), query_pos, key_pos
     ).reshape(row_count, q_width)
     out_terms = lax.dot_general(
@@ -97,11 +333,21 @@
         (((1,), (1,)), ((), ())),
         preferred_element_type=jnp.float32,
     )
-    result = lax.psum_scatter(out_terms.astype(jnp.bfloat16), "tp", scatter_dimension=0, tiled=True)
-    return result
+    return lax.psum_scatter(out_terms.astype(jnp.bfloat16), "tp", scatter_dimension=0, tiled=True)
 
 
 def solution(mesh):
     in_specs = (P(("seq", "tp"), None), P("seq", "tp"), P("seq", "tp"), P("seq", "tp"), P("tp"))
     out_specs = P(("seq", "tp"), None)
+
+    def body(tokens, w_query, w_kv, w_out, sinks):
+        by_slabs = (
+            w_kv.shape[1] == SLICES * 2 * HEAD_WIDTH
+            and mesh.shape["tp"] == 2
+            and mesh.shape["seq"] == 4 * SLICES
+            and tokens.shape[0] % (2 * WINDOW_KEYS) == 0
+            and (w_query.shape[0] * SLICES) % 16 == 0
+        )
+        return (slab_body if by_slabs else row_body)(tokens, w_query, w_kv, w_out, sinks)
+
     return jax.shard_map(body, mesh=mesh, in_specs=in_specs, out_specs=out_specs, check_vma=False)

time: 368 us -> 284 us (0.77)
  waiting for transfers between devices: 243 us -> 154 us
  matrix products: 60.9 us -> 0 us
  Pallas kernels: 0 us -> 53.3 us
  starting transfers between devices: 1.9 us -> 29.2 us
  other arithmetic: 21.1 us -> 8.11 us
  local copies, waits for them, and re-layouts: 27 us -> 21.6 us
    all_gather x4 -> x1, waiting for transfers between devices: 200 us -> 0.01 us  [slab_body(): lax.all_gather(tokens.T, both, axis=0, tiled=False, axis_index_groups=gro...]
    ppermute x1 -> x29, waiting for transfers between devices: 0.59 us -> 154 us  [the longest x22 82.1 us: swap(): return lax.ppermute(value, both, pairs)]
    dot_general x5 -> x0, matrix products: 60.9 us -> none  [the longest x1 18.3 us: attend(): jnp.einsum('hgqk,khd->qhgd', weights, value_part, preferred_element_type=...]
    pallas_call x0 -> x6, Pallas kernels: none -> 53.3 us  [the longest x1 21.6 us: attend(): pl.pallas_call(attend_kernel, grid_spec=pltpu.PrefetchScalarGridSpec(num_...]
    reduce_scatter x1 -> x0, waiting for transfers between devices: 39.5 us -> none  [body(): lax.psum_scatter(out_terms.astype(jnp.bfloat16), 'tp', scatter_dimension=...]
    ppermute x1 -> x29, starting transfers between devices: 1.75 us -> 29.2 us  [the longest x22 24 us: swap(): return lax.ppermute(value, both, pairs)]
    reduce_sum x1 -> x0, other arithmetic: 19.3 us -> none  [attend(): jnp.sum(exponent, axis=-1) + jnp.exp(sink_scores[:, :, None] - row_max)]
    unnamed x3 -> x30, local copies, waits for them, and re-layouts: 26.3 us -> 9.79 us
  transfers between devices with their start and end apart: 6 -> 30, of which waited for: 6 -> 15; matrix products, arithmetic and copies ran while one was open for 23% -> 6% of each run, Pallas kernels for 0% -> 17%
where the time goes in v1:
time: 284 us; the launch traced here: 283 us
  waiting for transfers between devices  154 us (54%)
  Pallas kernels  53.3 us (19%)
  starting transfers between devices  29.2 us (10%)
  local copies, waits for them, and re-layouts  21.6 us (8%)
  between operations  16.5 us (6%)
  other arithmetic  8.11 us (3%)
    ppermute x22, waiting for transfers between devices, swap(): return lax.ppermute(value, both, pairs)  82.1 us
    ppermute x6, waiting for transfers between devices, turn(): return lax.ppermute(value, 'seq', pairs)  70.1 us
    ppermute x22, starting transfers between devices, swap(): return lax.ppermute(value, both, pairs)  24 us
    pallas_call x1, Pallas kernels, attend(): pl.pallas_call(attend_kernel, grid_spec=pltpu.PrefetchScalarGridSpec(num_...  21.6 us
    pallas_call x4, Pallas kernels, output_terms(): pl.pallas_call(output_kernel, grid_spec=pltpu.PrefetchScalarGridSpec(num_...  18.4 us
    pallas_call x1, Pallas kernels, project(): pl.pallas_call(functools.partial(project_kernel, depth=depth), grid_spec=...  13.3 us
    unnamed x30, local copies, waits for them, and re-layouts  9.79 us
    ppermute x3, local copies, waits for them, and re-layouts, turn(): return lax.ppermute(value, 'seq', pairs)  6.1 us
  transfers between devices with their start and end apart: 30, of which 15 were waited for; matrix products, arithmetic and copies ran while one was open for 6% of the time, Pallas kernels for 17%

profile of v1, /device:TPU:0, one launch (start us, length us, event | category | flops | bytes accessed | tf_op | source)
XLA Modules:
  0.0 283.0 jit_solution(1385721758049837205)
XLA Ops:
  8.4 2.6 collective-permute-start.4
  11.3 6.3 %collective-permute-done.4 = bf16[180,640]{1,0:T(8,128)(2,1)S(1)} collective-permute-done((bf16[180,640]{1,0:T(8,128)(2,1)S(1)}, bf16[180,640]{1,0:T(8,128)(2,1)S(1)}, u32[]{:S(2)}, u32[]{:S(2)}) %collective-permute-start.4) | collective-permute-done | bytes 230432 | tf_op jit(solution)/shard_map/ppermute | solution.py:186
  17.6 4.7 %collective-permute-done.5 = bf16[180,640]{1,0:T(8,128)(2,1)S(1)} collective-permute-done((bf16[180,640]{1,0:T(8,128)(2,1)S(1)}, bf16[180,640]{1,0:T(8,128)(2,1)S(1)}, u32[]{:S(2)}, u32[]{:S(2)}) %collective-permute-start.5) | collective-permute-done | bytes 230432 | tf_op jit(solution)/shard_map/ppermute | solution.py:186
  24.6 22.9 %collective-permute-done.6 = bf16[720,640]{1,0:T(8,128)(2,1)S(1)} collective-permute-done((bf16[720,640]{1,0:T(8,128)(2,1)S(1)}, bf16[720,640]{1,0:T(8,128)(2,1)S(1)}, u32[]{:S(2)}, u32[]{:S(2)}) %collective-permute-start.6) | collective-permute-done | bytes 921632 | tf_op jit(solution)/shard_map/ppermute | solution.py:190
  47.5 1.9 collective-permute-start.1
  49.8 9.5 %collective-permute-done.1 = bf16[180,512]{1,0:T(8,128)(2,1)S(1)} collective-permute-done((bf16[180,512]{1,0:T(8,128)(2,1)S(1)}, bf16[180,512]{1,0:T(8,128)(2,1)S(1)}, u32[]{:S(2)}, u32[]{:S(2)}) %collective-permute-start.1) | collective-permute-done | bytes 184352 | tf_op jit(solution)/shard_map/ppermute | solution.py:186
  59.2 7.2 %collective-permute-done.2 = bf16[180,512]{1,0:T(8,128)(2,1)S(1)} collective-permute-done((bf16[180,512]{1,0:T(8,128)(2,1)S(1)}, bf16[180,512]{1,0:T(8,128)(2,1)S(1)}, u32[]{:S(2)}, u32[]{:S(2)}) %collective-permute-start.2) | collective-permute-done | bytes 184352 | tf_op jit(solution)/shard_map/ppermute | solution.py:186
  66.6 4.5 %collective-permute-done.7 = bf16[720,640]{1,0:T(8,128)(2,1)} collective-permute-done((bf16[720,640]{1,0:T(8,128)(2,1)S(1)}, bf16[720,640]{1,0:T(8,128)(2,1)}, u32[]{:S(2)}, u32[]{:S(2)}) %collective-permute-start.7) | collective-permute-done | bytes 921632 | tf_op jit(solution)/shard_map/ppermute | solution.py:190
  74.4 35.5 %collective-permute-done.14.w = bf16[720,512]{1,0:T(8,128)(2,1)} collective-permute-done((bf16[720,512]{1,0:T(8,128)(2,1)S(1)}, bf16[720,512]{1,0:T(8,128)(2,1)}, u32[]{:S(2)}, u32[]{:S(2)}) %collective-permute-start.14) | collective-permute-done | bytes 737312 | tf_op jit(solution)/shard_map/ppermute | solution.py:190
  111.4 2.2 copy.12
  113.7 2.3 copy.13
  120.3 13.3 %project.1 = (bf16[128,2048]{1,0:T(8,128)(2,1)S(1)}, bf16[512,2048]{1,0:T(8,128)(2,1)}) custom-call(s32[4]{0:T(128)S(1)} %and_select_fusion.zs, bf16[8,2880,256]{2,1,0:T(8,128)(2,1)} %bitcast.117, bf16[640,720]{1,0:T(8,128)(2,1)S(1)} %bitcast.104, bf16[640,720]{1,0:T(8,128)(2,1)S(1)} %bitcast.105, bf16[640,720]{1,0:T(8,128)(2,1)S(1)} %bitcast.106, ...), custom_call_target="tpu_custom_call" | custom-call | flops 7549747200 | bytes 15482880 | tf_op jit(solution)/shard_map/project/pallas_call | solution.py:60
  138.1 21.6 %attend.1.attended = bf16[512,2048]{1,0:T(8,128)(2,1)S(1)} custom-call(s32[1]{0:T(128)} %bitcast.13.first, f32[8]{0:T(128)S(1)} %dynamic_slice.43.sinks, bf16[512,2048]{1,0:T(8,128)(2,1)S(1)} %copy-done.4, bf16[128,2176]{1,0:T(8,128)(2,1)S(1)} %pad_maximum_fusion.2.kv_before.kv_own, bf16[128,2176]{1,0:T(8,128)(2,1)S(1)} %pad_maximum_fusion.2.kv_before.kv_own), custom_call_target="tpu_custom_call" | custom-call | flops 1073741824 | bytes 4194304 | tf_op jit(solution)/shard_map/attend/pallas_call | solution.py:120
  159.7 4.9 %output_terms.6 = bf16[8,720,256]{2,1,0:T(8,128)(2,1)S(1)} custom-call(s32[8]{0:T(128)S(1)} %stack.65.order, bf16[720,512]{1,0:T(8,128)(2,1)} %collective-permute-done.19.w, bf16[512,2048]{1,0:T(8,128)(2,1)S(1)} %attend.1.attended), custom_call_target="tpu_custom_call" | custom-call | flops 1509949440 | bytes 5783552 | tf_op jit(solution)/shard_map/output_terms/pallas_call | solution.py:149
  166.8 2.3 collective-permute-start.24
  169.1 4.9 %output_terms.5 = bf16[8,720,256]{2,1,0:T(8,128)(2,1)S(1)} custom-call(s32[8]{0:T(128)S(1)} %stack.65.order, bf16[720,512]{1,0:T(8,128)(2,1)} %collective-permute-done.14.w, bf16[512,2048]{1,0:T(8,128)(2,1)S(1)} %attend.1.attended), custom_call_target="tpu_custom_call" | custom-call | flops 1509949440 | bytes 5783552 | tf_op jit(solution)/shard_map/output_terms/pallas_call | solution.py:149
  178.6 3.8 %output_terms.4 = bf16[8,720,256]{2,1,0:T(8,128)(2,1)S(1)} custom-call(s32[8]{0:T(128)S(1)} %stack.65.order, bf16[720,512]{1,0:T(8,128)(2,1)S(1)} %reshape.31.w, bf16[512,2048]{1,0:T(8,128)(2,1)S(1)} %attend.1.attended), custom_call_target="tpu_custom_call" | custom-call | flops 1509949440 | bytes 5783552 | tf_op jit(solution)/shard_map/output_terms/pallas_call | solution.py:149
  183.0 7.3 %collective-permute-done.24.w = bf16[720,512]{1,0:T(8,128)(2,1)} collective-permute-done((bf16[720,512]{1,0:T(8,128)(2,1)}, bf16[720,512]{1,0:T(8,128)(2,1)}, u32[]{:S(2)}, u32[]{:S(2)}) %collective-permute-start.24) | collective-permute-done | bytes 737312 | tf_op jit(solution)/shard_map/ppermute | solution.py:190
  190.2 4.9 %output_terms.7 = bf16[8,720,256]{2,1,0:T(8,128)(2,1)S(1)} custom-call(s32[8]{0:T(128)S(1)} %stack.65.order, bf16[720,512]{1,0:T(8,128)(2,1)} %collective-permute-done.24.w, bf16[512,2048]{1,0:T(8,128)(2,1)S(1)} %attend.1.attended), custom_call_target="tpu_custom_call" | custom-call | flops 1509949440 | bytes 5783552 | tf_op jit(solution)/shard_map/output_terms/pallas_call | solution.py:149
  197.0 1.9 convert_add_fusion.1
  199.0 2.9 %collective-permute-start.21 = (bf16[720,256]{1,0:T(8,128)(2,1)S(1)}, bf16[720,256]{1,0:T(8,128)(2,1)S(1)}, u32[]{:S(2)}, u32[]{:S(2)}) collective-permute-start(bf16[720,256]{1,0:T(8,128)(2,1)S(1)} %get-tuple-element.20), channel_id=1, source_target_pairs={{0,1},{1,0},{2,3},{3,2},{4,5},{5,4},{6,7},{7,6},{8,9},{9,8},{10,11... | collective-permute-start | bytes 1105928 | tf_op jit(solution)/shard_map/ppermute | solution.py:186
  204.5 1.9 collective-permute-start.11
  206.4 2.2 collective-permute-start.12
  208.9 2.5 collective-permute-done.21
  211.4 2.7 collective-permute-start.17
  214.0 13.1 %collective-permute-done.11 = bf16[720,256]{1,0:T(8,128)(2,1)S(1)} collective-permute-done((bf16[720,256]{1,0:T(8,128)(2,1)S(1)}, bf16[720,256]{1,0:T(8,128)(2,1)S(1)}, u32[]{:S(2)}, u32[]{:S(2)}) %collective-permute-start.11) | collective-permute-done | bytes 368672 | tf_op jit(solution)/shard_map/ppermute | solution.py:186
  227.2 3.6 %collective-permute-start.18 = (bf16[720,256]{1,0:T(8,128)(2,1)S(1)}, bf16[720,256]{1,0:T(8,128)(2,1)S(1)}, u32[]{:S(2)}, u32[]{:S(2)}) collective-permute-start(bf16[720,256]{1,0:T(8,128)(2,1)S(1)} %get-tuple-element.24), channel_id=1, source_target_pairs={{0,5},{1,4},{2,7},{3,6},{4,1},{5,0},{6,3},{7,2},{8,13},{9,12},{10,... | collective-permute-start | bytes 1105928 | tf_op jit(solution)/shard_map/ppermute | solution.py:186
  231.0 6.3 %collective-permute-done.13 = bf16[720,256]{1,0:T(8,128)(2,1)S(1)} collective-permute-done((bf16[720,256]{1,0:T(8,128)(2,1)S(1)}, bf16[720,256]{1,0:T(8,128)(2,1)S(1)}, u32[]{:S(2)}, u32[]{:S(2)}) %collective-permute-start.13) | collective-permute-done | bytes 368672 | tf_op jit(solution)/shard_map/ppermute | solution.py:186
  239.2 2.0 collective-permute-start.27
  241.2 4.0 %collective-permute-done.18 = bf16[720,256]{1,0:T(8,128)(2,1)S(1)} collective-permute-done((bf16[720,256]{1,0:T(8,128)(2,1)S(1)}, bf16[720,256]{1,0:T(8,128)(2,1)S(1)}, u32[]{:S(2)}, u32[]{:S(2)}) %collective-permute-start.18) | collective-permute-done | bytes 368672 | tf_op jit(solution)/shard_map/ppermute | solution.py:186
  246.2 14.8 %collective-permute-done.22 = bf16[720,256]{1,0:T(8,128)(2,1)S(1)} collective-permute-done((bf16[720,256]{1,0:T(8,128)(2,1)S(1)}, bf16[720,256]{1,0:T(8,128)(2,1)S(1)}, u32[]{:S(2)}, u32[]{:S(2)}) %collective-permute-start.22) | collective-permute-done | bytes 368672 | tf_op jit(solution)/shard_map/ppermute | solution.py:186
  261.2 13.6 %collective-permute-done.27 = bf16[720,256]{1,0:T(8,128)(2,1)S(1)} collective-permute-done((bf16[720,256]{1,0:T(8,128)(2,1)S(1)}, bf16[720,256]{1,0:T(8,128)(2,1)S(1)}, u32[]{:S(2)}, u32[]{:S(2)}) %collective-permute-start.27) | collective-permute-done | bytes 368672 | tf_op jit(solution)/shard_map/ppermute | solution.py:186
  (110 shorter events, 32.6 us)
Async XLA Ops:
  6.5 109.4 %all-gather.3.cloned.1.call-start = ((), (), s32[]{:S(2)}) async-start(), calls=%async_computation | async-start | bytes 13271040 | tf_op jit(solution)/shard_map/all_gather | solution.py:195
  7.9 3.4 %collective-permute-start.3 = (bf16[180,640]{1,0:T(8,128)(2,1)S(1)}, bf16[180,640]{1,0:T(8,128)(2,1)S(1)}, u32[]{:S(2)}, u32[]{:S(2)}) collective-permute-start(bf16[180,640]{1,0:T(8,128)(2,1)S(1)} %pad_maximum_fusion.3), channel_id=1, source_target_pairs={{0,2},{1,3},{2,0},{3,1},{4,6},{5,7},{6,4},{7,5},{8,10},{9,11},{10,... | collective-permute-start | bytes 691208 | tf_op jit(solution)/shard_map/ppermute | solution.py:186
  8.4 9.2 %collective-permute-start.4 = (bf16[180,640]{1,0:T(8,128)(2,1)S(1)}, bf16[180,640]{1,0:T(8,128)(2,1)S(1)}, u32[]{:S(2)}, u32[]{:S(2)}) collective-permute-start(bf16[180,640]{1,0:T(8,128)(2,1)S(1)} %pad_maximum_fusion.4), channel_id=1, source_target_pairs={{0,4},{1,5},{2,6},{3,7},{4,0},{5,1},{6,2},{7,3},{8,12},{9,13},{10,... | collective-permute-start | bytes 691208 | tf_op jit(solution)/shard_map/ppermute | solution.py:186
  11.0 11.3 %collective-permute-start.5 = (bf16[180,640]{1,0:T(8,128)(2,1)S(1)}, bf16[180,640]{1,0:T(8,128)(2,1)S(1)}, u32[]{:S(2)}, u32[]{:S(2)}) collective-permute-start(bf16[180,640]{1,0:T(8,128)(2,1)S(1)} %pad_maximum_fusion.5), channel_id=1, source_target_pairs={{0,6},{1,7},{2,4},{3,5},{4,2},{5,3},{6,0},{7,1},{8,14},{9,15},{10,... | collective-permute-start | bytes 691208 | tf_op jit(solution)/shard_map/ppermute | solution.py:186
  22.7 24.8 %copy-start.12 = (bf16[180,2048]{1,0:T(8,128)(2,1)S(1)}, bf16[180,2048]{1,0:T(8,128)(2,1)}, u32[]{:S(2)}) copy-start(bf16[180,2048]{1,0:T(8,128)(2,1)} %param.8) | copy-start | bytes 2211844
  23.0 24.4 %collective-permute-start.6 = (bf16[720,640]{1,0:T(8,128)(2,1)S(1)}, bf16[720,640]{1,0:T(8,128)(2,1)S(1)}, u32[]{:S(2)}, u32[]{:S(2)}) collective-permute-start(bf16[720,640]{1,0:T(8,128)(2,1)S(1)} %reshape.33), channel_id=1, source_target_pairs={{0,8},{2,10},{4,12},{6,14},{8,16},{10,18},{12,20},{14,22},{16,24},... | collective-permute-start | bytes 2764808 | tf_op jit(solution)/shard_map/ppermute | solution.py:190
  47.5 23.7 %copy-start.10 = (bf16[720,640]{1,0:T(8,128)(2,1)}, bf16[720,640]{1,0:T(8,128)(2,1)S(1)}, u32[]{:S(2)}) copy-start(bf16[720,640]{1,0:T(8,128)(2,1)S(1)} %collective-permute-done.6) | copy-start | bytes 2764804
  47.5 23.6 %collective-permute-start.7 = (bf16[720,640]{1,0:T(8,128)(2,1)S(1)}, bf16[720,640]{1,0:T(8,128)(2,1)}, u32[]{:S(2)}, u32[]{:S(2)}) collective-permute-start(bf16[720,640]{1,0:T(8,128)(2,1)S(1)} %collective-permute-done.6), channel_id=1, source_target_pairs={{0,8},{2,10},{4,12},{6,14},{8,16},{10,18},{12,20},{14,22},{16,24},... | collective-permute-start | bytes 2764808 | tf_op jit(solution)/shard_map/ppermute | solution.py:190
  47.5 11.7 %collective-permute-start.1 = (bf16[180,512]{1,0:T(8,128)(2,1)S(1)}, bf16[180,512]{1,0:T(8,128)(2,1)S(1)}, u32[]{:S(2)}, u32[]{:S(2)}) collective-permute-start(bf16[180,512]{1,0:T(8,128)(2,1)S(1)} %get-tuple-element.36), channel_id=1, source_target_pairs={{0,4},{1,5},{2,6},{3,7},{4,0},{5,1},{6,2},{7,3},{8,12},{9,13},{10,... | collective-permute-start | bytes 552968 | tf_op jit(solution)/shard_map/ppermute | solution.py:186
  49.5 16.9 %collective-permute-start.2 = (bf16[180,512]{1,0:T(8,128)(2,1)S(1)}, bf16[180,512]{1,0:T(8,128)(2,1)S(1)}, u32[]{:S(2)}, u32[]{:S(2)}) collective-permute-start(bf16[180,512]{1,0:T(8,128)(2,1)S(1)} %get-tuple-element.35), channel_id=1, source_target_pairs={{0,6},{1,7},{2,4},{3,5},{4,2},{5,3},{6,0},{7,1},{8,14},{9,15},{10,... | collective-permute-start | bytes 552968 | tf_op jit(solution)/shard_map/ppermute | solution.py:186
  49.5 16.9 %collective-permute-start = (bf16[180,512]{1,0:T(8,128)(2,1)S(1)}, bf16[180,512]{1,0:T(8,128)(2,1)S(1)}, u32[]{:S(2)}, u32[]{:S(2)}) collective-permute-start(bf16[180,512]{1,0:T(8,128)(2,1)S(1)} %get-tuple-element.34), channel_id=1, source_target_pairs={{0,2},{1,3},{2,0},{3,1},{4,6},{5,7},{6,4},{7,5},{8,10},{9,11},{10,... | collective-permute-start | bytes 552968 | tf_op jit(solution)/shard_map/ppermute | solution.py:186
  71.1 42.6 %collective-permute-start.8 = (bf16[720,640]{1,0:T(8,128)(2,1)}, bf16[720,640]{1,0:T(8,128)(2,1)}, u32[]{:S(2)}, u32[]{:S(2)}) collective-permute-start(bf16[720,640]{1,0:T(8,128)(2,1)} %collective-permute-done.7), channel_id=1, source_target_pairs={{0,8},{2,10},{4,12},{6,14},{8,16},{10,18},{12,20},{14,22},{16,24},... | collective-permute-start | bytes 2764808 | tf_op jit(solution)/shard_map/ppermute | solution.py:190
  71.4 38.4 %collective-permute-start.14 = (bf16[720,512]{1,0:T(8,128)(2,1)S(1)}, bf16[720,512]{1,0:T(8,128)(2,1)}, u32[]{:S(2)}, u32[]{:S(2)}) collective-permute-start(bf16[720,512]{1,0:T(8,128)(2,1)S(1)} %reshape.31.w), channel_id=1, source_target_pairs={{0,8},{2,10},{4,12},{6,14},{8,16},{10,18},{12,20},{14,22},{16,24},... | collective-permute-start | bytes 2211848 | tf_op jit(solution)/shard_map/ppermute | solution.py:190
  109.8 49.9 %collective-permute-start.19 = (bf16[720,512]{1,0:T(8,128)(2,1)}, bf16[720,512]{1,0:T(8,128)(2,1)}, u32[]{:S(2)}, u32[]{:S(2)}) collective-permute-start(bf16[720,512]{1,0:T(8,128)(2,1)} %collective-permute-done.14.w), channel_id=1, source_target_pairs={{0,8},{2,10},{4,12},{6,14},{8,16},{10,18},{12,20},{14,22},{16,24},... | collective-permute-start | bytes 2211848 | tf_op jit(solution)/shard_map/ppermute | solution.py:190
  133.6 2.9 %collective-permute-start.9 = (bf16[128,128]{1,0:T(8,128)(2,1)S(1)}, bf16[128,128]{1,0:T(8,128)(2,1)S(1)}, u32[]{:S(2)}, u32[]{:S(2)}) collective-permute-start(bf16[128,128]{1,0:T(8,128)(2,1)S(1)} %slice.87), channel_id=1, source_target_pairs={{0,8},{2,10},{4,12},{6,14},{8,16},{10,18},{12,20},{14,22},{16,24},... | collective-permute-start | bytes 98312 | tf_op jit(solution)/shard_map/ppermute | solution.py:22
  166.0 29.3 %collective-permute-start.20 = (bf16[4,720,256]{2,1,0:T(8,128)(2,1)}, bf16[4,720,256]{2,1,0:T(8,128)(2,1)}, u32[]{:S(2)}, u32[]{:S(2)}) collective-permute-start(bf16[4,720,256]{2,1,0:T(8,128)(2,1)} %slice.129), channel_id=1, source_target_pairs={{0,2},{1,3},{2,0},{3,1},{4,6},{5,7},{6,4},{7,5},{8,10},{9,11},{10,... | collective-permute-start | bytes 4423688 | tf_op jit(solution)/shard_map/ppermute | solution.py:186
  166.8 23.5 %collective-permute-start.24 = (bf16[720,512]{1,0:T(8,128)(2,1)}, bf16[720,512]{1,0:T(8,128)(2,1)}, u32[]{:S(2)}, u32[]{:S(2)}) collective-permute-start(bf16[720,512]{1,0:T(8,128)(2,1)} %collective-permute-done.19.w), channel_id=1, source_target_pairs={{0,8},{2,10},{4,12},{6,14},{8,16},{10,18},{12,20},{14,22},{16,24},... | collective-permute-start | bytes 2211848 | tf_op jit(solution)/shard_map/ppermute | solution.py:190
  175.3 26.6 %collective-permute-start.15 = (bf16[4,720,256]{2,1,0:T(8,128)(2,1)}, bf16[4,720,256]{2,1,0:T(8,128)(2,1)}, u32[]{:S(2)}, u32[]{:S(2)}) collective-permute-start(bf16[4,720,256]{2,1,0:T(8,128)(2,1)} %slice.123), channel_id=1, source_target_pairs={{0,2},{1,3},{2,0},{3,1},{4,6},{5,7},{6,4},{7,5},{8,10},{9,11},{10,... | collective-permute-start | bytes 4423688 | tf_op jit(solution)/shard_map/ppermute | solution.py:186
  182.5 21.5 %collective-permute-start.10 = (bf16[4,720,256]{2,1,0:T(8,128)(2,1)S(1)}, bf16[4,720,256]{2,1,0:T(8,128)(2,1)S(1)}, u32[]{:S(2)}, u32[]{:S(2)}) collective-permute-start(bf16[4,720,256]{2,1,0:T(8,128)(2,1)S(1)} %slice.117), channel_id=1, source_target_pairs={{0,2},{1,3},{2,0},{3,1},{4,6},{5,7},{6,4},{7,5},{8,10},{9,11},{10,... | collective-permute-start | bytes 4423688 | tf_op jit(solution)/shard_map/ppermute | solution.py:186
  195.2 13.3 %collective-permute-start.25 = (bf16[4,720,256]{2,1,0:T(8,128)(2,1)S(1)}, bf16[4,720,256]{2,1,0:T(8,128)(2,1)S(1)}, u32[]{:S(2)}, u32[]{:S(2)}) collective-permute-start(bf16[4,720,256]{2,1,0:T(8,128)(2,1)S(1)} %slice.135), channel_id=1, source_target_pairs={{0,2},{1,3},{2,0},{3,1},{4,6},{5,7},{6,4},{7,5},{8,10},{9,11},{10,... | collective-permute-start | bytes 4423688 | tf_op jit(solution)/shard_map/ppermute | solution.py:186
  199.0 12.4 %collective-permute-start.21 = (bf16[720,256]{1,0:T(8,128)(2,1)S(1)}, bf16[720,256]{1,0:T(8,128)(2,1)S(1)}, u32[]{:S(2)}, u32[]{:S(2)}) collective-permute-start(bf16[720,256]{1,0:T(8,128)(2,1)S(1)} %get-tuple-element.20), channel_id=1, source_target_pairs={{0,1},{1,0},{2,3},{3,2},{4,5},{5,4},{6,7},{7,6},{8,9},{9,8},{10,11... | collective-permute-start | bytes 1105928 | tf_op jit(solution)/shard_map/ppermute | solution.py:186
  203.7 34.7 %collective-permute-start.16 = (bf16[720,256]{1,0:T(8,128)(2,1)S(1)}, bf16[720,256]{1,0:T(8,128)(2,1)S(1)}, u32[]{:S(2)}, u32[]{:S(2)}) collective-permute-start(bf16[720,256]{1,0:T(8,128)(2,1)S(1)} %get-tuple-element.23), channel_id=1, source_target_pairs={{0,1},{1,0},{2,3},{3,2},{4,5},{5,4},{6,7},{7,6},{8,9},{9,8},{10,11... | collective-permute-start | bytes 1105928 | tf_op jit(solution)/shard_map/ppermute | solution.py:186
  204.5 22.7 %collective-permute-start.11 = (bf16[720,256]{1,0:T(8,128)(2,1)S(1)}, bf16[720,256]{1,0:T(8,128)(2,1)S(1)}, u32[]{:S(2)}, u32[]{:S(2)}) collective-permute-start(bf16[720,256]{1,0:T(8,128)(2,1)S(1)} %get-tuple-element.26), channel_id=1, source_target_pairs={{0,1},{1,0},{2,3},{3,2},{4,5},{5,4},{6,7},{7,6},{8,9},{9,8},{10,11... | collective-permute-start | bytes 1105928 | tf_op jit(solution)/shard_map/ppermute | solution.py:186
  206.4 24.5 %collective-permute-start.12 = (bf16[720,256]{1,0:T(8,128)(2,1)S(1)}, bf16[720,256]{1,0:T(8,128)(2,1)S(1)}, u32[]{:S(2)}, u32[]{:S(2)}) collective-permute-start(bf16[720,256]{1,0:T(8,128)(2,1)S(1)} %get-tuple-element.28), channel_id=1, source_target_pairs={{0,4},{1,5},{2,6},{3,7},{4,0},{5,1},{6,2},{7,3},{8,12},{9,13},{10,... | collective-permute-start | bytes 1105928 | tf_op jit(solution)/shard_map/ppermute | solution.py:186
  208.5 28.7 %collective-permute-start.13 = (bf16[720,256]{1,0:T(8,128)(2,1)S(1)}, bf16[720,256]{1,0:T(8,128)(2,1)S(1)}, u32[]{:S(2)}, u32[]{:S(2)}) collective-permute-start(bf16[720,256]{1,0:T(8,128)(2,1)S(1)} %get-tuple-element.27), channel_id=1, source_target_pairs={{0,5},{1,4},{2,7},{3,6},{4,1},{5,0},{6,3},{7,2},{8,13},{9,12},{10,... | collective-permute-start | bytes 1105928 | tf_op jit(solution)/shard_map/ppermute | solution.py:186
  211.4 27.8 %collective-permute-start.17 = (bf16[720,256]{1,0:T(8,128)(2,1)S(1)}, bf16[720,256]{1,0:T(8,128)(2,1)S(1)}, u32[]{:S(2)}, u32[]{:S(2)}) collective-permute-start(bf16[720,256]{1,0:T(8,128)(2,1)S(1)} %get-tuple-element.25), channel_id=1, source_target_pairs={{0,4},{1,5},{2,6},{3,7},{4,0},{5,1},{6,2},{7,3},{8,12},{9,13},{10,... | collective-permute-start | bytes 1105928 | tf_op jit(solution)/shard_map/ppermute | solution.py:186
  227.2 18.0 %collective-permute-start.18 = (bf16[720,256]{1,0:T(8,128)(2,1)S(1)}, bf16[720,256]{1,0:T(8,128)(2,1)S(1)}, u32[]{:S(2)}, u32[]{:S(2)}) collective-permute-start(bf16[720,256]{1,0:T(8,128)(2,1)S(1)} %get-tuple-element.24), channel_id=1, source_target_pairs={{0,5},{1,4},{2,7},{3,6},{4,1},{5,0},{6,3},{7,2},{8,13},{9,12},{10,... | collective-permute-start | bytes 1105928 | tf_op jit(solution)/shard_map/ppermute | solution.py:186
  230.9 30.1 %collective-permute-start.22 = (bf16[720,256]{1,0:T(8,128)(2,1)S(1)}, bf16[720,256]{1,0:T(8,128)(2,1)S(1)}, u32[]{:S(2)}, u32[]{:S(2)}) collective-permute-start(bf16[720,256]{1,0:T(8,128)(2,1)S(1)} %get-tuple-element.22), channel_id=1, source_target_pairs={{0,4},{1,5},{2,6},{3,7},{4,0},{5,1},{6,2},{7,3},{8,12},{9,13},{10,... | collective-permute-start | bytes 1105928 | tf_op jit(solution)/shard_map/ppermute | solution.py:186
  237.3 23.7 %collective-permute-start.23 = (bf16[720,256]{1,0:T(8,128)(2,1)S(1)}, bf16[720,256]{1,0:T(8,128)(2,1)S(1)}, u32[]{:S(2)}, u32[]{:S(2)}) collective-permute-start(bf16[720,256]{1,0:T(8,128)(2,1)S(1)} %get-tuple-element.21), channel_id=1, source_target_pairs={{0,5},{1,4},{2,7},{3,6},{4,1},{5,0},{6,3},{7,2},{8,13},{9,12},{10,... | collective-permute-start | bytes 1105928 | tf_op jit(solution)/shard_map/ppermute | solution.py:186
  238.4 22.8 %collective-permute-start.26 = (bf16[720,256]{1,0:T(8,128)(2,1)S(1)}, bf16[720,256]{1,0:T(8,128)(2,1)S(1)}, u32[]{:S(2)}, u32[]{:S(2)}) collective-permute-start(bf16[720,256]{1,0:T(8,128)(2,1)S(1)} %get-tuple-element.17), channel_id=1, source_target_pairs={{0,1},{1,0},{2,3},{3,2},{4,5},{5,4},{6,7},{7,6},{8,9},{9,8},{10,11... | collective-permute-start | bytes 1105928 | tf_op jit(solution)/shard_map/ppermute | solution.py:186
  239.2 35.6 %collective-permute-start.27 = (bf16[720,256]{1,0:T(8,128)(2,1)S(1)}, bf16[720,256]{1,0:T(8,128)(2,1)S(1)}, u32[]{:S(2)}, u32[]{:S(2)}) collective-permute-start(bf16[720,256]{1,0:T(8,128)(2,1)S(1)} %get-tuple-element.19), channel_id=1, source_target_pairs={{0,4},{1,5},{2,6},{3,7},{4,0},{5,1},{6,2},{7,3},{8,12},{9,13},{10,... | collective-permute-start | bytes 1105928 | tf_op jit(solution)/shard_map/ppermute | solution.py:186
  245.2 29.7 %collective-permute-start.28 = (bf16[720,256]{1,0:T(8,128)(2,1)S(1)}, bf16[720,256]{1,0:T(8,128)(2,1)S(1)}, u32[]{:S(2)}, u32[]{:S(2)}) collective-permute-start(bf16[720,256]{1,0:T(8,128)(2,1)S(1)} %get-tuple-element.18), channel_id=1, source_target_pairs={{0,5},{1,4},{2,7},{3,6},{4,1},{5,0},{6,3},{7,2},{8,13},{9,12},{10,... | collective-permute-start | bytes 1105928 | tf_op jit(solution)/shard_map/ppermute | solution.py:186
  (13 other events, 34.8 us)
Sparse Core Ops, SparseCore 0:
  9.2 79.9 all-gather.2

commit v2 on v0

--- a/solution.py
+++ b/solution.py
@@ -1,29 +1,441 @@
+import functools
 import math
 
 import jax
 import jax.numpy as jnp
 from jax import lax
+from jax.experimental import pallas as pl
+from jax.experimental.pallas import tpu as pltpu
 from jax.sharding import PartitionSpec as P
 
 HEAD_WIDTH = 64
 WINDOW_KEYS = 128
-
+SLICES = 4
 
 rope_base = 150000.0
-
-
-def from_behind(value, axis, by):
+vmem_bytes = 48 * 1024 * 1024
+log2e = math.log2(math.e)
+score_scale = HEAD_WIDTH**-0.5 * log2e
+
+
+def shift(value, axis, by):
     devices = lax.axis_size(axis)
     pairs = [(i, i + by) for i in range(devices) if 0 <= i + by < devices]
     return lax.ppermute(value, axis, pairs)
 
 
+def angles_of(places):
+    half_dim = HEAD_WIDTH // 2
+    frequency = jnp.exp(
+        jnp.arange(half_dim, dtype=jnp.float32) * (-2.0 * math.log(rope_base) / HEAD_WIDTH)
+    )
+    return places.astype(jnp.float32)[None, :] * frequency[:, None]
+
+
+def columns_dot(one, other):
+    return lax.dot_general(one, other, (((0,), (0,)), ((), ())), preferred_element_type=jnp.float32)
+
+
+def gather_project_kernel(zs, *refs, depth, cuts):
+    pieces, (w0, w1, w2, total, last, held, sems) = refs[: len(cuts)], refs[len(cuts) :]
+    copies = []
+    for i, (block, start, rows) in enumerate(cuts):
+        copy = pltpu.make_async_copy(pieces[i], held.at[block, pl.ds(start, rows)], sems.at[i])
+        copy.start()
+        copies.append((block, copy))
+    for block in range(held.shape[0]):
+        for at, copy in copies:
+            if at == block:
+                copy.wait()
+        term = None
+        for k, w in enumerate((w0, w1, w2)):
+            rows = pl.ds(pl.multiple_of(zs[k] * depth, 16), depth)
+            more = columns_dot(w[...], held[block, rows, :])
+            term = more if term is None else term + more
+        total[block] = term
+        last[block] = held[block, pl.ds(pl.multiple_of(zs[3] * depth, 16), depth), :]
+
+
+def gather_project(zs, pieces, cuts, weights):
+    blocks = 1 + max(at for at, _, _ in cuts)
+    features = max(start + rows for _, start, rows in cuts)
+    block = pieces[0].shape[1]
+    depth, width = weights[0].shape
+    return pl.pallas_call(
+        functools.partial(gather_project_kernel, depth=depth, cuts=cuts),
+        in_specs=[pl.BlockSpec(memory_space=pltpu.SMEM)]
+        + [pl.BlockSpec(memory_space=pl.ANY)] * len(pieces)
+        + [pl.BlockSpec(memory_space=pltpu.VMEM)] * 3,
+        out_specs=[pl.BlockSpec(memory_space=pltpu.VMEM)] * 2,
+        out_shape=[
+            jax.ShapeDtypeStruct((blocks, width, block), jnp.float32),
+            jax.ShapeDtypeStruct((blocks, depth, block), jnp.bfloat16),
+        ],
+        scratch_shapes=[
+            pltpu.VMEM((blocks, features, block), jnp.bfloat16),
+            pltpu.SemaphoreType.DMA((len(pieces),)),
+        ],
+        compiler_params=pltpu.CompilerParams(vmem_limit_bytes=vmem_bytes),
+        cost_estimate=pl.CostEstimate(
+            flops=6 * width * depth * blocks * block,
+            bytes_accessed=2 * features * blocks * block,
+            transcendentals=0,
+        ),
+        name="gather_project",
+    )(zs, *pieces, *weights)
+
+
+def project_kernel(order, before_a, before_b, last_a, last_b, w, cosine, sine, kv_out, q_out):
+    half = HEAD_WIDTH // 2
+    block = before_a.shape[2]
+    step = before_a.shape[0] + before_b.shape[0]
+    for at in range(step):
+        before, last = ((before_a, last_a), (before_b, last_b))[at // before_a.shape[0]]
+        i = at % before_a.shape[0]
+        total = before[i] + columns_dot(w[...], last[i])
+        place = order[pl.program_id(0) * step + at]
+        lanes = pl.ds(pl.multiple_of(place * block, block), block)
+        cos, sin = cosine[:, lanes], sine[:, lanes]
+
+        def rotated(at_row):
+            lower, upper = total[at_row : at_row + half], total[at_row + half : at_row + 2 * half]
+            return jnp.concatenate([lower * cos - upper * sin, upper * cos + lower * sin], axis=0)
+
+        kv_out[0:HEAD_WIDTH, lanes] = rotated(0).astype(jnp.bfloat16)
+        kv_out[HEAD_WIDTH : 2 * HEAD_WIDTH, lanes] = total[HEAD_WIDTH : 2 * HEAD_WIDTH].astype(jnp.bfloat16)
+        for h in range(q_out.shape[1] // HEAD_WIDTH):
+            q_out[place, h * HEAD_WIDTH : (h + 1) * HEAD_WIDTH] = (
+                rotated((h + 2) * HEAD_WIDTH) * score_scale
+            ).astype(jnp.bfloat16)
+
+
+def project(order, before, last, w, cosine, sine):
+    blocks, depth, block = last[0].shape
+    blocks *= 2
+    width = w.shape[1]
+    kv_width = 2 * HEAD_WIDTH
+    pair = lambda *shape: pl.BlockSpec((2, *shape), lambda j, order: (j, 0, 0))
+    whole = lambda *shape: pl.BlockSpec(shape, lambda j, order: (0,) * len(shape))
+    angle = whole(HEAD_WIDTH // 2, blocks * block)
+    return pl.pallas_call(
+        project_kernel,
+        grid_spec=pltpu.PrefetchScalarGridSpec(
+            num_scalar_prefetch=1,
+            grid=(2,),
+            in_specs=[
+                pair(width, block),
+                pair(width, block),
+                pair(depth, block),
+                pair(depth, block),
+                whole(depth, width),
+                angle,
+                angle,
+            ],
+            out_specs=[whole(kv_width, blocks * block), whole(blocks, width - kv_width, block)],
+        ),
+        out_shape=[
+            jax.ShapeDtypeStruct((kv_width, blocks * block), jnp.bfloat16),
+            jax.ShapeDtypeStruct((blocks, width - kv_width, block), jnp.bfloat16),
+        ],
+        compiler_params=pltpu.CompilerParams(vmem_limit_bytes=vmem_bytes),
+        cost_estimate=pl.CostEstimate(
+            flops=2 * width * depth * blocks * block,
+            bytes_accessed=2 * depth * (blocks * block + width),
+            transcendentals=0,
+        ),
+        name="project",
+    )(order, *before, *last, w, cosine, sine)
+
+
+def attend_kernel(first, sinks, q, kv, *refs, low):
+    *tail, give, keep, keys, values = refs
+    window = WINDOW_KEYS
+    width, block = q.shape[1:]
+    heads = width // HEAD_WIDTH
+    parts = block // window
+    span = 4 * block
+    if tail:
+        keys[:window] = jnp.transpose(tail[0][:HEAD_WIDTH])
+        values[:, :window] = tail[0][HEAD_WIDTH:]
+        keys[window:] = jnp.transpose(kv[:HEAD_WIDTH, low : low + span])
+        values[:, window:] = kv[HEAD_WIDTH:, low : low + span]
+    else:
+        keys[...] = jnp.transpose(kv[:HEAD_WIDTH, low - window : low + span])
+        values[...] = kv[HEAD_WIDTH:, low - window : low + span]
+
+    row = lax.broadcasted_iota(jnp.int32, (2 * window, window), 0)
+    lane = lax.broadcasted_iota(jnp.int32, (2 * window, window), 1)
+    seen = (row > lane) & (row <= lane + window)
+    left = lax.broadcasted_iota(jnp.int32, (1, 2 * window), 1) < window
+    core = first[1]
+    units = [(mine, side, part) for mine in range(2) for side in range(2) for part in range(parts)]
+
+    def at_block(unit):
+        mine, side, _ = unit
+        return (core if mine else 1 - core) * 2 + side
+
+    def at_token(unit):
+        return pl.multiple_of(at_block(unit) * block + unit[2] * window, window)
+
+    def bias_of(unit):
+        allowed = seen
+        if tail and unit[1:] == (0, 0):
+            allowed = seen & (row >= jnp.where(first[0] + at_block(unit) == 0, window, 0))
+        bias = jnp.where(allowed, 0.0, -jnp.inf)
+        return jnp.concatenate([bias, bias], axis=1)
+
+    def scores_of(unit):
+        lanes = slice(unit[2] * window, (unit[2] + 1) * window)
+        key_rows = keys[pl.ds(at_token(unit), 2 * window), :]
+        out = []
+        for h in range(0, heads, 2):
+            rows = slice(h * HEAD_WIDTH, (h + 1) * HEAD_WIDTH), slice((h + 1) * HEAD_WIDTH, (h + 2) * HEAD_WIDTH)
+            pair = jnp.concatenate([q[at_block(unit), r, lanes] for r in rows], axis=1)
+            out.append(jnp.dot(key_rows, pair, preferred_element_type=jnp.float32))
+        return out
+
+    def weights_of(unit, scores):
+        bias = bias_of(unit)
+        out = []
+        for i, score in enumerate(scores):
+            score = score + bias
+            sink = jnp.where(left, sinks[2 * i], sinks[2 * i + 1]) * log2e
+            top = jnp.maximum(jnp.max(score, axis=0, keepdims=True), sink)
+            exponent = jnp.exp2(score - top)
+            denominator = jnp.sum(exponent, axis=0, keepdims=True) + jnp.exp2(sink - top)
+            out.append((exponent.astype(jnp.bfloat16), 1.0 / denominator))
+        return out
+
+    def mix(unit, weights):
+        mine, side, part = unit
+        lanes = slice(part * window, (part + 1) * window)
+        value_rows = values[:, pl.ds(at_token(unit), 2 * window)]
+        out = keep if mine else give
+        for i, (weight, scale) in enumerate(weights):
+            mixture = jnp.dot(value_rows, weight, preferred_element_type=jnp.float32)
+            result = (mixture * scale).astype(jnp.bfloat16)
+            for j in range(2):
+                rows = slice((2 * i + j) * HEAD_WIDTH, (2 * i + j + 1) * HEAD_WIDTH)
+                out[side, rows, lanes] = result[:, j * window : (j + 1) * window]
+
+    ahead = scores_of(units[0])
+    behind = None
+    for n, unit in enumerate(units):
+        scores = ahead
+        if n + 1 < len(units):
+            ahead = scores_of(units[n + 1])
+        weights = weights_of(unit, scores)
+        if behind is not None:
+            mix(*behind)
+        behind = unit, weights
+    mix(*behind)
+
+
+def attend(first, sinks, q, kv, half, tail=()):
+    _, width, block = q.shape
+    window = WINDOW_KEYS
+    return pl.pallas_call(
+        functools.partial(attend_kernel, low=half * 4 * block),
+        grid_spec=pltpu.PrefetchScalarGridSpec(
+            num_scalar_prefetch=2,
+            grid=(1,),
+            in_specs=[pl.BlockSpec((4, width, block), lambda i, *_: (half, 0, 0))]
+            + [pl.BlockSpec(x.shape, lambda i, *_: (0, 0)) for x in (kv, *tail)],
+            out_specs=[pl.BlockSpec((2, width, block), lambda i, *_: (0, 0, 0))] * 2,
+            scratch_shapes=[
+                pltpu.VMEM((4 * block + window, HEAD_WIDTH), jnp.bfloat16),
+                pltpu.VMEM((HEAD_WIDTH, 4 * block + window), jnp.bfloat16),
+            ],
+        ),
+        out_shape=[jax.ShapeDtypeStruct((2, width, block), jnp.bfloat16)] * 2,
+        compiler_params=pltpu.CompilerParams(vmem_limit_bytes=vmem_bytes),
+        cost_estimate=pl.CostEstimate(
+            flops=32 * width * block * window, bytes_accessed=16 * width * block, transcendentals=0
+        ),
+        name="attend",
+    )(first, sinks, q, kv, *tail)
+
+
+def sums_kernel(sides, w_near, w_far, near0, near1, far0, far1, own, to_x, to_y, cross_a, cross_b):
+    row, side = sides[0], sides[1]
+    middle = cross_a.shape[0]
+
+    def of(near, far, place):
+        total = jnp.dot(w_near[...], near[place], preferred_element_type=jnp.float32)
+        return total + jnp.dot(w_far[...], far[place], preferred_element_type=jnp.float32)
+
+    def all_of(mine, other):
+        cross = of(*other, 1 - side).astype(jnp.bfloat16)
+        cross_a[...] = cross[:middle]
+        cross_b[...] = cross[middle:]
+        to_x[...] = of(*mine, 1 - side).astype(jnp.bfloat16)
+        to_y[...] = of(*other, side).astype(jnp.bfloat16)
+        own[...] = of(*mine, side)
+
+    @pl.when(row == 0)
+    def _():
+        all_of((near0, far0), (near1, far1))
+
+    @pl.when(row == 1)
+    def _():
+        all_of((near1, far1), (near0, far0))
+
+
+def output_sums(sides, w_near, w_far, near, far):
+    depth = w_near.shape[0]
+    block = near[0].shape[2]
+    vmem = pl.BlockSpec(memory_space=pltpu.VMEM)
+    bf16 = lambda rows: jax.ShapeDtypeStruct((rows, block), jnp.bfloat16)
+    return pl.pallas_call(
+        sums_kernel,
+        in_specs=[pl.BlockSpec(memory_space=pltpu.SMEM)] + [vmem] * 6,
+        out_specs=[vmem] * 5,
+        out_shape=[
+            jax.ShapeDtypeStruct((depth, block), jnp.float32),
+            bf16(depth),
+            bf16(depth),
+            bf16(depth // 2),
+            bf16(depth - depth // 2),
+        ],
+        compiler_params=pltpu.CompilerParams(vmem_limit_bytes=vmem_bytes),
+        cost_estimate=pl.CostEstimate(
+            flops=16 * w_near.shape[1] * depth * block,
+            bytes_accessed=16 * depth * block,
+            transcendentals=0,
+        ),
+        name="output_sums",
+    )(sides, w_near, w_far, *near, *far)
+
+
+def slab_body(tokens, w_query, w_kv, w_out, sinks):
+    devices = lax.axis_size("seq")
+    slabs = devices // SLICES
+    tp = lax.axis_size("tp")
+    place = lax.axis_index("seq")
+    slab, part = place // SLICES, place % SLICES
+    side = lax.axis_index("tp")
+    block = tokens.shape[0]
+    blocks = SLICES * tp
+    both = ("seq", "tp")
+
+    def swap(value, flip_seq, flip_tp):
+        pairs = [
+            (s * tp + t, (s ^ flip_seq) * tp + (t ^ flip_tp)) for s in range(devices) for t in range(tp)
+        ]
+        return lax.ppermute(value, both, pairs)
+
+    def turn(value):
+        pairs = [(s, (s + SLICES) % devices) for s in range(devices)]
+        return lax.ppermute(value, "seq", pairs)
+
+    tie = lambda *values: lax.optimization_barrier(values)
+
+    core, row = part % 2, part // 2
+    order = jnp.stack(
+        [
+            (row ^ r) * 2 * tp + (core ^ c) * tp + (side ^ t)
+            for c in range(2)
+            for r in range(2)
+            for t in range(tp)
+        ]
+    ).astype(jnp.int32)
+
+    def of_head(weight, head):
+        width = weight.shape[1] // SLICES
+        return lax.dynamic_slice_in_dim(weight, head * width, width, 1)
+
+    def by(flag, one, other):
+        joined = jnp.concatenate([one, other], axis=0)
+        return jnp.where(flag == 1, jnp.concatenate([other, one], axis=0), joined)
+
+    def of_chip(make):
+        return by(core, make(part), swap(make(part ^ 1), 1, 0))
+
+    def of_next_chip(make):
+        return by(core, swap(make(part ^ 2), 2, 0), swap(make(part ^ 3), 3, 0))
+
+    def in_head(head):
+        return jnp.concatenate([of_head(w_kv, head), of_head(w_query, head)], axis=1)
+
+    def out_head(head):
+        return of_head(w_out, head)
+
+    own = tokens.T
+    features = own.shape[0]
+    upper = features // 2
+    near, far = [of_chip(in_head)], [of_next_chip(in_head)]
+    near.append(turn(near[0]))
+    from_x = swap(own[:upper], 0, 1), swap(own[upper:], 0, 1)
+    near[1], far[0], own_late = tie(near[1], far[0], own)
+    far.append(turn(far[0]))
+    near.append(turn(near[1]))
+    from_y = swap(own_late[:upper], 2, 0), swap(own_late[upper:], 2, 0)
+    far.append(turn(far[1]))
+    near.append(turn(near[2]))
+    far.append(turn(far[2]))
+    diagonal = swap(from_x[0], 2, 0), swap(from_y[1], 0, 1)
+    weights_in = [by(row, n, f) for n, f in zip(near[:-1], far[:-1])]
+
+    first = slab * (blocks * block)
+    places = first + jnp.arange(blocks * block, dtype=jnp.int32)
+    angles = angles_of(places)
+    slabs_held = (slab - jnp.arange(slabs, dtype=jnp.int32)) % slabs
+    whole = (0, 0, features)
+    parts = [(0, upper), (upper, features - upper)]
+    before_a, last_a = gather_project(
+        slabs_held,
+        [own, *from_x, swap(own, 1, 0), *(swap(x, 1, 0) for x in from_x)],
+        [whole, *((1, *p) for p in parts), (2, *whole[1:]), *((3, *p) for p in parts)],
+        weights_in,
+    )
+    before_b, last_b = gather_project(
+        slabs_held,
+        [*from_y, *diagonal, *(swap(x, 1, 0) for x in (*from_y, *diagonal))],
+        [(at, *p) for at in range(4) for p in parts],
+        weights_in,
+    )
+
+    near_out, far_out = [of_chip(out_head)], [of_next_chip(out_head)]
+    near_out[0], far[-1] = tie(near_out[0], far[-1])
+    near_out.append(turn(near_out[0]))
+    kv, q = project(order, (before_a, before_b), (last_a, last_b), by(row, near[-1], far[-1]), jnp.cos(angles), jnp.sin(angles))
+    kv_tail = shift(kv[:, -WINDOW_KEYS:], "seq", SLICES)
+    heads = sinks.shape[0] // SLICES
+    head_sinks = lax.dynamic_slice_in_dim(sinks, part * heads, heads, 0)
+    first_row = jnp.stack([first, core])
+    mixed = [None, attend(first_row, head_sinks, q, kv, 1)]
+    q, near_out[1], far_out[0] = tie(q, near_out[1], far_out[0])
+    far_out.append(turn(far_out[0]))
+    near_out.append(turn(near_out[1]))
+    mixed[0] = attend(first_row, head_sinks, q, kv, 0, (kv_tail,))
+    came = [swap(give, 1, 0) for give, _ in mixed]
+    kept = [keep for _, keep in mixed]
+
+    sides = jnp.stack([row, side])
+    depth = 2 * near_out[0].shape[0]
+    middle = depth // 2
+    result = jnp.zeros((features, block), jnp.bfloat16)
+    for k in range(slabs):
+        weight = by(row, near_out[k], far_out[k])
+        total, to_x, to_y, cross_a, cross_b = output_sums(sides, weight, swap(weight, 1, 0), kept, came)
+        if k == 0:
+            total, near_out[2], far_out[1] = tie(total, near_out[2], far_out[1])
+            far_out.append(turn(far_out[1]))
+            near_out.append(turn(near_out[2]))
+            far_out.append(turn(far_out[2]))
+        by_x = swap(cross_a, 0, 1).astype(jnp.float32)
+        by_y = swap(cross_b, 2, 0).astype(jnp.float32)
+        to_x = jnp.concatenate([to_x[:middle], (to_x[middle:].astype(jnp.float32) + by_y).astype(jnp.bfloat16)], axis=0)
+        to_y = jnp.concatenate([(to_y[:middle].astype(jnp.float32) + by_x).astype(jnp.bfloat16), to_y[middle:]], axis=0)
+        total += swap(to_x, 0, 1).astype(jnp.float32)
+        total += swap(to_y, 2, 0).astype(jnp.float32)
+        result = lax.dynamic_update_slice_in_dim(result, total.astype(jnp.bfloat16), slabs_held[k] * depth, 0)
+    return result.T
+
+
 def rotary(vectors, places):
     half_dim = vectors.shape[-1] // 2
-    frequency = jnp.exp(
-        jnp.arange(half_dim, dtype=jnp.float32) * (-2.0 * math.log(rope_base) / vectors.shape[-1])
-    )
-    angles = places.astype(jnp.float32)[:, None, None] * frequency[None, None, :]
+    angles = angles_of(places).T[:, None, :]
     cosine = jnp.cos(angles)
     sine = jnp.sin(angles)
     lower_half = vectors[..., :half_dim]
@@ -33,7 +445,7 @@
     )
 
 
-def attend(query_rows, key_value_rows, sink_scores, query_pos, key_pos):
+def attend_rows(query_rows, key_value_rows, sink_scores, query_pos, key_pos):
     key_part = key_value_rows[:, :, 0, :]
     value_part = key_value_rows[:, :, 1, :]
     scores = jnp.einsum(
@@ -59,7 +471,7 @@
     return jnp.stack([key_part, split_key_value[:, :, 1, :]], axis=2).astype(jnp.bfloat16)
 
 
-def body(tokens, w_query, w_kv, w_out, sinks):
+def row_body(tokens, w_query, w_kv, w_out, sinks):
     token_rows = lax.all_gather(tokens, "tp", axis=0, tiled=True)
     row_count = token_rows.shape[0]
     kv_width = w_kv.shape[1]
@@ -84,11 +496,11 @@
     ).astype(jnp.bfloat16)
     query_rows = query_rows.reshape(row_count, kv_heads, head_groups, HEAD_WIDTH)
     local_kv = finish(kv_sum, query_pos, kv_heads).reshape(row_count, kv_width)
-    kv_tail = from_behind(local_kv[row_count - WINDOW_KEYS :], "seq", 1)
+    kv_tail = shift(local_kv[row_count - WINDOW_KEYS :], "seq", 1)
     key_value_rows = jnp.concatenate([kv_tail, local_kv], axis=0).reshape(
         row_count + WINDOW_KEYS, kv_heads, 2, HEAD_WIDTH
     )
-    attended = attend(
+    attended = attend_rows(
         query_rows, key_value_rows, sinks.reshape(kv_heads, head_groups), query_pos, key_pos
     ).reshape(row_count, q_width)
     out_terms = lax.dot_general(
@@ -97,11 +509,21 @@
         (((1,), (1,)), ((), ())),
         preferred_element_type=jnp.float32,
     )
-    result = lax.psum_scatter(out_terms.astype(jnp.bfloat16), "tp", scatter_dimension=0, tiled=True)
-    return result
+    return lax.psum_scatter(out_terms.astype(jnp.bfloat16), "tp", scatter_dimension=0, tiled=True)
 
 
 def solution(mesh):
     in_specs = (P(("seq", "tp"), None), P("seq", "tp"), P("seq", "tp"), P("seq", "tp"), P("tp"))
     out_specs = P(("seq", "tp"), None)
+
+    def body(tokens, w_query, w_kv, w_out, sinks):
+        by_slabs = (
+            w_kv.shape[1] == SLICES * 2 * HEAD_WIDTH
+            and mesh.shape["tp"] == 2
+            and mesh.shape["seq"] == 4 * SLICES
+            and tokens.shape[0] % (2 * WINDOW_KEYS) == 0
+            and (w_query.shape[0] * SLICES) % 16 == 0
+        )
+        return (slab_body if by_slabs else row_body)(tokens, w_query, w_kv, w_out, sinks)
+
     return jax.shard_map(body, mesh=mesh, in_specs=in_specs, out_specs=out_specs, check_vma=False)

time: 368 us -> 244 us (0.66)
  waiting for transfers between devices: 243 us -> 119 us
  matrix products: 60.9 us -> 0 us
  Pallas kernels: 0 us -> 46.4 us
  starting transfers between devices: 1.9 us -> 47.6 us
  local copies, waits for them, and re-layouts: 27 us -> 12.1 us
  between operations: 13.3 us -> 3.32 us
  other arithmetic: 21.1 us -> 15.3 us
    all_gather x4 -> x0, waiting for transfers between devices: 200 us -> none  [the longest x1 93.2 us: body(): lax.all_gather(w_query, 'seq', axis=0, tiled=True)]
    ppermute x1 -> x54, waiting for transfers between devices: 0.59 us -> 119 us  [the longest x41 75.8 us: swap(): return lax.ppermute(value, both, pairs)]
    dot_general x5 -> x0, matrix products: 60.9 us -> none  [the longest x1 18.3 us: attend(): jnp.einsum('hgqk,khd->qhgd', weights, value_part, preferred_element_type=...]
    pallas_call x0 -> x9, Pallas kernels: none -> 46.4 us  [the longest x2 23.6 us: gather_project(): pl.pallas_call(functools.partial(gather_project_kernel, depth=depth, cuts...]
    ppermute x1 -> x54, starting transfers between devices: 1.75 us -> 47.6 us  [the longest x41 31.2 us: swap(): return lax.ppermute(value, both, pairs)]
    reduce_scatter x1 -> x0, waiting for transfers between devices: 39.5 us -> none  [body(): lax.psum_scatter(out_terms.astype(jnp.bfloat16), 'tp', scatter_dimension=...]
    unnamed x3 -> x46, local copies, waits for them, and re-layouts: 26.3 us -> 4.89 us
    reduce_sum x1 -> x0, other arithmetic: 19.3 us -> none  [attend(): jnp.sum(exponent, axis=-1) + jnp.exp(sink_scores[:, :, None] - row_max)]
  transfers between devices with their start and end apart: 6 -> 54, of which waited for: 6 -> 21; matrix products, arithmetic and copies ran while one was open for 23% -> 8% of each run, Pallas kernels for 0% -> 19%
where the time goes in v2:
time: 244 us
  waiting for transfers between devices  119 us (49%)
  starting transfers between devices  47.6 us (20%)
  Pallas kernels  46.4 us (19%)
  other arithmetic  15.3 us (6%)
  local copies, waits for them, and re-layouts  12.1 us (5%)
  between operations  3.32 us (1%)
    ppermute x41, waiting for transfers between devices, swap(): return lax.ppermute(value, both, pairs)  75.8 us
    ppermute x12, waiting for transfers between devices, turn(): return lax.ppermute(value, 'seq', pairs)  43.5 us
    ppermute x41, starting transfers between devices, swap(): return lax.ppermute(value, both, pairs)  31.2 us
    pallas_call x2, Pallas kernels, gather_project(): pl.pallas_call(functools.partial(gather_project_kernel, depth=depth, cuts...  23.6 us
    ppermute x12, starting transfers between devices, turn(): return lax.ppermute(value, 'seq', pairs)  13.4 us
    select_n x12, other arithmetic, by(): return jnp.where(flag == 1, jnp.concatenate([other, one], axis=0), joined)  10.4 us
    pallas_call x4, Pallas kernels, output_sums(): pl.pallas_call(sums_kernel, in_specs=[pl.BlockSpec(memory_space=pltpu.SME...  8.94 us
    pallas_call x2, Pallas kernels, attend(): pl.pallas_call(functools.partial(attend_kernel, low=half * 4 * block), gr...  7.05 us
  transfers between devices with their start and end apart: 54, of which 21 were waited for; matrix products, arithmetic and copies ran while one was open for 8% of the time, Pallas kernels for 19%

profile of v2, /device:TPU:0, one launch (start us, length us, event | category | flops | bytes accessed | tf_op | source)
XLA Modules:
  0.0 243.9 jit_solution(12910163616861715985)
XLA Ops:
  2.0 2.7 %collective-permute-start.7 = (bf16[180,640]{1,0:T(8,128)(2,1)S(1)}, bf16[180,640]{1,0:T(8,128)(2,1)S(1)}, u32[]{:S(2)}, u32[]{:S(2)}) collective-permute-start(bf16[180,640]{1,0:T(8,128)(2,1)S(1)} %pad_maximum_fusion.9), channel_id=1, source_target_pairs={{0,6},{1,7},{2,4},{3,5},{4,2},{5,3},{6,0},{7,1},{8,14},{9,15},{10,... | collective-permute-start | bytes 691208 | tf_op jit(solution)/shard_map/ppermute | solution.py:325
  5.0 2.1 collective-permute-start.6
  12.2 3.8 %collective-permute-done.8 = bf16[180,640]{1,0:T(8,128)(2,1)S(1)} collective-permute-done((bf16[180,640]{1,0:T(8,128)(2,1)S(1)}, bf16[180,640]{1,0:T(8,128)(2,1)S(1)}, u32[]{:S(2)}, u32[]{:S(2)}) %collective-permute-start.8) | collective-permute-done | bytes 230432 | tf_op jit(solution)/shard_map/ppermute | solution.py:325
  17.0 2.6 %collective-permute-done.6 = bf16[360,640]{1,0:T(8,128)(2,1)} collective-permute-done((bf16[360,640]{1,0:T(8,128)(2,1)S(1)}, bf16[360,640]{1,0:T(8,128)(2,1)}, u32[]{:S(2)}, u32[]{:S(2)}) %collective-permute-start.6) | collective-permute-done | bytes 460832 | tf_op jit(solution)/shard_map/ppermute | solution.py:329
  21.2 2.5 %fusion.5 = (bf16[1440,256]{1,0:T(8,128)(2,1)}, bf16[1440,256]{1,0:T(8,128)(2,1)}) fusion(bf16[2880,256]{1,0:T(8,128)(2,1)} %bitcast.10.refs_0_), kind=kLoop, calls=%fused_computation.61 | loop fusion | bytes 2949120 | tf_op jit(solution)/shard_map/slice | solution.py:372
  24.4 2.8 %collective-permute-done.25 = bf16[180,512]{1,0:T(8,128)(2,1)S(1)} collective-permute-done((bf16[180,512]{1,0:T(8,128)(2,1)S(1)}, bf16[180,512]{1,0:T(8,128)(2,1)S(1)}, u32[]{:S(2)}, u32[]{:S(2)}) %collective-permute-start.25) | collective-permute-done | bytes 184352 | tf_op jit(solution)/shard_map/ppermute | solution.py:325
  29.6 12.7 %collective-permute-done.1.refs_2_ = bf16[1440,256]{1,0:T(8,128)(2,1)S(1)} collective-permute-done((bf16[1440,256]{1,0:T(8,128)(2,1)S(1)}, bf16[1440,256]{1,0:T(8,128)(2,1)S(1)}, u32[]{:S(2)}, u32[]{:S(2)}) %collective-permute-start.1) | collective-permute-done | bytes 737312 | tf_op jit(solution)/shard_map/ppermute | solution.py:325
  44.8 13.3 %collective-permute-done.11 = bf16[360,640]{1,0:T(8,128)(2,1)} collective-permute-done((bf16[360,640]{1,0:T(8,128)(2,1)}, bf16[360,640]{1,0:T(8,128)(2,1)}, u32[]{:S(2)}, u32[]{:S(2)}) %collective-permute-start.11) | collective-permute-done | bytes 460832 | tf_op jit(solution)/shard_map/ppermute | solution.py:329
  60.5 14.1 %collective-permute-done.14.refs_2_ = bf16[1440,256]{1,0:T(8,128)(2,1)} collective-permute-done((bf16[1440,256]{1,0:T(8,128)(2,1)S(1)}, bf16[1440,256]{1,0:T(8,128)(2,1)}, u32[]{:S(2)}, u32[]{:S(2)}) %collective-permute-start.14) | collective-permute-done | bytes 737312 | tf_op jit(solution)/shard_map/ppermute | solution.py:325
  82.3 10.2 %collective-permute-done.15.refs_3_ = bf16[1440,256]{1,0:T(8,128)(2,1)S(1)} collective-permute-done((bf16[1440,256]{1,0:T(8,128)(2,1)S(1)}, bf16[1440,256]{1,0:T(8,128)(2,1)S(1)}, u32[]{:S(2)}, u32[]{:S(2)}) %collective-permute-start.15) | collective-permute-done | bytes 737312 | tf_op jit(solution)/shard_map/ppermute | solution.py:325
  92.9 2.2 collective-permute-start.22
  98.3 10.7 %gather_project.2 = (f32[4,640,256]{2,1,0:T(8,128)}, bf16[4,720,256]{2,1,0:T(8,128)(2,1)}) custom-call(s32[4]{0:T(128)S(1)} %and_select_fusion.zs, bf16[2880,256]{1,0:T(8,128)(2,1)} %bitcast.10.refs_0_, bf16[1440,256]{1,0:T(8,128)(2,1)S(1)} %collective-permute-done.refs_1_, bf16[1440,256]{1,0:T(8,128)(2,1)S(1)} %collective-permute-done.1.refs_2_, ...), custom_call_target="tpu_custom_call" | custom-call | flops 2831155200 | bytes 5898240 | tf_op jit(solution)/shard_map/gather_project/pallas_call | solution.py:64
  111.2 12.9 %gather_project.3 = (f32[4,640,256]{2,1,0:T(8,128)}, bf16[4,720,256]{2,1,0:T(8,128)(2,1)}) custom-call(s32[4]{0:T(128)S(1)} %and_select_fusion.zs, bf16[1440,256]{1,0:T(8,128)(2,1)S(1)} %collective-permute-done.12.refs_0_, bf16[1440,256]{1,0:T(8,128)(2,1)S(1)} %collective-permute-done.13.refs_1_, bf16[1440,256]{1,0:T(8,128)(2,1)} %collective-permute-done.14.refs_2_, ...), custom_call_target="tpu_custom_call" | custom-call | flops 2831155200 | bytes 5898240 | tf_op jit(solution)/shard_map/gather_project/pallas_call | solution.py:64
  125.5 6.8 %project.1 = (bf16[128,2048]{1,0:T(8,128)(2,1)S(1)}, bf16[8,512,256]{2,1,0:T(8,128)(2,1)}) custom-call(s32[8]{0:T(128)S(1)} %stack.56.order, f32[4,640,256]{2,1,0:T(8,128)} %get-tuple-element.48.before_a, f32[4,640,256]{2,1,0:T(8,128)} %get-tuple-element.50.before_b, bf16[4,720,256]{2,1,0:T(8,128)(2,1)S(1)} %copy-done.1, bf16[4,720,256]{2,1,0:T(8,128)(2,1)S(1)} %copy-done.2, ...), custom_call_target="tpu_custom_call" | custom-call | flops 1887436800 | bytes 3870720 | tf_op jit(solution)/shard_map/project/pallas_call | solution.py:120
  132.7 3.0 %collective-permute-start.27 = (bf16[128,128]{1,0:T(8,128)(2,1)S(1)}, bf16[128,128]{1,0:T(8,128)(2,1)S(1)}, u32[]{:S(2)}, u32[]{:S(2)}) collective-permute-start(bf16[128,128]{1,0:T(8,128)(2,1)S(1)} %slice.79), channel_id=1, source_target_pairs={{0,8},{2,10},{4,12},{6,14},{8,16},{10,18},{12,20},{14,22},{16,24},... | collective-permute-start | bytes 98312 | tf_op jit(solution)/shard_map/ppermute | solution.py:24
  137.3 3.5 %attend.3 = (bf16[2,512,256]{2,1,0:T(8,128)(2,1)S(1)}, bf16[2,512,256]{2,1,0:T(8,128)(2,1)S(1)}) custom-call(s32[2]{0:T(128)S(1)} %pad_add_fusion.1.first, f32[8]{0:T(128)S(1)} %dynamic_slice.51.sinks, bf16[8,512,256]{2,1,0:T(8,128)(2,1)S(1)} %copy-done, bf16[128,2048]{1,0:T(8,128)(2,1)S(1)} %get-tuple-element.58.kv), custom_call_target="tpu_custom_call" | custom-call | flops 536870912 | bytes 2097152 | tf_op jit(solution)/shard_map/attend/pallas_call | solution.py:237
  141.1 3.5 %attend.2 = (bf16[2,512,256]{2,1,0:T(8,128)(2,1)S(1)}, bf16[2,512,256]{2,1,0:T(8,128)(2,1)S(1)}) custom-call(s32[2]{0:T(128)S(1)} %pad_add_fusion.1.first, f32[8]{0:T(128)S(1)} %dynamic_slice.51.sinks, bf16[8,512,256]{2,1,0:T(8,128)(2,1)S(1)} %copy-done, bf16[128,2048]{1,0:T(8,128)(2,1)S(1)} %get-tuple-element.58.kv, ...), custom_call_target="tpu_custom_call" | custom-call | flops 536870912 | bytes 2097152 | tf_op jit(solution)/shard_map/attend/pallas_call | solution.py:237
  147.4 2.2 output_sums.4
  151.2 7.0 %collective-permute-done.30 = bf16[360,512]{1,0:T(8,128)(2,1)S(1)} collective-permute-done((bf16[360,512]{1,0:T(8,128)(2,1)S(1)}, bf16[360,512]{1,0:T(8,128)(2,1)S(1)}, u32[]{:S(2)}, u32[]{:S(2)}) %collective-permute-start.30) | collective-permute-done | bytes 368672 | tf_op jit(solution)/shard_map/ppermute | solution.py:329
  158.3 7.3 %collective-permute-done.31 = bf16[360,512]{1,0:T(8,128)(2,1)} collective-permute-done((bf16[360,512]{1,0:T(8,128)(2,1)S(1)}, bf16[360,512]{1,0:T(8,128)(2,1)}, u32[]{:S(2)}, u32[]{:S(2)}) %collective-permute-start.31) | collective-permute-done | bytes 368672 | tf_op jit(solution)/shard_map/ppermute | solution.py:329
  169.9 4.6 %collective-permute-done.34 = bf16[360,256]{1,0:T(8,128)(2,1)S(1)} collective-permute-done((bf16[360,256]{1,0:T(8,128)(2,1)S(1)}, bf16[360,256]{1,0:T(8,128)(2,1)S(1)}, u32[]{:S(2)}, u32[]{:S(2)}) %collective-permute-start.34) | collective-permute-done | bytes 184352 | tf_op jit(solution)/shard_map/ppermute | solution.py:325
  182.7 2.2 output_sums.5
  187.0 7.0 %collective-permute-done.48 = bf16[360,512]{1,0:T(8,128)(2,1)S(1)} collective-permute-done((bf16[360,512]{1,0:T(8,128)(2,1)}, bf16[360,512]{1,0:T(8,128)(2,1)S(1)}, u32[]{:S(2)}, u32[]{:S(2)}) %collective-permute-start.48) | collective-permute-done | bytes 368672 | tf_op jit(solution)/shard_map/ppermute | solution.py:329
  194.0 6.2 %collective-permute-done.47 = bf16[360,512]{1,0:T(8,128)(2,1)S(1)} collective-permute-done((bf16[360,512]{1,0:T(8,128)(2,1)}, bf16[360,512]{1,0:T(8,128)(2,1)S(1)}, u32[]{:S(2)}, u32[]{:S(2)}) %collective-permute-start.47) | collective-permute-done | bytes 368672 | tf_op jit(solution)/shard_map/ppermute | solution.py:329
  202.9 2.2 output_sums.6
  205.5 2.6 %collective-permute-done.39 = bf16[360,256]{1,0:T(8,128)(2,1)S(1)} collective-permute-done((bf16[360,256]{1,0:T(8,128)(2,1)S(1)}, bf16[360,256]{1,0:T(8,128)(2,1)S(1)}, u32[]{:S(2)}, u32[]{:S(2)}) %collective-permute-start.39) | collective-permute-done | bytes 184352 | tf_op jit(solution)/shard_map/ppermute | solution.py:325
  210.1 2.6 %collective-permute-done.43 = bf16[360,256]{1,0:T(8,128)(2,1)S(1)} collective-permute-done((bf16[360,256]{1,0:T(8,128)(2,1)S(1)}, bf16[360,256]{1,0:T(8,128)(2,1)S(1)}, u32[]{:S(2)}, u32[]{:S(2)}) %collective-permute-start.43) | collective-permute-done | bytes 184352 | tf_op jit(solution)/shard_map/ppermute | solution.py:325
  214.3 2.2 output_sums.7
  216.9 3.0 %collective-permute-done.45 = bf16[360,256]{1,0:T(8,128)(2,1)S(1)} collective-permute-done((bf16[360,256]{1,0:T(8,128)(2,1)S(1)}, bf16[360,256]{1,0:T(8,128)(2,1)S(1)}, u32[]{:S(2)}, u32[]{:S(2)}) %collective-permute-start.45) | collective-permute-done | bytes 184352 | tf_op jit(solution)/shard_map/ppermute | solution.py:325
  220.4 4.1 %collective-permute-done.50 = bf16[360,256]{1,0:T(8,128)(2,1)S(1)} collective-permute-done((bf16[360,256]{1,0:T(8,128)(2,1)S(1)}, bf16[360,256]{1,0:T(8,128)(2,1)S(1)}, u32[]{:S(2)}, u32[]{:S(2)}) %collective-permute-start.50) | collective-permute-done | bytes 184352 | tf_op jit(solution)/shard_map/ppermute | solution.py:325
  226.1 5.3 %collective-permute-done.52 = bf16[360,256]{1,0:T(8,128)(2,1)S(1)} collective-permute-done((bf16[360,256]{1,0:T(8,128)(2,1)S(1)}, bf16[360,256]{1,0:T(8,128)(2,1)S(1)}, u32[]{:S(2)}, u32[]{:S(2)}) %collective-permute-start.52) | collective-permute-done | bytes 184352 | tf_op jit(solution)/shard_map/ppermute | solution.py:325
  233.6 7.7 %collective-permute-done.51 = bf16[720,256]{1,0:T(8,128)(2,1)S(1)} collective-permute-done((bf16[720,256]{1,0:T(8,128)(2,1)S(1)}, bf16[720,256]{1,0:T(8,128)(2,1)S(1)}, u32[]{:S(2)}, u32[]{:S(2)}) %collective-permute-start.51) | collective-permute-done | bytes 368672 | tf_op jit(solution)/shard_map/ppermute | solution.py:325
  (190 shorter events, 64.9 us)
Async XLA Ops:
  5.0 14.7 %collective-permute-start.6 = (bf16[360,640]{1,0:T(8,128)(2,1)S(1)}, bf16[360,640]{1,0:T(8,128)(2,1)}, u32[]{:S(2)}, u32[]{:S(2)}) collective-permute-start(bf16[360,640]{1,0:T(8,128)(2,1)S(1)} %maximum_select_fusion.8), channel_id=1, source_target_pairs={{0,8},{2,10},{4,12},{6,14},{8,16},{10,18},{12,20},{14,22},{16,24},... | collective-permute-start | bytes 1382408 | tf_op jit(solution)/shard_map/ppermute | solution.py:329
  8.6 20.3 %collective-permute-start = (bf16[1440,256]{1,0:T(8,128)(2,1)S(1)}, bf16[1440,256]{1,0:T(8,128)(2,1)S(1)}, u32[]{:S(2)}, u32[]{:S(2)}) collective-permute-start(bf16[1440,256]{1,0:T(8,128)(2,1)S(1)} %get-tuple-element.90), channel_id=1, source_target_pairs={{0,1},{1,0},{2,3},{3,2},{4,5},{5,4},{6,7},{7,6},{8,9},{9,8},{10,11... | collective-permute-start | bytes 2211848 | tf_op jit(solution)/shard_map/ppermute | solution.py:325
  10.9 31.4 %collective-permute-start.1 = (bf16[1440,256]{1,0:T(8,128)(2,1)S(1)}, bf16[1440,256]{1,0:T(8,128)(2,1)S(1)}, u32[]{:S(2)}, u32[]{:S(2)}) collective-permute-start(bf16[1440,256]{1,0:T(8,128)(2,1)S(1)} %get-tuple-element.89), channel_id=1, source_target_pairs={{0,1},{1,0},{2,3},{3,2},{4,5},{5,4},{6,7},{7,6},{8,9},{9,8},{10,11... | collective-permute-start | bytes 2211848 | tf_op jit(solution)/shard_map/ppermute | solution.py:325
  21.2 21.1 %collective-permute-start.9 = (bf16[360,640]{1,0:T(8,128)(2,1)S(1)}, bf16[360,640]{1,0:T(8,128)(2,1)S(1)}, u32[]{:S(2)}, u32[]{:S(2)}) collective-permute-start(bf16[360,640]{1,0:T(8,128)(2,1)S(1)} %maximum_select_fusion.9), channel_id=1, source_target_pairs={{0,8},{2,10},{4,12},{6,14},{8,16},{10,18},{12,20},{14,22},{16,24},... | collective-permute-start | bytes 1382408 | tf_op jit(solution)/shard_map/ppermute | solution.py:329
  23.7 34.4 %collective-permute-start.13 = (bf16[1440,256]{1,0:T(8,128)(2,1)}, bf16[1440,256]{1,0:T(8,128)(2,1)S(1)}, u32[]{:S(2)}, u32[]{:S(2)}) collective-permute-start(bf16[1440,256]{1,0:T(8,128)(2,1)} %get-tuple-element.87), channel_id=1, source_target_pairs={{0,4},{1,5},{2,6},{3,7},{4,0},{5,1},{6,2},{7,3},{8,12},{9,13},{10,... | collective-permute-start | bytes 2211848 | tf_op jit(solution)/shard_map/ppermute | solution.py:325
  27.2 32.0 %collective-permute-start.12 = (bf16[1440,256]{1,0:T(8,128)(2,1)}, bf16[1440,256]{1,0:T(8,128)(2,1)S(1)}, u32[]{:S(2)}, u32[]{:S(2)}) collective-permute-start(bf16[1440,256]{1,0:T(8,128)(2,1)} %get-tuple-element.88), channel_id=1, source_target_pairs={{0,4},{1,5},{2,6},{3,7},{4,0},{5,1},{6,2},{7,3},{8,12},{9,13},{10,... | collective-permute-start | bytes 2211848 | tf_op jit(solution)/shard_map/ppermute | solution.py:325
  28.8 45.7 %collective-permute-start.14 = (bf16[1440,256]{1,0:T(8,128)(2,1)S(1)}, bf16[1440,256]{1,0:T(8,128)(2,1)}, u32[]{:S(2)}, u32[]{:S(2)}) collective-permute-start(bf16[1440,256]{1,0:T(8,128)(2,1)S(1)} %collective-permute-done.refs_1_), channel_id=1, source_target_pairs={{0,4},{1,5},{2,6},{3,7},{4,0},{5,1},{6,2},{7,3},{8,12},{9,13},{10,... | collective-permute-start | bytes 2211848 | tf_op jit(solution)/shard_map/ppermute | solution.py:325
  42.3 39.9 %collective-permute-start.2 = (bf16[2880,256]{1,0:T(8,128)(2,1)}, bf16[2880,256]{1,0:T(8,128)(2,1)}, u32[]{:S(2)}, u32[]{:S(2)}) collective-permute-start(bf16[2880,256]{1,0:T(8,128)(2,1)} %bitcast.10.refs_0_), channel_id=1, source_target_pairs={{0,2},{1,3},{2,0},{3,1},{4,6},{5,7},{6,4},{7,5},{8,10},{9,11},{10,... | collective-permute-start | bytes 4423688 | tf_op jit(solution)/shard_map/ppermute | solution.py:325
  43.1 15.1 %collective-permute-start.11 = (bf16[360,640]{1,0:T(8,128)(2,1)}, bf16[360,640]{1,0:T(8,128)(2,1)}, u32[]{:S(2)}, u32[]{:S(2)}) collective-permute-start(bf16[360,640]{1,0:T(8,128)(2,1)} %collective-permute-done.6), channel_id=1, source_target_pairs={{0,8},{2,10},{4,12},{6,14},{8,16},{10,18},{12,20},{14,22},{16,24},... | collective-permute-start | bytes 1382408 | tf_op jit(solution)/shard_map/ppermute | solution.py:329
  58.1 23.4 %collective-permute-start.3 = (bf16[1440,256]{1,0:T(8,128)(2,1)S(1)}, bf16[1440,256]{1,0:T(8,128)(2,1)S(1)}, u32[]{:S(2)}, u32[]{:S(2)}) collective-permute-start(bf16[1440,256]{1,0:T(8,128)(2,1)S(1)} %collective-permute-done.refs_1_), channel_id=1, source_target_pairs={{0,2},{1,3},{2,0},{3,1},{4,6},{5,7},{6,4},{7,5},{8,10},{9,11},{10,... | collective-permute-start | bytes 2211848 | tf_op jit(solution)/shard_map/ppermute | solution.py:325
  58.1 23.5 %collective-permute-start.4 = (bf16[1440,256]{1,0:T(8,128)(2,1)S(1)}, bf16[1440,256]{1,0:T(8,128)(2,1)S(1)}, u32[]{:S(2)}, u32[]{:S(2)}) collective-permute-start(bf16[1440,256]{1,0:T(8,128)(2,1)S(1)} %collective-permute-done.1.refs_2_), channel_id=1, source_target_pairs={{0,2},{1,3},{2,0},{3,1},{4,6},{5,7},{6,4},{7,5},{8,10},{9,11},{10,... | collective-permute-start | bytes 2211848 | tf_op jit(solution)/shard_map/ppermute | solution.py:325
  59.2 17.9 %collective-permute-start.10 = (bf16[360,640]{1,0:T(8,128)(2,1)}, bf16[360,640]{1,0:T(8,128)(2,1)S(1)}, u32[]{:S(2)}, u32[]{:S(2)}) collective-permute-start(bf16[360,640]{1,0:T(8,128)(2,1)} %copy-done.16), channel_id=1, source_target_pairs={{0,8},{2,10},{4,12},{6,14},{8,16},{10,18},{12,20},{14,22},{16,24},... | collective-permute-start | bytes 1382408 | tf_op jit(solution)/shard_map/ppermute | solution.py:329
  74.6 17.9 %collective-permute-start.15 = (bf16[1440,256]{1,0:T(8,128)(2,1)S(1)}, bf16[1440,256]{1,0:T(8,128)(2,1)S(1)}, u32[]{:S(2)}, u32[]{:S(2)}) collective-permute-start(bf16[1440,256]{1,0:T(8,128)(2,1)S(1)} %collective-permute-done.13.refs_1_), channel_id=1, source_target_pairs={{0,1},{1,0},{2,3},{3,2},{4,5},{5,4},{6,7},{7,6},{8,9},{9,8},{10,11... | collective-permute-start | bytes 2211848 | tf_op jit(solution)/shard_map/ppermute | solution.py:325
  77.2 15.7 %collective-permute-start.21 = (bf16[360,640]{1,0:T(8,128)(2,1)S(1)}, bf16[360,640]{1,0:T(8,128)(2,1)S(1)}, u32[]{:S(2)}, u32[]{:S(2)}) collective-permute-start(bf16[360,640]{1,0:T(8,128)(2,1)S(1)} %collective-permute-done.10), channel_id=1, source_target_pairs={{0,8},{2,10},{4,12},{6,14},{8,16},{10,18},{12,20},{14,22},{16,24},... | collective-permute-start | bytes 1382408 | tf_op jit(solution)/shard_map/ppermute | solution.py:329
  81.6 29.6 %collective-permute-start.17 = (bf16[1440,256]{1,0:T(8,128)(2,1)S(1)}, bf16[1440,256]{1,0:T(8,128)(2,1)S(1)}, u32[]{:S(2)}, u32[]{:S(2)}) collective-permute-start(bf16[1440,256]{1,0:T(8,128)(2,1)S(1)} %collective-permute-done.13.refs_1_), channel_id=1, source_target_pairs={{0,2},{1,3},{2,0},{3,1},{4,6},{5,7},{6,4},{7,5},{8,10},{9,11},{10,... | collective-permute-start | bytes 2211848 | tf_op jit(solution)/shard_map/ppermute | solution.py:325
  81.7 29.5 %collective-permute-start.16 = (bf16[1440,256]{1,0:T(8,128)(2,1)S(1)}, bf16[1440,256]{1,0:T(8,128)(2,1)S(1)}, u32[]{:S(2)}, u32[]{:S(2)}) collective-permute-start(bf16[1440,256]{1,0:T(8,128)(2,1)S(1)} %collective-permute-done.12.refs_0_), channel_id=1, source_target_pairs={{0,2},{1,3},{2,0},{3,1},{4,6},{5,7},{6,4},{7,5},{8,10},{9,11},{10,... | collective-permute-start | bytes 2211848 | tf_op jit(solution)/shard_map/ppermute | solution.py:325
  82.2 29.0 %collective-permute-start.18 = (bf16[1440,256]{1,0:T(8,128)(2,1)}, bf16[1440,256]{1,0:T(8,128)(2,1)S(1)}, u32[]{:S(2)}, u32[]{:S(2)}) collective-permute-start(bf16[1440,256]{1,0:T(8,128)(2,1)} %collective-permute-done.14.refs_2_), channel_id=1, source_target_pairs={{0,2},{1,3},{2,0},{3,1},{4,6},{5,7},{6,4},{7,5},{8,10},{9,11},{10,... | collective-permute-start | bytes 2211848 | tf_op jit(solution)/shard_map/ppermute | solution.py:325
  92.5 18.7 %collective-permute-start.19 = (bf16[1440,256]{1,0:T(8,128)(2,1)S(1)}, bf16[1440,256]{1,0:T(8,128)(2,1)S(1)}, u32[]{:S(2)}, u32[]{:S(2)}) collective-permute-start(bf16[1440,256]{1,0:T(8,128)(2,1)S(1)} %collective-permute-done.15.refs_3_), channel_id=1, source_target_pairs={{0,2},{1,3},{2,0},{3,1},{4,6},{5,7},{6,4},{7,5},{8,10},{9,11},{10,... | collective-permute-start | bytes 2211848 | tf_op jit(solution)/shard_map/ppermute | solution.py:325
  92.9 16.2 %collective-permute-start.22 = (bf16[360,640]{1,0:T(8,128)(2,1)}, bf16[360,640]{1,0:T(8,128)(2,1)S(1)}, u32[]{:S(2)}, u32[]{:S(2)}) collective-permute-start(bf16[360,640]{1,0:T(8,128)(2,1)} %collective-permute-done.11), channel_id=1, source_target_pairs={{0,8},{2,10},{4,12},{6,14},{8,16},{10,18},{12,20},{14,22},{16,24},... | collective-permute-start | bytes 1382408 | tf_op jit(solution)/shard_map/ppermute | solution.py:329
  109.0 23.2 %collective-permute-start.23 = (bf16[360,512]{1,0:T(8,128)(2,1)S(1)}, bf16[360,512]{1,0:T(8,128)(2,1)S(1)}, u32[]{:S(2)}, u32[]{:S(2)}) collective-permute-start(bf16[360,512]{1,0:T(8,128)(2,1)S(1)} %maximum_select_fusion.10), channel_id=1, source_target_pairs={{0,8},{2,10},{4,12},{6,14},{8,16},{10,18},{12,20},{14,22},{16,24},... | collective-permute-start | bytes 1105928 | tf_op jit(solution)/shard_map/ppermute | solution.py:329
  132.5 14.9 %collective-permute-start.26 = (bf16[720,512]{1,0:T(8,128)(2,1)S(1)}, bf16[720,512]{1,0:T(8,128)(2,1)S(1)}, u32[]{:S(2)}, u32[]{:S(2)}) collective-permute-start(bf16[720,512]{1,0:T(8,128)(2,1)S(1)} %maximum_select_fusion.4.w_near), channel_id=1, source_target_pairs={{0,2},{1,3},{2,0},{3,1},{4,6},{5,7},{6,4},{7,5},{8,10},{9,11},{10,... | collective-permute-start | bytes 2211848 | tf_op jit(solution)/shard_map/ppermute | solution.py:325
  145.5 20.0 %collective-permute-start.31 = (bf16[360,512]{1,0:T(8,128)(2,1)S(1)}, bf16[360,512]{1,0:T(8,128)(2,1)}, u32[]{:S(2)}, u32[]{:S(2)}) collective-permute-start(bf16[360,512]{1,0:T(8,128)(2,1)S(1)} %copy-done.13), channel_id=1, source_target_pairs={{0,8},{2,10},{4,12},{6,14},{8,16},{10,18},{12,20},{14,22},{16,24},... | collective-permute-start | bytes 1105928 | tf_op jit(solution)/shard_map/ppermute | solution.py:329
  149.7 18.8 %collective-permute-start.32 = (bf16[360,256]{1,0:T(8,128)(2,1)S(1)}, bf16[360,256]{1,0:T(8,128)(2,1)S(1)}, u32[]{:S(2)}, u32[]{:S(2)}) collective-permute-start(bf16[360,256]{1,0:T(8,128)(2,1)S(1)} %get-tuple-element.67), channel_id=1, source_target_pairs={{0,4},{1,5},{2,6},{3,7},{4,0},{5,1},{6,2},{7,3},{8,12},{9,13},{10,... | collective-permute-start | bytes 552968 | tf_op jit(solution)/shard_map/ppermute | solution.py:325
  165.5 15.0 %collective-permute-start.41 = (bf16[360,512]{1,0:T(8,128)(2,1)}, bf16[360,512]{1,0:T(8,128)(2,1)}, u32[]{:S(2)}, u32[]{:S(2)}) collective-permute-start(bf16[360,512]{1,0:T(8,128)(2,1)} %collective-permute-done.31), channel_id=1, source_target_pairs={{0,8},{2,10},{4,12},{6,14},{8,16},{10,18},{12,20},{14,22},{16,24},... | collective-permute-start | bytes 1105928 | tf_op jit(solution)/shard_map/ppermute | solution.py:329
  166.9 15.3 %collective-permute-start.36 = (bf16[720,512]{1,0:T(8,128)(2,1)S(1)}, bf16[720,512]{1,0:T(8,128)(2,1)S(1)}, u32[]{:S(2)}, u32[]{:S(2)}) collective-permute-start(bf16[720,512]{1,0:T(8,128)(2,1)S(1)} %maximum_select_fusion.5.w_near), channel_id=1, source_target_pairs={{0,2},{1,3},{2,0},{3,1},{4,6},{5,7},{6,4},{7,5},{8,10},{9,11},{10,... | collective-permute-start | bytes 2211848 | tf_op jit(solution)/shard_map/ppermute | solution.py:325
  169.4 15.6 %collective-permute-start.33 = (bf16[720,256]{1,0:T(8,128)(2,1)}, bf16[720,256]{1,0:T(8,128)(2,1)}, u32[]{:S(2)}, u32[]{:S(2)}) collective-permute-start(bf16[720,256]{1,0:T(8,128)(2,1)} %pad_maximum_fusion), channel_id=1, source_target_pairs={{0,1},{1,0},{2,3},{3,2},{4,5},{5,4},{6,7},{7,6},{8,9},{9,8},{10,11... | collective-permute-start | bytes 1105928 | tf_op jit(solution)/shard_map/ppermute | solution.py:325
  182.1 20.8 %collective-permute-start.42 = (bf16[720,512]{1,0:T(8,128)(2,1)S(1)}, bf16[720,512]{1,0:T(8,128)(2,1)S(1)}, u32[]{:S(2)}, u32[]{:S(2)}) collective-permute-start(bf16[720,512]{1,0:T(8,128)(2,1)S(1)} %maximum_select_fusion.6.w_near), channel_id=1, source_target_pairs={{0,2},{1,3},{2,0},{3,1},{4,6},{5,7},{6,4},{7,5},{8,10},{9,11},{10,... | collective-permute-start | bytes 2211848 | tf_op jit(solution)/shard_map/ppermute | solution.py:325
  182.2 18.0 %collective-permute-start.47 = (bf16[360,512]{1,0:T(8,128)(2,1)}, bf16[360,512]{1,0:T(8,128)(2,1)S(1)}, u32[]{:S(2)}, u32[]{:S(2)}) collective-permute-start(bf16[360,512]{1,0:T(8,128)(2,1)} %collective-permute-done.41), channel_id=1, source_target_pairs={{0,8},{2,10},{4,12},{6,14},{8,16},{10,18},{12,20},{14,22},{16,24},... | collective-permute-start | bytes 1105928 | tf_op jit(solution)/shard_map/ppermute | solution.py:329
  185.0 17.2 %collective-permute-start.37 = (bf16[360,256]{1,0:T(8,128)(2,1)S(1)}, bf16[360,256]{1,0:T(8,128)(2,1)S(1)}, u32[]{:S(2)}, u32[]{:S(2)}) collective-permute-start(bf16[360,256]{1,0:T(8,128)(2,1)S(1)} %get-tuple-element.73), channel_id=1, source_target_pairs={{0,4},{1,5},{2,6},{3,7},{4,0},{5,1},{6,2},{7,3},{8,12},{9,13},{10,... | collective-permute-start | bytes 552968 | tf_op jit(solution)/shard_map/ppermute | solution.py:325
  202.3 30.7 %collective-permute-start.38 = (bf16[720,256]{1,0:T(8,128)(2,1)S(1)}, bf16[720,256]{1,0:T(8,128)(2,1)S(1)}, u32[]{:S(2)}, u32[]{:S(2)}) collective-permute-start(bf16[720,256]{1,0:T(8,128)(2,1)S(1)} %pad_maximum_fusion.2), channel_id=1, source_target_pairs={{0,1},{1,0},{2,3},{3,2},{4,5},{5,4},{6,7},{7,6},{8,9},{9,8},{10,11... | collective-permute-start | bytes 1105928 | tf_op jit(solution)/shard_map/ppermute | solution.py:325
  208.2 25.2 %collective-permute-start.40 = (bf16[720,256]{1,0:T(8,128)(2,1)S(1)}, bf16[720,256]{1,0:T(8,128)(2,1)S(1)}, u32[]{:S(2)}, u32[]{:S(2)}) collective-permute-start(bf16[720,256]{1,0:T(8,128)(2,1)S(1)} %pad_maximum_fusion.3), channel_id=1, source_target_pairs={{0,4},{1,5},{2,6},{3,7},{4,0},{5,1},{6,2},{7,3},{8,12},{9,13},{10,... | collective-permute-start | bytes 1105928 | tf_op jit(solution)/shard_map/ppermute | solution.py:325
  212.8 20.7 %collective-permute-start.44 = (bf16[720,256]{1,0:T(8,128)(2,1)S(1)}, bf16[720,256]{1,0:T(8,128)(2,1)S(1)}, u32[]{:S(2)}, u32[]{:S(2)}) collective-permute-start(bf16[720,256]{1,0:T(8,128)(2,1)S(1)} %pad_maximum_fusion.4), channel_id=1, source_target_pairs={{0,1},{1,0},{2,3},{3,2},{4,5},{5,4},{6,7},{7,6},{8,9},{9,8},{10,11... | collective-permute-start | bytes 1105928 | tf_op jit(solution)/shard_map/ppermute | solution.py:325
  (45 other events, 456.9 us)

commit v3 on v2

v3 whole, which is shorter than its diff:
```python
import functools
import math

import jax
import jax.numpy as jnp
from jax import lax
from jax.experimental import pallas as pl
from jax.experimental.pallas import tpu as pltpu
from jax.sharding import PartitionSpec as P

HEAD_WIDTH = 64
WINDOW_KEYS = 128
SLICES = 4

rope_base = 150000.0
vmem_bytes = 48 * 1024 * 1024
wide_vmem_bytes = 62 * 1024 * 1024
log2e = math.log2(math.e)
small_cost = pl.CostEstimate(flops=1000, bytes_accessed=1000, transcendentals=0)
score_scale = HEAD_WIDTH**-0.5 * log2e


def shift(value, axis, by):
    devices = lax.axis_size(axis)
    pairs = [(i, i + by) for i in range(devices) if 0 <= i + by < devices]
    return lax.ppermute(value, axis, pairs)


def angles_of(places):
    half_dim = HEAD_WIDTH // 2
    frequency = jnp.exp(
        jnp.arange(half_dim, dtype=jnp.float32) * (-2.0 * math.log(rope_base) / HEAD_WIDTH)
    )
    return places.astype(jnp.float32)[None, :] * frequency[:, None]


def columns_dot(one, other):
    return lax.dot_general(one, other, (((0,), (0,)), ((), ())), preferred_element_type=jnp.float32)


def project_kernel(zs, order, *refs, cuts):
    slabs = zs.shape[0]
    pieces, weights = refs[: len(cuts)], refs[len(cuts) : -8]
    cosine, sine, kv_out, q_out, tail_out, held, w_held, sems = refs[-8:]
    pairs, features, lanes = held.shape
    depth, block, half = features // slabs, lanes // 2, HEAD_WIDTH // 2
    loads = []
    row = 0
    for i, w in enumerate(weights):
        rows = pl.ds(pl.multiple_of(zs[row // depth] * depth + row % depth, 16), w.shape[0])
        loads.append((0, pltpu.make_async_copy(w, w_held.at[rows], sems.at[len(cuts) + i])))
        row += w.shape[0]
    for i, (at, start, rows) in enumerate(cuts):
        target = held.at[at // 2, pl.ds(start, rows), pl.ds(at % 2 * block, block)]
        loads.append((at // 2, pltpu.make_async_copy(pieces[i], target, sems.at[i])))
    for _, load in loads:
        load.start()

    def product_of(pair):
        for at, load in loads:
            if at == pair:
                load.wait()
        return columns_dot(w_held[...], held[pair])

    def finish_of(pair, product):
        for side in range(2):
            place = order[2 * pair + side]
            total = product[:, side * block : (side + 1) * block]
            lanes = pl.ds(pl.multiple_of(place * block, block), block)
            cos, sin = cosine[:, lanes], sine[:, lanes]

            def rotated(at):
                lower, upper = total[at : at + half], total[at + half : at + 2 * half]
                return jnp.concatenate([lower * cos - upper * sin, upper * cos + lower * sin], axis=0)

            kv_out[0:HEAD_WIDTH, lanes] = rotated(0).astype(jnp.bfloat16)
            kv_out[HEAD_WIDTH : 2 * HEAD_WIDTH, lanes] = total[HEAD_WIDTH : 2 * HEAD_WIDTH].astype(jnp.bfloat16)
            for h in range(q_out.shape[1] // HEAD_WIDTH):
                q_out[place, h * HEAD_WIDTH : (h + 1) * HEAD_WIDTH] = (
                    rotated((h + 2) * HEAD_WIDTH) * score_scale
                ).astype(jnp.bfloat16)

    ahead = product_of(0)
    for pair in range(pairs):
        product = ahead
        if pair + 1 < pairs:
            ahead = product_of(pair + 1)
        finish_of(pair, product)
    tail_out[...] = kv_out[:, kv_out.shape[1] - WINDOW_KEYS :]


def project(zs, order, pieces, weights, cosine, sine):
    (features, width), block = (sum(w.shape[0] for w in weights), weights[0].shape[1]), pieces[0].shape[1]
    blocks = order.shape[0]
    kv_width = 2 * HEAD_WIDTH
    cuts, at, start = [], 0, 0
    for piece in pieces:
        cuts.append((at, start, piece.shape[0]))
        at, start = (at, start + piece.shape[0]) if start + piece.shape[0] < features else (at + 1, 0)
    vmem = pl.BlockSpec(memory_space=pltpu.VMEM)
    return pl.pallas_call(
        functools.partial(project_kernel, cuts=cuts),
        in_specs=[pl.BlockSpec(memory_space=pltpu.SMEM)] * 2
        + [pl.BlockSpec(memory_space=pl.ANY)] * (len(pieces) + len(weights))
        + [vmem] * 2,
        out_specs=[vmem] * 3,
        out_shape=[
            jax.ShapeDtypeStruct((kv_width, blocks * block), jnp.bfloat16),
            jax.ShapeDtypeStruct((blocks, width - kv_width, block), jnp.bfloat16),
            jax.ShapeDtypeStruct((kv_width, WINDOW_KEYS), jnp.bfloat16),
        ],
        scratch_shapes=[
            pltpu.VMEM((blocks // 2, features, 2 * block), jnp.bfloat16),
            pltpu.VMEM((features, width), jnp.bfloat16),
            pltpu.SemaphoreType.DMA((len(pieces) + len(weights),)),
        ],
        compiler_params=pltpu.CompilerParams(vmem_limit_bytes=wide_vmem_bytes),
        cost_estimate=small_cost,
        name="project",
    )(zs, order, *pieces, *weights, cosine, sine)


def attend_kernel(first, sinks, q, kv, *refs, low):
    *tail, give, keep, keys, values = refs
    window = WINDOW_KEYS
    width, block = q.shape[1:]
    heads = width // HEAD_WIDTH
    parts = block // window
    span = 4 * block
    if tail:
        keys[:window] = jnp.transpose(tail[0][:HEAD_WIDTH])
        values[:, :window] = tail[0][HEAD_WIDTH:]
        keys[window:] = jnp.transpose(kv[:HEAD_WIDTH, low : low + span])
        values[:, window:] = kv[HEAD_WIDTH:, low : low + span]
    else:
        keys[...] = jnp.transpose(kv[:HEAD_WIDTH, low - window : low + span])
        values[...] = kv[HEAD_WIDTH:, low - window : low + span]

    row = lax.broadcasted_iota(jnp.int32, (2 * window, window), 0)
    lane = lax.broadcasted_iota(jnp.int32, (2 * window, window), 1)
    seen = (row > lane) & (row <= lane + window)
    left = lax.broadcasted_iota(jnp.int32, (1, 2 * window), 1) < window
    core = first[1]
    units = [(mine, side, part) for mine in range(2) for side in range(2) for part in range(parts)]

    def at_block(unit):
        mine, side, _ = unit
        return (core if mine else 1 - core) * 2 + side

    def at_token(unit):
        return pl.multiple_of(at_block(unit) * block + unit[2] * window, window)

    def bias_of(unit):
        allowed = seen
        if tail and unit[1:] == (0, 0):
            allowed = seen & (row >= jnp.where(first[0] + at_block(unit) == 0, window, 0))
        bias = jnp.where(allowed, 0.0, -jnp.inf)
        return jnp.concatenate([bias, bias], axis=1)

    def scores_of(unit):
        lanes = slice(unit[2] * window, (unit[2] + 1) * window)
        key_rows = keys[pl.ds(at_token(unit), 2 * window), :]
        out = []
        for h in range(0, heads, 2):
            rows = slice(h * HEAD_WIDTH, (h + 1) * HEAD_WIDTH), slice((h + 1) * HEAD_WIDTH, (h + 2) * HEAD_WIDTH)
            pair = jnp.concatenate([q[at_block(unit), r, lanes] for r in rows], axis=1)
            out.append(jnp.dot(key_rows, pair, preferred_element_type=jnp.float32))
        return out

    def weights_of(unit, scores):
        bias = bias_of(unit)
        out = []
        for i, score in enumerate(scores):
            score = score + bias
            sink = jnp.where(left, sinks[2 * i], sinks[2 * i + 1]) * log2e
            top = jnp.maximum(jnp.max(score, axis=0, keepdims=True), sink)
            exponent = jnp.exp2(score - top)
            denominator = jnp.sum(exponent, axis=0, keepdims=True) + jnp.exp2(sink - top)
            out.append((exponent.astype(jnp.bfloat16), 1.0 / denominator))
        return out

    def mix(unit, weights):
        mine, side, part = unit
        lanes = slice(part * window, (part + 1) * window)
        value_rows = values[:, pl.ds(at_token(unit), 2 * window)]
        out = keep if mine else give
        for i, (weight, scale) in enumerate(weights):
            mixture = jnp.dot(value_rows, weight, preferred_element_type=jnp.float32)
            result = (mixture * scale).astype(jnp.bfloat16)
            for j in range(2):
                rows = slice((2 * i + j) * HEAD_WIDTH, (2 * i + j + 1) * HEAD_WIDTH)
                out[side, rows, lanes] = result[:, j * window : (j + 1) * window]

    ahead = scores_of(units[0])
    behind = None
    for n, unit in enumerate(units):
        scores = ahead
        if n + 1 < len(units):
            ahead = scores_of(units[n + 1])
        weights = weights_of(unit, scores)
        if behind is not None:
            mix(*behind)
        behind = unit, weights
    mix(*behind)


def attend(first, sinks, q, kv, half, tail=()):
    _, width, block = q.shape
    window = WINDOW_KEYS
    return pl.pallas_call(
        functools.partial(attend_kernel, low=half * 4 * block),
        grid_spec=pltpu.PrefetchScalarGridSpec(
            num_scalar_prefetch=2,
            grid=(1,),
            in_specs=[pl.BlockSpec((4, width, block), lambda i, *_: (half, 0, 0))]
            + [pl.BlockSpec(x.shape, lambda i, *_: (0, 0)) for x in (kv, *tail)],
            out_specs=[pl.BlockSpec((2, width, block), lambda i, *_: (0, 0, 0))] * 2,
            scratch_shapes=[
                pltpu.VMEM((4 * block + window, HEAD_WIDTH), jnp.bfloat16),
                pltpu.VMEM((HEAD_WIDTH, 4 * block + window), jnp.bfloat16),
            ],
        ),
        out_shape=[jax.ShapeDtypeStruct((2, width, block), jnp.bfloat16)] * 2,
        compiler_params=pltpu.CompilerParams(vmem_limit_bytes=vmem_bytes),
        cost_estimate=small_cost,
        name="attend",
    )(first, sinks, q, kv, *tail)


def first_part(weights):
    rows = weights[0].shape[0]
    return rows if len(weights) > 1 else rows // 32 * 16 + 16


def sums_kernel(sides, *refs, count, crossing):
    weights, (near0, near1, far0, far1), outs = refs[: 2 * count], refs[2 * count : 2 * count + 4], refs[2 * count + 4 :]
    row, side = sides[0], sides[1]
    middle = outs[0].shape[0]

    def all_of(mine, other):
        start = 0
        for w_near, w_far in zip(weights[:count], weights[count:]):

            def write(halves, place, top, bottom, w_near=w_near, w_far=w_far, start=start):
                near, far = halves
                total = jnp.dot(w_near[...], near[place], preferred_element_type=jnp.float32)
                total += jnp.dot(w_far[...], far[place], preferred_element_type=jnp.float32)
                if count > 1:
                    out = bottom if start else top
                    out[...] = total.astype(out.dtype)
                else:
                    top[...] = total[:middle].astype(top.dtype)
                    bottom[...] = total[middle:].astype(bottom.dtype)

            if crossing:
                write(other, 1 - side, *outs)
            else:
                write(mine, 1 - side, *outs[2:4])
                write(other, side, *outs[4:6])
                write(mine, side, *outs[:2])
            start += w_near.shape[0]

    @pl.when(row == 0)
    def _():
        all_of((near0, far0), (near1, far1))

    @pl.when(row == 1)
    def _():
        all_of((near1, far1), (near0, far0))


def output_sums(sides, w_near, w_far, near, far, crossing):
    depth = sum(w.shape[0] for w in w_near)
    middle = first_part(w_near)
    block = near[0].shape[2]
    vmem = pl.BlockSpec(memory_space=pltpu.VMEM)
    types = [jnp.bfloat16] * 2
    if not crossing:
        types = [jnp.float32, jnp.float32, jnp.bfloat16, jnp.float32, jnp.float32, jnp.bfloat16]
    return pl.pallas_call(
        functools.partial(sums_kernel, count=len(w_near), crossing=crossing),
        in_specs=[pl.BlockSpec(memory_space=pltpu.SMEM)] + [vmem] * (2 * len(w_near) + 4),
        out_specs=[vmem] * len(types),
        out_shape=[
            jax.ShapeDtypeStruct((depth - middle if i % 2 else middle, block), kind) for i, kind in enumerate(types)
        ],
        compiler_params=pltpu.CompilerParams(vmem_limit_bytes=vmem_bytes),
        cost_estimate=small_cost,
        name="crossing_sums" if crossing else "output_sums",
    )(sides, *w_near, *w_far, *near, *far)


def slab_body(tokens, w_query, w_kv, w_out, sinks):
    devices = lax.axis_size("seq")
    slabs = devices // SLICES
    tp = lax.axis_size("tp")
    place = lax.axis_index("seq")
    slab, part = place // SLICES, place % SLICES
    side = lax.axis_index("tp")
    block = tokens.shape[0]
    blocks = SLICES * tp
    both = ("seq", "tp")

    def swap(value, flip_seq, flip_tp):
        pairs = [
            (s * tp + t, (s ^ flip_seq) * tp + (t ^ flip_tp)) for s in range(devices) for t in range(tp)
        ]
        return lax.ppermute(value, both, pairs)

    def turn(value):
        pairs = [(s, (s + SLICES) % devices) for s in range(devices)]
        return lax.ppermute(value, "seq", pairs)

    tie = lambda *values: lax.optimization_barrier(values)

    core, row = part % 2, part // 2
    def of_head(weight, head):
        width = weight.shape[1] // SLICES
        return lax.dynamic_slice_in_dim(weight, head * width, width, 1)

    def by(flag, one, other):
        joined = jnp.concatenate([one, other], axis=0)
        return jnp.where(flag == 1, jnp.concatenate([other, one], axis=0), joined)

    def of_chip(make):
        return by(core, make(part), swap(make(part ^ 1), 1, 0))

    def of_next_chip(make):
        return [swap(make(part ^ 2), 2, 0), swap(make(part ^ 3), 3, 0)]

    def in_head(head):
        return jnp.concatenate([of_head(w_kv, head), of_head(w_query, head)], axis=1)

    def out_head(head):
        return of_head(w_out, head)

    order = jnp.stack(
        [
            (row ^ r) * 2 * tp + (core ^ c) * tp + (side ^ t)
            for r in range(2)
            for c in range(2)
            for t in range(tp)
        ]
    ).astype(jnp.int32)

    own = tokens.T
    features = own.shape[0]
    third = features // 3
    near, far = of_chip(in_head), of_next_chip(in_head)
    near, own_late = tie(near, own)
    a, b, c = (own_late[i * third : (i + 1) * third] for i in range(3))
    next_near = turn(near)
    *far, x_a = tie(*far, swap(a, 0, 1))
    far = by(core, *far)
    weights_in = [by(row, near, far)]
    near, far, x_a, a, b, c = tie(next_near, far, x_a, a, b, c)
    far, x_b, y_b, near, x_a, a, c = tie(turn(far), swap(b, 0, 1), swap(b, 2, 0), near, x_a, a, c)
    weights_in.append(by(row, near, far))
    weight = turn(weights_in[1])
    first = slab * (blocks * block)
    places = first + jnp.arange(blocks * block, dtype=jnp.int32)
    angles = angles_of(places)
    cosine, sine = jnp.cos(angles), jnp.sin(angles)
    slabs_held = jnp.stack([(slab - k) % slabs for k in range(slabs)]).astype(jnp.int32)
    sides = jnp.stack([row, side])
    first_row = jnp.stack([first, core])
    heads = sinks.shape[0] // SLICES
    head_sinks = lax.dynamic_slice_in_dim(sinks, part * heads, heads, 0)
    small = [cosine, sine, slabs_held, order, sides, first_row, head_sinks]
    x_c, y_c, x_a, y_b, a, weights_in[0], *small = tie(
        swap(c, 0, 1), swap(c, 2, 0), x_a, y_b, a, weights_in[0], *small
    )
    cosine, sine, slabs_held, order, sides, first_row, head_sinks = small
    weight, y_a, d_b, x_a, y_c = tie(weight, swap(a, 2, 0), swap(y_b, 0, 1), x_a, y_c)
    cut = weight.shape[0] // 32 * 16 + 16
    weights_in += [weight, turn(weight[:cut]), weight[cut:]]
    d_a, d_c, w_out, *weights_in[-2:] = tie(swap(x_a, 2, 0), swap(y_c, 0, 1), w_out, *weights_in[-2:])
    weights_in[-1] = turn(weights_in[-1])

    def of_cores(*pieces):
        return [*pieces, *(swap(piece, 1, 0) for piece in pieces)]

    pieces = of_cores(own, x_a, x_b, x_c) + of_cores(y_a, y_b, y_c, d_a, d_b, d_c)
    near_out = of_chip(out_head)
    far_out = of_next_chip(out_head)
    *pieces, far_out[0], far_out[1] = tie(*pieces, *far_out)
    own_out = by(row, near_out, by(core, *far_out))
    own_out_late, weights_in[-1] = tie(own_out, weights_in[-1])
    weights_out = [own_out, turn(own_out_late)]
    kv, q, kv_tail = project(slabs_held, order, pieces, weights_in, cosine, sine)
    kv_tail = shift(kv_tail, "seq", SLICES)
    mixed = [None, list(attend(first_row, head_sinks, q, kv, 1))]
    mixed[1][1], kv_tail, weights_out[1] = tie(mixed[1][1], kv_tail, weights_out[1])
    mixed[0] = attend(first_row, head_sinks, q, kv, 0, (kv_tail,))
    came = [swap(give, 1, 0) for give, _ in mixed]
    kept = [keep for _, keep in mixed]

    depth = weights_out[0].shape[0]
    result = jnp.zeros((features, block), jnp.bfloat16)
    weights_out.append(turn(weights_out[1]))
    chunks = ((0, 1), (2,), (3,))
    sums, plain, merged = [], [], []
    for n, chunk in enumerate(chunks):
        w_near = [weights_out[k] for k in chunk]
        w_far = [swap(w, 1, 0) for w in w_near]
        crosses = output_sums(sides, w_near, w_far, kept, came, True)
        by_x, by_y = swap(crosses[0], 0, 1), swap(crosses[1], 2, 0)
        *own_sums, x_top, x_bottom, y_top, y_bottom = output_sums(sides, w_near, w_far, kept, came, False)
        if n == 0:
            own_sums[0], weights_out[2] = tie(own_sums[0], weights_out[2])
            weights_out.append(turn(weights_out[2]))
        plain.append([swap(x_top, 0, 1), swap(y_bottom, 2, 0)])
        if n:
            by_x, by_y, *merged[n - 1] = tie(by_x, by_y, *merged[n - 1])
        else:
            by_x, by_y = tie(by_x, by_y)
        y_top = (y_top + by_x.astype(jnp.float32)).astype(jnp.bfloat16)
        x_bottom = (x_bottom + by_y.astype(jnp.float32)).astype(jnp.bfloat16)
        if n + 1 < len(chunks):
            kept[0], *plain[n] = tie(kept[0], *plain[n])
        merged.append([swap(x_bottom, 0, 1), swap(y_top, 2, 0)])
        sums.append(own_sums)
    for n, chunk in enumerate(chunks):
        top = sums[n][0] + plain[n][0].astype(jnp.float32) + merged[n][1].astype(jnp.float32)
        bottom = sums[n][1] + merged[n][0].astype(jnp.float32) + plain[n][1].astype(jnp.float32)
        place = (slab - chunk[0]) % slabs * depth
        result = lax.dynamic_update_slice_in_dim(result, top.astype(jnp.bfloat16), place, 0)
        place = (slab - chunk[1]) % slabs * depth if len(chunk) > 1 else place + top.shape[0]
        result = lax.dynamic_update_slice_in_dim(result, bottom.astype(jnp.bfloat16), place, 0)
    return result.T


def rotary(vectors, places):
    half_dim = vectors.shape[-1] // 2
    angles = angles_of(places).T[:, None, :]
    cosine = jnp.cos(angles)
    sine = jnp.sin(angles)
    lower_half = vectors[..., :half_dim]
    upper_half = vectors[..., half_dim:]
    return jnp.concatenate(
        [lower_half * cosine - upper_half * sine, upper_half * cosine + lower_half * sine], axis=-1
    )


def attend_rows(query_rows, key_value_rows, sink_scores, query_pos, key_pos):
    key_part = key_value_rows[:, :, 0, :]
    value_part = key_value_rows[:, :, 1, :]
    scores = jnp.einsum(
        "qhgd,khd->hgqk", query_rows, key_part, preferred_element_type=jnp.float32
    ) * HEAD_WIDTH ** (-0.5)
    allowed = (
        (key_pos[None, :] <= query_pos[:, None])
        & (key_pos[None, :] > query_pos[:, None] - WINDOW_KEYS)
        & (key_pos[None, :] >= 0)
    )
    scores = jnp.where(allowed[None, None], scores, -jnp.inf)
    row_max = jnp.maximum(jnp.max(scores, axis=-1), sink_scores[:, :, None])
    exponent = jnp.exp(scores - row_max[..., None])
    denominator = jnp.sum(exponent, axis=-1) + jnp.exp(sink_scores[:, :, None] - row_max)
    weights = exponent.astype(jnp.bfloat16)
    mixture = jnp.einsum("hgqk,khd->qhgd", weights, value_part, preferred_element_type=jnp.float32)
    return (mixture / jnp.transpose(denominator, (2, 0, 1))[..., None]).astype(jnp.bfloat16)


def finish(kv_sum, places, kv_heads):
    split_key_value = kv_sum.reshape(kv_sum.shape[0], kv_heads, 2, HEAD_WIDTH)
    key_part = rotary(split_key_value[:, :, 0, :], places)
    return jnp.stack([key_part, split_key_value[:, :, 1, :]], axis=2).astype(jnp.bfloat16)


def row_body(tokens, w_query, w_kv, w_out, sinks):
    token_rows = lax.all_gather(tokens, "tp", axis=0, tiled=True)
    row_count = token_rows.shape[0]
    kv_width = w_kv.shape[1]
    kv_heads = kv_width // (2 * HEAD_WIDTH)
    q_width = w_query.shape[1]
    head_groups = q_width // HEAD_WIDTH // kv_heads
    start_pos = lax.axis_index("seq") * row_count
    query_pos = start_pos + jnp.arange(row_count, dtype=jnp.int32)
    key_pos = start_pos - WINDOW_KEYS + jnp.arange(row_count + WINDOW_KEYS, dtype=jnp.int32)
    query_sum = jnp.dot(
        token_rows,
        lax.all_gather(w_query, "seq", axis=0, tiled=True),
        preferred_element_type=jnp.float32,
    )
    kv_sum = jnp.dot(
        token_rows,
        lax.all_gather(w_kv, "seq", axis=0, tiled=True),
        preferred_element_type=jnp.float32,
    )
    query_rows = rotary(
        query_sum.reshape(row_count, kv_heads * head_groups, HEAD_WIDTH), query_pos
    ).astype(jnp.bfloat16)
    query_rows = query_rows.reshape(row_count, kv_heads, head_groups, HEAD_WIDTH)
    local_kv = finish(kv_sum, query_pos, kv_heads).reshape(row_count, kv_width)
    kv_tail = shift(local_kv[row_count - WINDOW_KEYS :], "seq", 1)
    key_value_rows = jnp.concatenate([kv_tail, local_kv], axis=0).reshape(
        row_count + WINDOW_KEYS, kv_heads, 2, HEAD_WIDTH
    )
    attended = attend_rows(
        query_rows, key_value_rows, sinks.reshape(kv_heads, head_groups), query_pos, key_pos
    ).reshape(row_count, q_width)
    out_terms = lax.dot_general(
        attended,
        lax.all_gather(w_out, "seq", axis=0, tiled=True),
        (((1,), (1,)), ((), ())),
        preferred_element_type=jnp.float32,
    )
    return lax.psum_scatter(out_terms.astype(jnp.bfloat16), "tp", scatter_dimension=0, tiled=True)


def solution(mesh):
    in_specs = (P(("seq", "tp"), None), P("seq", "tp"), P("seq", "tp"), P("seq", "tp"), P("tp"))
    out_specs = P(("seq", "tp"), None)

    def body(tokens, w_query, w_kv, w_out, sinks):
        by_slabs = (
            w_kv.shape[1] == SLICES * 2 * HEAD_WIDTH
            and mesh.shape["tp"] == 2
            and mesh.shape["seq"] == 4 * SLICES
            and tokens.shape[0] % (2 * WINDOW_KEYS) == 0
            and (w_query.shape[0] * SLICES) % 16 == 0
        )
        return (slab_body if by_slabs else row_body)(tokens, w_query, w_kv, w_out, sinks)

    return jax.shard_map(body, mesh=mesh, in_specs=in_specs, out_specs=out_specs, check_vma=False)
```

time: 244 us -> 194 us (0.80)
  waiting for transfers between devices: 119 us -> 85.4 us
  Pallas kernels: 46.4 us -> 35.9 us
  starting transfers between devices: 47.6 us -> 42.5 us
  between operations: 3.32 us -> 0.7 us
    ppermute x41 -> x49, waiting for transfers between devices: 75.8 us -> 41 us  [swap(): return lax.ppermute(value, both, pairs)]
    pallas_call x7, Pallas kernels: 39.3 us -> 28.9 us  [the longest x1 14.8 us: project(): pl.pallas_call(functools.partial(project_kernel, cuts=cuts), in_specs=[pl...]
    ppermute x12 -> x8, starting transfers between devices: 13.4 us -> 4.74 us  [turn(): return lax.ppermute(value, 'seq', pairs)]
    select_n x12 -> x7, other arithmetic: 10.4 us -> 4.96 us  [by(): return jnp.where(flag == 1, jnp.concatenate([other, one], axis=0), joined)]
    unnamed x46 -> x102, local copies, waits for them, and re-layouts: 4.89 us -> 10 us
    ppermute x41 -> x49, starting transfers between devices: 31.2 us -> 35.6 us  [swap(): return lax.ppermute(value, both, pairs)]
    slice x12 -> x3, local copies, waits for them, and re-layouts: 4.82 us -> 1.15 us  [the longest x1 1.07 us: slab_body(): a, b, c = (own_late[i * third:(i + 1) * third] for i in range(3))]
    convert_element_type x8 -> x6, other arithmetic: 0.42 us -> 4.02 us  [the longest x3 2.08 us: slab_body(): y_top = (y_top + by_x.astype(jnp.float32)).astype(jnp.bfloat16)]
  transfers between devices with their start and end apart: 54 -> 58, of which waited for: 21 -> 25; matrix products, arithmetic and copies ran while one was open for 8% -> 8% of each run, Pallas kernels for 19% -> 19%
where the time goes in v3:
time: 194 us; the launch traced here: 193 us
  waiting for transfers between devices  85.4 us (44%)
  starting transfers between devices  42.5 us (22%)
  Pallas kernels  35.9 us (19%)
  other arithmetic  15 us (8%)
  local copies, waits for them, and re-layouts  13.5 us (7%)
    ppermute x8, waiting for transfers between devices, turn(): return lax.ppermute(value, 'seq', pairs)  44.3 us
    ppermute x49, waiting for transfers between devices, swap(): return lax.ppermute(value, both, pairs)  41 us
    ppermute x49, starting transfers between devices, swap(): return lax.ppermute(value, both, pairs)  35.6 us
    pallas_call x1, Pallas kernels, project(): pl.pallas_call(functools.partial(project_kernel, cuts=cuts), in_specs=[pl...  14.8 us
    pallas_call x6, Pallas kernels, output_sums(): pl.pallas_call(functools.partial(sums_kernel, count=len(w_near), crossing...  14.1 us
    unnamed x102, local copies, waits for them, and re-layouts  10 us
    pallas_call x2, Pallas kernels, attend(): pl.pallas_call(functools.partial(attend_kernel, low=half * 4 * block), gr...  7.02 us
    select_n x7, other arithmetic, by(): return jnp.where(flag == 1, jnp.concatenate([other, one], axis=0), joined)  4.96 us
  transfers between devices with their start and end apart: 58, of which 25 were waited for; matrix products, arithmetic and copies ran while one was open for 8% of the time, Pallas kernels for 19%

profile of v3, /device:TPU:0, one launch (start us, length us, event | category | flops | bytes accessed | tf_op | source)
XLA Modules:
  0.0 193.0 jit_solution(4184824000618108718)
XLA Ops:
  4.4 2.9 %collective-permute-start.4 = (bf16[960,256]{1,0:T(8,128)(2,1)S(1)}, bf16[960,256]{1,0:T(8,128)(2,1)}, u32[]{:S(2)}, u32[]{:S(2)}) collective-permute-start(bf16[960,256]{1,0:T(8,128)(2,1)S(1)} %get-tuple-element.140), channel_id=1, source_target_pairs={{0,1},{1,0},{2,3},{3,2},{4,5},{5,4},{6,7},{7,6},{8,9},{9,8},{10,11... | collective-permute-start | bytes 1474568 | tf_op jit(solution)/shard_map/ppermute | solution.py:308
  11.2 4.8 %collective-permute-done.2 = bf16[180,640]{1,0:T(8,128)(2,1)S(1)} collective-permute-done((bf16[180,640]{1,0:T(8,128)(2,1)S(1)}, bf16[180,640]{1,0:T(8,128)(2,1)S(1)}, u32[]{:S(2)}, u32[]{:S(2)}) %collective-permute-start.2) | collective-permute-done | bytes 230432 | tf_op jit(solution)/shard_map/ppermute | solution.py:308
  16.0 3.0 %collective-permute-done.3 = bf16[180,640]{1,0:T(8,128)(2,1)S(1)} collective-permute-done((bf16[180,640]{1,0:T(8,128)(2,1)S(1)}, bf16[180,640]{1,0:T(8,128)(2,1)S(1)}, u32[]{:S(2)}, u32[]{:S(2)}) %collective-permute-start.3) | collective-permute-done | bytes 230432 | tf_op jit(solution)/shard_map/ppermute | solution.py:308
  19.1 3.7 %collective-permute-done.1 = bf16[360,640]{1,0:T(8,128)(2,1)S(1)} collective-permute-done((bf16[360,640]{1,0:T(8,128)(2,1)S(1)}, bf16[360,640]{1,0:T(8,128)(2,1)S(1)}, u32[]{:S(2)}, u32[]{:S(2)}) %collective-permute-start.1) | collective-permute-done | bytes 460832 | tf_op jit(solution)/shard_map/ppermute | solution.py:312
  25.5 11.2 %collective-permute-done.5 = bf16[360,640]{1,0:T(8,128)(2,1)} collective-permute-done((bf16[360,640]{1,0:T(8,128)(2,1)S(1)}, bf16[360,640]{1,0:T(8,128)(2,1)}, u32[]{:S(2)}, u32[]{:S(2)}) %collective-permute-start.5) | collective-permute-done | bytes 460832 | tf_op jit(solution)/shard_map/ppermute | solution.py:312
  39.5 1.7 maximum_select_fusion.1.refs_21_
  41.3 1.8 multiply_sine_fusion
  43.1 2.4 %maximum_select_fusion.refs_20_ = bf16[720,640]{1,0:T(8,128)(2,1)} fusion(bf16[360,640]{1,0:T(8,128)(2,1)} %copy-done.16, bf16[360,640]{1,0:T(8,128)(2,1)S(1)} %copy-done.18, pred[]{:T(512)S(6)} %eq.23), kind=kLoop, calls=%fused_computation | loop fusion | flops 4147200 | bytes 1843201 | tf_op jit(solution)/shard_map/jit(_where)/select_n | solution.py:323
  45.5 2.1 %collective-permute-done.8.refs_3_ = bf16[960,256]{1,0:T(8,128)(2,1)S(1)} collective-permute-done((bf16[960,256]{1,0:T(8,128)(2,1)}, bf16[960,256]{1,0:T(8,128)(2,1)S(1)}, u32[]{:S(2)}, u32[]{:S(2)}) %collective-permute-start.8) | collective-permute-done | bytes 491552 | tf_op jit(solution)/shard_map/ppermute | solution.py:308
  47.6 1.9 collective-permute-done.9.refs_10_
  51.8 10.3 %collective-permute-done.10.refs_22_ = bf16[720,640]{1,0:T(8,128)(2,1)S(1)} collective-permute-done((bf16[720,640]{1,0:T(8,128)(2,1)S(1)}, bf16[720,640]{1,0:T(8,128)(2,1)S(1)}, u32[]{:S(2)}, u32[]{:S(2)}) %collective-permute-start.10) | collective-permute-done | bytes 921632 | tf_op jit(solution)/shard_map/ppermute | solution.py:312
  64.5 12.7 %collective-permute-done.19.refs_23_ = bf16[368,640]{1,0:T(8,128)(2,1)S(1)} collective-permute-done((bf16[368,640]{1,0:T(8,128)(2,1)S(1)}, bf16[368,640]{1,0:T(8,128)(2,1)S(1)}, u32[]{:S(2)}, u32[]{:S(2)}) %collective-permute-start.19) | collective-permute-done | bytes 471072 | tf_op jit(solution)/shard_map/ppermute | solution.py:312
  82.8 5.4 %collective-permute-done.26 = bf16[180,512]{1,0:T(8,128)(2,1)S(1)} collective-permute-done((bf16[180,512]{1,0:T(8,128)(2,1)S(1)}, bf16[180,512]{1,0:T(8,128)(2,1)S(1)}, u32[]{:S(2)}, u32[]{:S(2)}) %collective-permute-start.26) | collective-permute-done | bytes 184352 | tf_op jit(solution)/shard_map/ppermute | solution.py:308
  88.1 2.6 %collective-permute-done.27 = bf16[180,512]{1,0:T(8,128)(2,1)S(1)} collective-permute-done((bf16[180,512]{1,0:T(8,128)(2,1)S(1)}, bf16[180,512]{1,0:T(8,128)(2,1)S(1)}, u32[]{:S(2)}, u32[]{:S(2)}) %collective-permute-start.27) | collective-permute-done | bytes 184352 | tf_op jit(solution)/shard_map/ppermute | solution.py:308
  92.7 2.0 %collective-permute-done.29.refs_24_ = bf16[352,640]{1,0:T(8,128)(2,1)S(1)} collective-permute-done((bf16[352,640]{1,0:T(8,128)(2,1)S(1)}, bf16[352,640]{1,0:T(8,128)(2,1)S(1)}, u32[]{:S(2)}, u32[]{:S(2)}) %collective-permute-start.29) | collective-permute-done | bytes 450592 | tf_op jit(solution)/shard_map/ppermute | solution.py:312
  95.5 14.8 %project.1 = (bf16[128,2048]{1,0:T(8,128)(2,1)}, bf16[8,512,256]{2,1,0:T(8,128)(2,1)}, bf16[128,128]{1,0:T(8,128)(2,1)}) custom-call(s32[4]{0:T(128)} %pad_add_fusion.zs, s32[8]{0:T(128)} %stack.73.order, bf16[2880,256]{1,0:T(8,128)(2,1)} %bitcast.18, bf16[960,256]{1,0:T(8,128)(2,1)} %collective-permute-done.4.refs_1_, bf16[960,256]{1,0:T(8,128)(2,1)} %copy-done.21, ...), custom_call_target="tpu_custom_call" | custom-call | flops 1000 | bytes 1000 | tf_op jit(solution)/shard_map/project/pallas_call | solution.py:101
  110.4 2.2 %collective-permute-start.30 = (bf16[128,128]{1,0:T(8,128)(2,1)}, bf16[128,128]{1,0:T(8,128)(2,1)S(1)}, u32[]{:S(2)}, u32[]{:S(2)}) collective-permute-start(bf16[128,128]{1,0:T(8,128)(2,1)} %get-tuple-element.189), channel_id=1, source_target_pairs={{0,8},{2,10},{4,12},{6,14},{8,16},{10,18},{12,20},{14,22},{16,24},... | collective-permute-start | bytes 98312 | tf_op jit(solution)/shard_map/ppermute | solution.py:26
  115.4 3.5 %attend.2 = (bf16[2,512,256]{2,1,0:T(8,128)(2,1)S(1)}, bf16[2,512,256]{2,1,0:T(8,128)(2,1)S(1)}) custom-call(s32[2]{0:T(128)S(1)} %pad_add_fusion.2.first, f32[8]{0:T(128)S(1)} %dynamic_slice.47.sinks, bf16[8,512,256]{2,1,0:T(8,128)(2,1)S(1)} %copy-done, bf16[128,2048]{1,0:T(8,128)(2,1)S(1)} %copy-done.4), custom_call_target="tpu_custom_call" | custom-call | flops 1000 | bytes 1000 | tf_op jit(solution)/shard_map/attend/pallas_call | solution.py:210
  119.4 2.3 %collective-permute-start.36 = (bf16[720,512]{1,0:T(8,128)(2,1)}, bf16[720,512]{1,0:T(8,128)(2,1)S(1)}, u32[]{:S(2)}, u32[]{:S(2)}) collective-permute-start(bf16[720,512]{1,0:T(8,128)(2,1)} %collective-permute-done.31.refs_1_), channel_id=1, source_target_pairs={{0,8},{2,10},{4,12},{6,14},{8,16},{10,18},{12,20},{14,22},{16,24},... | collective-permute-start | bytes 2211848 | tf_op jit(solution)/shard_map/ppermute | solution.py:312
  121.7 3.5 %attend.3 = (bf16[2,512,256]{2,1,0:T(8,128)(2,1)S(1)}, bf16[2,512,256]{2,1,0:T(8,128)(2,1)S(1)}) custom-call(s32[2]{0:T(128)S(1)} %pad_add_fusion.2.first, f32[8]{0:T(128)S(1)} %dynamic_slice.47.sinks, bf16[8,512,256]{2,1,0:T(8,128)(2,1)S(1)} %copy-done, bf16[128,2048]{1,0:T(8,128)(2,1)S(1)} %copy-done.4, bf16[128,128]{1,0:T(8,128)(2,1)S(1)} %collective-permute-done.30.refs_0_), custom_call_target="tpu_custom_call" | custom-call | flops 1000 | bytes 1000 | tf_op jit(solution)/shard_map/attend/pallas_call | solution.py:210
  127.3 2.3 %crossing_sums.4 = (bf16[720,256]{1,0:T(8,128)(2,1)S(1)}, bf16[720,256]{1,0:T(8,128)(2,1)S(1)}) custom-call(s32[2]{0:T(128)S(1)} %pad_add_fusion.1.sides, bf16[720,512]{1,0:T(8,128)(2,1)S(1)} %maximum_select_fusion.2.refs_0_, bf16[720,512]{1,0:T(8,128)(2,1)} %collective-permute-done.31.refs_1_, bf16[720,512]{1,0:T(8,128)(2,1)S(1)} %collective-permute-done.32.refs_2_, ...), custom_call_target="tpu_custom_call" | custom-call | flops 1000 | bytes 1000 | tf_op jit(solution)/shard_map/crossing_sums/pallas_call | solution.py:280
  131.5 4.2 %output_sums.3 = (f32[720,256]{1,0:T(8,128)S(1)}, f32[720,256]{1,0:T(8,128)S(1)}, bf16[720,256]{1,0:T(8,128)(2,1)S(1)}, f32[720,256]{1,0:T(8,128)S(1)}, f32[720,...) custom-call(s32[2]{0:T(128)S(1)} %pad_add_fusion.1.sides, bf16[720,512]{1,0:T(8,128)(2,1)} %copy-done.1, ...), custom_call_target="tpu_custom_call" | custom-call | flops 1000 | bytes 1000 | tf_op jit(solution)/shard_map/output_sums/pallas_call | solution.py:280
  136.6 3.4 %collective-permute-done.36.refs_0_ = bf16[720,512]{1,0:T(8,128)(2,1)S(1)} collective-permute-done((bf16[720,512]{1,0:T(8,128)(2,1)}, bf16[720,512]{1,0:T(8,128)(2,1)S(1)}, u32[]{:S(2)}, u32[]{:S(2)}) %collective-permute-start.36) | collective-permute-done | bytes 737312 | tf_op jit(solution)/shard_map/ppermute | solution.py:312
  145.3 6.0 %collective-permute-done.37 = bf16[720,256]{1,0:T(8,128)(2,1)S(1)} collective-permute-done((bf16[720,256]{1,0:T(8,128)(2,1)S(1)}, bf16[720,256]{1,0:T(8,128)(2,1)S(1)}, u32[]{:S(2)}, u32[]{:S(2)}) %collective-permute-start.37) | collective-permute-done | bytes 368672 | tf_op jit(solution)/shard_map/ppermute | solution.py:308
  153.1 2.5 %output_sums.4 = (f32[368,256]{1,0:T(8,128)S(1)}, f32[352,256]{1,0:T(8,128)S(1)}, bf16[368,256]{1,0:T(8,128)(2,1)}, f32[352,256]{1,0:T(8,128)S(1)}, f32[368,256]...) custom-call(s32[2]{0:T(128)S(1)} %pad_add_fusion.1.sides, bf16[720,512]{1,0:T(8,128)(2,1)S(1)} %collective-permute-done.36.refs_0_, ...), custom_call_target="tpu_custom_call" | custom-call | flops 1000 | bytes 1000 | tf_op jit(solution)/shard_map/output_sums/pallas_call | solution.py:280
  158.0 1.8 crossing_sums.3
  161.9 1.9 collective-permute-done.47
  165.2 2.0 %collective-permute-done.46 = bf16[368,256]{1,0:T(8,128)(2,1)} collective-permute-done((bf16[368,256]{1,0:T(8,128)(2,1)}, bf16[368,256]{1,0:T(8,128)(2,1)}, u32[]{:S(2)}, u32[]{:S(2)}) %collective-permute-start.46) | collective-permute-done | bytes 188448 | tf_op jit(solution)/shard_map/ppermute | solution.py:308
  167.2 3.2 %collective-permute-done.41 = bf16[352,256]{1,0:T(8,128)(2,1)} collective-permute-done((bf16[352,256]{1,0:T(8,128)(2,1)}, bf16[352,256]{1,0:T(8,128)(2,1)}, u32[]{:S(2)}, u32[]{:S(2)}) %collective-permute-start.41) | collective-permute-done | bytes 180256 | tf_op jit(solution)/shard_map/ppermute | solution.py:308
  180.7 1.9 output_sums.5
  185.6 1.8 collective-permute-start.55
  189.1 2.6 %collective-permute-done.55 = bf16[368,256]{1,0:T(8,128)(2,1)S(1)} collective-permute-done((bf16[368,256]{1,0:T(8,128)(2,1)S(1)}, bf16[368,256]{1,0:T(8,128)(2,1)S(1)}, u32[]{:S(2)}, u32[]{:S(2)}) %collective-permute-start.55) | collective-permute-done | bytes 188448 | tf_op jit(solution)/shard_map/ppermute | solution.py:308
  (232 shorter events, 63.8 us)
Async XLA Ops:
  4.4 14.5 %collective-permute-start.4 = (bf16[960,256]{1,0:T(8,128)(2,1)S(1)}, bf16[960,256]{1,0:T(8,128)(2,1)}, u32[]{:S(2)}, u32[]{:S(2)}) collective-permute-start(bf16[960,256]{1,0:T(8,128)(2,1)S(1)} %get-tuple-element.140), channel_id=1, source_target_pairs={{0,1},{1,0},{2,3},{3,2},{4,5},{5,4},{6,7},{7,6},{8,9},{9,8},{10,11... | collective-permute-start | bytes 1474568 | tf_op jit(solution)/shard_map/ppermute | solution.py:308
  8.9 13.9 %collective-permute-start.1 = (bf16[360,640]{1,0:T(8,128)(2,1)S(1)}, bf16[360,640]{1,0:T(8,128)(2,1)S(1)}, u32[]{:S(2)}, u32[]{:S(2)}) collective-permute-start(bf16[360,640]{1,0:T(8,128)(2,1)S(1)} %maximum_select_fusion.3), channel_id=1, source_target_pairs={{0,8},{2,10},{4,12},{6,14},{8,16},{10,18},{12,20},{14,22},{16,24},... | collective-permute-start | bytes 1382408 | tf_op jit(solution)/shard_map/ppermute | solution.py:312
  10.6 52.4 %collective-permute-start.13 = (bf16[2880,256]{1,0:T(8,128)(2,1)S(1)}, bf16[2880,256]{1,0:T(8,128)(2,1)}, u32[]{:S(2)}, u32[]{:S(2)}) collective-permute-start(bf16[2880,256]{1,0:T(8,128)(2,1)S(1)} %bitcast.20), channel_id=1, source_target_pairs={{0,2},{1,3},{2,0},{3,1},{4,6},{5,7},{6,4},{7,5},{8,10},{9,11},{10,... | collective-permute-start | bytes 4423688 | tf_op jit(solution)/shard_map/ppermute | solution.py:308
  22.8 13.9 %collective-permute-start.6 = (bf16[960,256]{1,0:T(8,128)(2,1)}, bf16[960,256]{1,0:T(8,128)(2,1)S(1)}, u32[]{:S(2)}, u32[]{:S(2)}) collective-permute-start(bf16[960,256]{1,0:T(8,128)(2,1)} %get-tuple-element.128), channel_id=1, source_target_pairs={{0,1},{1,0},{2,3},{3,2},{4,5},{5,4},{6,7},{7,6},{8,9},{9,8},{10,11... | collective-permute-start | bytes 1474568 | tf_op jit(solution)/shard_map/ppermute | solution.py:308
  23.3 13.4 %collective-permute-start.7 = (bf16[960,256]{1,0:T(8,128)(2,1)}, bf16[960,256]{1,0:T(8,128)(2,1)}, u32[]{:S(2)}, u32[]{:S(2)}) collective-permute-start(bf16[960,256]{1,0:T(8,128)(2,1)} %get-tuple-element.128), channel_id=1, source_target_pairs={{0,4},{1,5},{2,6},{3,7},{4,0},{5,1},{6,2},{7,3},{8,12},{9,13},{10,... | collective-permute-start | bytes 1474568 | tf_op jit(solution)/shard_map/ppermute | solution.py:308
  23.8 12.8 %collective-permute-start.5 = (bf16[360,640]{1,0:T(8,128)(2,1)S(1)}, bf16[360,640]{1,0:T(8,128)(2,1)}, u32[]{:S(2)}, u32[]{:S(2)}) collective-permute-start(bf16[360,640]{1,0:T(8,128)(2,1)S(1)} %maximum_select_fusion.4), channel_id=1, source_target_pairs={{0,8},{2,10},{4,12},{6,14},{8,16},{10,18},{12,20},{14,22},{16,24},... | collective-permute-start | bytes 1382408 | tf_op jit(solution)/shard_map/ppermute | solution.py:312
  36.7 10.9 %collective-permute-start.8 = (bf16[960,256]{1,0:T(8,128)(2,1)}, bf16[960,256]{1,0:T(8,128)(2,1)S(1)}, u32[]{:S(2)}, u32[]{:S(2)}) collective-permute-start(bf16[960,256]{1,0:T(8,128)(2,1)} %get-tuple-element.133), channel_id=1, source_target_pairs={{0,1},{1,0},{2,3},{3,2},{4,5},{5,4},{6,7},{7,6},{8,9},{9,8},{10,11... | collective-permute-start | bytes 1474568 | tf_op jit(solution)/shard_map/ppermute | solution.py:308
  37.9 11.6 %collective-permute-start.9 = (bf16[960,256]{1,0:T(8,128)(2,1)}, bf16[960,256]{1,0:T(8,128)(2,1)S(1)}, u32[]{:S(2)}, u32[]{:S(2)}) collective-permute-start(bf16[960,256]{1,0:T(8,128)(2,1)} %get-tuple-element.133), channel_id=1, source_target_pairs={{0,4},{1,5},{2,6},{3,7},{4,0},{5,1},{6,2},{7,3},{8,12},{9,13},{10,... | collective-permute-start | bytes 1474568 | tf_op jit(solution)/shard_map/ppermute | solution.py:308
  41.2 20.9 %collective-permute-start.10 = (bf16[720,640]{1,0:T(8,128)(2,1)S(1)}, bf16[720,640]{1,0:T(8,128)(2,1)S(1)}, u32[]{:S(2)}, u32[]{:S(2)}) collective-permute-start(bf16[720,640]{1,0:T(8,128)(2,1)S(1)} %maximum_select_fusion.1.refs_21_), channel_id=1, source_target_pairs={{0,8},{2,10},{4,12},{6,14},{8,16},{10,18},{12,20},{14,22},{16,24},... | collective-permute-start | bytes 2764808 | tf_op jit(solution)/shard_map/ppermute | solution.py:312
  49.5 12.6 %collective-permute-start.11 = (bf16[960,256]{1,0:T(8,128)(2,1)S(1)}, bf16[960,256]{1,0:T(8,128)(2,1)S(1)}, u32[]{:S(2)}, u32[]{:S(2)}) collective-permute-start(bf16[960,256]{1,0:T(8,128)(2,1)S(1)} %copy-done.24), channel_id=1, source_target_pairs={{0,4},{1,5},{2,6},{3,7},{4,0},{5,1},{6,2},{7,3},{8,12},{9,13},{10,... | collective-permute-start | bytes 1474568 | tf_op jit(solution)/shard_map/ppermute | solution.py:308
  51.1 11.1 %collective-permute-start.12 = (bf16[960,256]{1,0:T(8,128)(2,1)}, bf16[960,256]{1,0:T(8,128)(2,1)S(1)}, u32[]{:S(2)}, u32[]{:S(2)}) collective-permute-start(bf16[960,256]{1,0:T(8,128)(2,1)} %collective-permute-done.7.refs_9_), channel_id=1, source_target_pairs={{0,1},{1,0},{2,3},{3,2},{4,5},{5,4},{6,7},{7,6},{8,9},{9,8},{10,11... | collective-permute-start | bytes 1474568 | tf_op jit(solution)/shard_map/ppermute | solution.py:308
  51.8 12.2 %collective-permute-start.15 = (bf16[960,256]{1,0:T(8,128)(2,1)S(1)}, bf16[960,256]{1,0:T(8,128)(2,1)S(1)}, u32[]{:S(2)}, u32[]{:S(2)}) collective-permute-start(bf16[960,256]{1,0:T(8,128)(2,1)S(1)} %copy-done.22), channel_id=1, source_target_pairs={{0,2},{1,3},{2,0},{3,1},{4,6},{5,7},{6,4},{7,5},{8,10},{9,11},{10,... | collective-permute-start | bytes 1474568 | tf_op jit(solution)/shard_map/ppermute | solution.py:308
  62.2 15.0 %collective-permute-start.19 = (bf16[368,640]{1,0:T(8,128)(2,1)S(1)}, bf16[368,640]{1,0:T(8,128)(2,1)S(1)}, u32[]{:S(2)}, u32[]{:S(2)}) collective-permute-start(bf16[368,640]{1,0:T(8,128)(2,1)S(1)} %slice.18), channel_id=1, source_target_pairs={{0,8},{2,10},{4,12},{6,14},{8,16},{10,18},{12,20},{14,22},{16,24},... | collective-permute-start | bytes 1413128 | tf_op jit(solution)/shard_map/ppermute | solution.py:312
  62.3 15.8 %collective-permute-start.17 = (bf16[960,256]{1,0:T(8,128)(2,1)}, bf16[960,256]{1,0:T(8,128)(2,1)S(1)}, u32[]{:S(2)}, u32[]{:S(2)}) collective-permute-start(bf16[960,256]{1,0:T(8,128)(2,1)} %collective-permute-done.4.refs_1_), channel_id=1, source_target_pairs={{0,4},{1,5},{2,6},{3,7},{4,0},{5,1},{6,2},{7,3},{8,12},{9,13},{10,... | collective-permute-start | bytes 1474568 | tf_op jit(solution)/shard_map/ppermute | solution.py:308
  62.9 15.1 %collective-permute-start.18 = (bf16[960,256]{1,0:T(8,128)(2,1)S(1)}, bf16[960,256]{1,0:T(8,128)(2,1)S(1)}, u32[]{:S(2)}, u32[]{:S(2)}) collective-permute-start(bf16[960,256]{1,0:T(8,128)(2,1)S(1)} %collective-permute-done.9.refs_10_), channel_id=1, source_target_pairs={{0,1},{1,0},{2,3},{3,2},{4,5},{5,4},{6,7},{7,6},{8,9},{9,8},{10,11... | collective-permute-start | bytes 1474568 | tf_op jit(solution)/shard_map/ppermute | solution.py:308
  64.0 14.6 %collective-permute-start.21 = (bf16[960,256]{1,0:T(8,128)(2,1)}, bf16[960,256]{1,0:T(8,128)(2,1)S(1)}, u32[]{:S(2)}, u32[]{:S(2)}) collective-permute-start(bf16[960,256]{1,0:T(8,128)(2,1)} %collective-permute-done.7.refs_9_), channel_id=1, source_target_pairs={{0,2},{1,3},{2,0},{3,1},{4,6},{5,7},{6,4},{7,5},{8,10},{9,11},{10,... | collective-permute-start | bytes 1474568 | tf_op jit(solution)/shard_map/ppermute | solution.py:308
  64.0 14.8 %collective-permute-start.14 = (bf16[960,256]{1,0:T(8,128)(2,1)}, bf16[960,256]{1,0:T(8,128)(2,1)S(1)}, u32[]{:S(2)}, u32[]{:S(2)}) collective-permute-start(bf16[960,256]{1,0:T(8,128)(2,1)} %collective-permute-done.4.refs_1_), channel_id=1, source_target_pairs={{0,2},{1,3},{2,0},{3,1},{4,6},{5,7},{6,4},{7,5},{8,10},{9,11},{10,... | collective-permute-start | bytes 1474568 | tf_op jit(solution)/shard_map/ppermute | solution.py:308
  78.6 12.1 %collective-permute-start.23 = (bf16[960,256]{1,0:T(8,128)(2,1)S(1)}, bf16[960,256]{1,0:T(8,128)(2,1)S(1)}, u32[]{:S(2)}, u32[]{:S(2)}) collective-permute-start(bf16[960,256]{1,0:T(8,128)(2,1)S(1)} %collective-permute-done.17.refs_11_), channel_id=1, source_target_pairs={{0,2},{1,3},{2,0},{3,1},{4,6},{5,7},{6,4},{7,5},{8,10},{9,11},{10,... | collective-permute-start | bytes 1474568 | tf_op jit(solution)/shard_map/ppermute | solution.py:308
  79.5 11.2 %collective-permute-start.25 = (bf16[960,256]{1,0:T(8,128)(2,1)S(1)}, bf16[960,256]{1,0:T(8,128)(2,1)S(1)}, u32[]{:S(2)}, u32[]{:S(2)}) collective-permute-start(bf16[960,256]{1,0:T(8,128)(2,1)S(1)} %collective-permute-done.18.refs_13_), channel_id=1, source_target_pairs={{0,2},{1,3},{2,0},{3,1},{4,6},{5,7},{6,4},{7,5},{8,10},{9,11},{10,... | collective-permute-start | bytes 1474568 | tf_op jit(solution)/shard_map/ppermute | solution.py:308
  80.3 14.5 %collective-permute-start.29 = (bf16[352,640]{1,0:T(8,128)(2,1)S(1)}, bf16[352,640]{1,0:T(8,128)(2,1)S(1)}, u32[]{:S(2)}, u32[]{:S(2)}) collective-permute-start(bf16[352,640]{1,0:T(8,128)(2,1)S(1)} %slice.19), channel_id=1, source_target_pairs={{0,8},{2,10},{4,12},{6,14},{8,16},{10,18},{12,20},{14,22},{16,24},... | collective-permute-start | bytes 1351688 | tf_op jit(solution)/shard_map/ppermute | solution.py:312
  95.5 23.4 %collective-permute-start.31 = (bf16[720,512]{1,0:T(8,128)(2,1)S(1)}, bf16[720,512]{1,0:T(8,128)(2,1)}, u32[]{:S(2)}, u32[]{:S(2)}) collective-permute-start(bf16[720,512]{1,0:T(8,128)(2,1)S(1)} %maximum_select_fusion.2.refs_0_), channel_id=1, source_target_pairs={{0,8},{2,10},{4,12},{6,14},{8,16},{10,18},{12,20},{14,22},{16,24},... | collective-permute-start | bytes 2211848 | tf_op jit(solution)/shard_map/ppermute | solution.py:312
  112.6 13.2 %collective-permute-start.32 = (bf16[720,512]{1,0:T(8,128)(2,1)S(1)}, bf16[720,512]{1,0:T(8,128)(2,1)S(1)}, u32[]{:S(2)}, u32[]{:S(2)}) collective-permute-start(bf16[720,512]{1,0:T(8,128)(2,1)S(1)} %maximum_select_fusion.2.refs_0_), channel_id=1, source_target_pairs={{0,2},{1,3},{2,0},{3,1},{4,6},{5,7},{6,4},{7,5},{8,10},{9,11},{10,... | collective-permute-start | bytes 2211848 | tf_op jit(solution)/shard_map/ppermute | solution.py:308
  119.4 20.7 %collective-permute-start.36 = (bf16[720,512]{1,0:T(8,128)(2,1)}, bf16[720,512]{1,0:T(8,128)(2,1)S(1)}, u32[]{:S(2)}, u32[]{:S(2)}) collective-permute-start(bf16[720,512]{1,0:T(8,128)(2,1)} %collective-permute-done.31.refs_1_), channel_id=1, source_target_pairs={{0,8},{2,10},{4,12},{6,14},{8,16},{10,18},{12,20},{14,22},{16,24},... | collective-permute-start | bytes 2211848 | tf_op jit(solution)/shard_map/ppermute | solution.py:312
  129.7 11.9 %collective-permute-start.42 = (bf16[720,256]{1,0:T(8,128)(2,1)S(1)}, bf16[720,256]{1,0:T(8,128)(2,1)S(1)}, u32[]{:S(2)}, u32[]{:S(2)}) collective-permute-start(bf16[720,256]{1,0:T(8,128)(2,1)S(1)} %get-tuple-element.207), channel_id=1, source_target_pairs={{0,1},{1,0},{2,3},{3,2},{4,5},{5,4},{6,7},{7,6},{8,9},{9,8},{10,11... | collective-permute-start | bytes 1105928 | tf_op jit(solution)/shard_map/ppermute | solution.py:308
  130.8 11.5 %collective-permute-start.43 = (bf16[720,256]{1,0:T(8,128)(2,1)S(1)}, bf16[720,256]{1,0:T(8,128)(2,1)S(1)}, u32[]{:S(2)}, u32[]{:S(2)}) collective-permute-start(bf16[720,256]{1,0:T(8,128)(2,1)S(1)} %get-tuple-element.208), channel_id=1, source_target_pairs={{0,4},{1,5},{2,6},{3,7},{4,0},{5,1},{6,2},{7,3},{8,12},{9,13},{10,... | collective-permute-start | bytes 1105928 | tf_op jit(solution)/shard_map/ppermute | solution.py:308
  140.1 13.0 %collective-permute-start.39 = (bf16[720,512]{1,0:T(8,128)(2,1)S(1)}, bf16[720,512]{1,0:T(8,128)(2,1)S(1)}, u32[]{:S(2)}, u32[]{:S(2)}) collective-permute-start(bf16[720,512]{1,0:T(8,128)(2,1)S(1)} %collective-permute-done.36.refs_0_), channel_id=1, source_target_pairs={{0,2},{1,3},{2,0},{3,1},{4,6},{5,7},{6,4},{7,5},{8,10},{9,11},{10,... | collective-permute-start | bytes 2211848 | tf_op jit(solution)/shard_map/ppermute | solution.py:308
  140.1 20.7 %collective-permute-start.48 = (bf16[720,512]{1,0:T(8,128)(2,1)S(1)}, bf16[720,512]{1,0:T(8,128)(2,1)S(1)}, u32[]{:S(2)}, u32[]{:S(2)}) collective-permute-start(bf16[720,512]{1,0:T(8,128)(2,1)S(1)} %collective-permute-done.36.refs_0_), channel_id=1, source_target_pairs={{0,8},{2,10},{4,12},{6,14},{8,16},{10,18},{12,20},{14,22},{16,24},... | collective-permute-start | bytes 2211848 | tf_op jit(solution)/shard_map/ppermute | solution.py:312
  140.6 10.7 %collective-permute-start.37 = (bf16[720,256]{1,0:T(8,128)(2,1)S(1)}, bf16[720,256]{1,0:T(8,128)(2,1)S(1)}, u32[]{:S(2)}, u32[]{:S(2)}) collective-permute-start(bf16[720,256]{1,0:T(8,128)(2,1)S(1)} %get-tuple-element.199), channel_id=1, source_target_pairs={{0,1},{1,0},{2,3},{3,2},{4,5},{5,4},{6,7},{7,6},{8,9},{9,8},{10,11... | collective-permute-start | bytes 1105928 | tf_op jit(solution)/shard_map/ppermute | solution.py:308
  141.6 11.5 %collective-permute-start.38 = (bf16[720,256]{1,0:T(8,128)(2,1)S(1)}, bf16[720,256]{1,0:T(8,128)(2,1)S(1)}, u32[]{:S(2)}, u32[]{:S(2)}) collective-permute-start(bf16[720,256]{1,0:T(8,128)(2,1)S(1)} %get-tuple-element.200), channel_id=1, source_target_pairs={{0,4},{1,5},{2,6},{3,7},{4,0},{5,1},{6,2},{7,3},{8,12},{9,13},{10,... | collective-permute-start | bytes 1105928 | tf_op jit(solution)/shard_map/ppermute | solution.py:308
  143.1 24.1 %collective-permute-start.45 = (bf16[720,256]{1,0:T(8,128)(2,1)}, bf16[720,256]{1,0:T(8,128)(2,1)}, u32[]{:S(2)}, u32[]{:S(2)}) collective-permute-start(bf16[720,256]{1,0:T(8,128)(2,1)} %add_convert_fusion.2), channel_id=1, source_target_pairs={{0,4},{1,5},{2,6},{3,7},{4,0},{5,1},{6,2},{7,3},{8,12},{9,13},{10,... | collective-permute-start | bytes 1105928 | tf_op jit(solution)/shard_map/ppermute | solution.py:308
  151.3 15.9 %collective-permute-start.44 = (bf16[720,256]{1,0:T(8,128)(2,1)}, bf16[720,256]{1,0:T(8,128)(2,1)}, u32[]{:S(2)}, u32[]{:S(2)}) collective-permute-start(bf16[720,256]{1,0:T(8,128)(2,1)} %add_convert_fusion.3), channel_id=1, source_target_pairs={{0,1},{1,0},{2,3},{3,2},{4,5},{5,4},{6,7},{7,6},{8,9},{9,8},{10,11... | collective-permute-start | bytes 1105928 | tf_op jit(solution)/shard_map/ppermute | solution.py:308
  171.6 12.8 %collective-permute-start.53 = (bf16[368,256]{1,0:T(8,128)(2,1)S(1)}, bf16[368,256]{1,0:T(8,128)(2,1)S(1)}, u32[]{:S(2)}, u32[]{:S(2)}) collective-permute-start(bf16[368,256]{1,0:T(8,128)(2,1)S(1)} %add_convert_fusion.7), channel_id=1, source_target_pairs={{0,4},{1,5},{2,6},{3,7},{4,0},{5,1},{6,2},{7,3},{8,12},{9,13},{10,... | collective-permute-start | bytes 565256 | tf_op jit(solution)/shard_map/ppermute | solution.py:308
  (77 other events, 617.8 us)

commit v4 on v3

--- a/solution.py
+++ b/solution.py
@@ -38,90 +38,12 @@
     return lax.dot_general(one, other, (((0,), (0,)), ((), ())), preferred_element_type=jnp.float32)
 
 
-def project_kernel(zs, order, *refs, cuts):
-    slabs = zs.shape[0]
-    pieces, weights = refs[: len(cuts)], refs[len(cuts) : -8]
-    cosine, sine, kv_out, q_out, tail_out, held, w_held, sems = refs[-8:]
-    pairs, features, lanes = held.shape
-    depth, block, half = features // slabs, lanes // 2, HEAD_WIDTH // 2
-    loads = []
-    row = 0
-    for i, w in enumerate(weights):
-        rows = pl.ds(pl.multiple_of(zs[row // depth] * depth + row % depth, 16), w.shape[0])
-        loads.append((0, pltpu.make_async_copy(w, w_held.at[rows], sems.at[len(cuts) + i])))
-        row += w.shape[0]
-    for i, (at, start, rows) in enumerate(cuts):
-        target = held.at[at // 2, pl.ds(start, rows), pl.ds(at % 2 * block, block)]
-        loads.append((at // 2, pltpu.make_async_copy(pieces[i], target, sems.at[i])))
-    for _, load in loads:
-        load.start()
-
-    def product_of(pair):
-        for at, load in loads:
-            if at == pair:
-                load.wait()
-        return columns_dot(w_held[...], held[pair])
-
-    def finish_of(pair, product):
-        for side in range(2):
-            place = order[2 * pair + side]
-            total = product[:, side * block : (side + 1) * block]
-            lanes = pl.ds(pl.multiple_of(place * block, block), block)
-            cos, sin = cosine[:, lanes], sine[:, lanes]
-
-            def rotated(at):
-                lower, upper = total[at : at + half], total[at + half : at + 2 * half]
-                return jnp.concatenate([lower * cos - upper * sin, upper * cos + lower * sin], axis=0)
-
-            kv_out[0:HEAD_WIDTH, lanes] = rotated(0).astype(jnp.bfloat16)
-            kv_out[HEAD_WIDTH : 2 * HEAD_WIDTH, lanes] = total[HEAD_WIDTH : 2 * HEAD_WIDTH].astype(jnp.bfloat16)
-            for h in range(q_out.shape[1] // HEAD_WIDTH):
-                q_out[place, h * HEAD_WIDTH : (h + 1) * HEAD_WIDTH] = (
-                    rotated((h + 2) * HEAD_WIDTH) * score_scale
-                ).astype(jnp.bfloat16)
-
-    ahead = product_of(0)
-    for pair in range(pairs):
-        product = ahead
-        if pair + 1 < pairs:
-            ahead = product_of(pair + 1)
-        finish_of(pair, product)
-    tail_out[...] = kv_out[:, kv_out.shape[1] - WINDOW_KEYS :]
-
-
-def project(zs, order, pieces, weights, cosine, sine):
-    (features, width), block = (sum(w.shape[0] for w in weights), weights[0].shape[1]), pieces[0].shape[1]
-    blocks = order.shape[0]
-    kv_width = 2 * HEAD_WIDTH
-    cuts, at, start = [], 0, 0
-    for piece in pieces:
-        cuts.append((at, start, piece.shape[0]))
-        at, start = (at, start + piece.shape[0]) if start + piece.shape[0] < features else (at + 1, 0)
-    vmem = pl.BlockSpec(memory_space=pltpu.VMEM)
-    return pl.pallas_call(
-        functools.partial(project_kernel, cuts=cuts),
-        in_specs=[pl.BlockSpec(memory_space=pltpu.SMEM)] * 2
-        + [pl.BlockSpec(memory_space=pl.ANY)] * (len(pieces) + len(weights))
-        + [vmem] * 2,
-        out_specs=[vmem] * 3,
-        out_shape=[
-            jax.ShapeDtypeStruct((kv_width, blocks * block), jnp.bfloat16),
-            jax.ShapeDtypeStruct((blocks, width - kv_width, block), jnp.bfloat16),
-            jax.ShapeDtypeStruct((kv_width, WINDOW_KEYS), jnp.bfloat16),
-        ],
-        scratch_shapes=[
-            pltpu.VMEM((blocks // 2, features, 2 * block), jnp.bfloat16),
-            pltpu.VMEM((features, width), jnp.bfloat16),
-            pltpu.SemaphoreType.DMA((len(pieces) + len(weights),)),
-        ],
-        compiler_params=pltpu.CompilerParams(vmem_limit_bytes=wide_vmem_bytes),
-        cost_estimate=small_cost,
-        name="project",
-    )(zs, order, *pieces, *weights, cosine, sine)
-
-
 def attend_kernel(first, sinks, q, kv, *refs, low):
     *tail, give, keep, keys, values = refs
+    attend_blocks(first, sinks, q, kv, tail, give, keep, keys, values, low, 0)
+
+
+def attend_blocks(first, sinks, q, kv, tail, give, keep, keys, values, low, base):
     window = WINDOW_KEYS
     width, block = q.shape[1:]
     heads = width // HEAD_WIDTH
@@ -163,7 +85,7 @@
         out = []
         for h in range(0, heads, 2):
             rows = slice(h * HEAD_WIDTH, (h + 1) * HEAD_WIDTH), slice((h + 1) * HEAD_WIDTH, (h + 2) * HEAD_WIDTH)
-            pair = jnp.concatenate([q[at_block(unit), r, lanes] for r in rows], axis=1)
+            pair = jnp.concatenate([q[base + at_block(unit), r, lanes] for r in rows], axis=1)
             out.append(jnp.dot(key_rows, pair, preferred_element_type=jnp.float32))
         return out
 
@@ -225,6 +147,96 @@
         cost_estimate=small_cost,
         name="attend",
     )(first, sinks, q, kv, *tail)
+
+
+def project_kernel(zs, order, first, sinks, *refs, cuts):
+    slabs = zs.shape[0]
+    pieces, weights = refs[: len(cuts)], refs[len(cuts) : -14]
+    cosine, sine, kv_low, q_low, tail_out, give, keep, held, w_held, kv_out, q_out, keys, values, sems = refs[-14:]
+    pairs, features, lanes = held.shape
+    depth, block, half = features // slabs, lanes // 2, HEAD_WIDTH // 2
+    loads = []
+    row = 0
+    for i, w in enumerate(weights):
+        rows = pl.ds(pl.multiple_of(zs[row // depth] * depth + row % depth, 16), w.shape[0])
+        loads.append((0, pltpu.make_async_copy(w, w_held.at[rows], sems.at[len(cuts) + i])))
+        row += w.shape[0]
+    for i, (at, start, rows) in enumerate(cuts):
+        target = held.at[at // 2, pl.ds(start, rows), pl.ds(at % 2 * block, block)]
+        loads.append((at // 2, pltpu.make_async_copy(pieces[i], target, sems.at[i])))
+    for _, load in loads:
+        load.start()
+
+    def product_of(pair):
+        for at, load in loads:
+            if at == pair:
+                load.wait()
+        return columns_dot(w_held[...], held[pair])
+
+    def finish_of(pair, product):
+        for side in range(2):
+            place = order[2 * pair + side]
+            total = product[:, side * block : (side + 1) * block]
+            lanes = pl.ds(pl.multiple_of(place * block, block), block)
+            cos, sin = cosine[:, lanes], sine[:, lanes]
+
+            def rotated(at):
+                lower, upper = total[at : at + half], total[at + half : at + 2 * half]
+                return jnp.concatenate([lower * cos - upper * sin, upper * cos + lower * sin], axis=0)
+
+            kv_out[0:HEAD_WIDTH, lanes] = rotated(0).astype(jnp.bfloat16)
+            kv_out[HEAD_WIDTH : 2 * HEAD_WIDTH, lanes] = total[HEAD_WIDTH : 2 * HEAD_WIDTH].astype(jnp.bfloat16)
+            for h in range(q_out.shape[1] // HEAD_WIDTH):
+                q_out[place, h * HEAD_WIDTH : (h + 1) * HEAD_WIDTH] = (
+                    rotated((h + 2) * HEAD_WIDTH) * score_scale
+                ).astype(jnp.bfloat16)
+
+    ahead = product_of(0)
+    for pair in range(pairs):
+        product = ahead
+        if pair + 1 < pairs:
+            ahead = product_of(pair + 1)
+        finish_of(pair, product)
+    tail_out[...] = kv_out[:, kv_out.shape[1] - WINDOW_KEYS :]
+    kv_low[...] = kv_out[:, : kv_low.shape[1]]
+    q_low[...] = q_out[: q_low.shape[0]]
+    attend_blocks(first, sinks, q_out, kv_out, (), give, keep, keys, values, pairs * block, pairs)
+
+
+def project(zs, order, first, sinks, pieces, weights, cosine, sine):
+    (features, width), block = (sum(w.shape[0] for w in weights), weights[0].shape[1]), pieces[0].shape[1]
+    blocks = order.shape[0]
+    kv_width = 2 * HEAD_WIDTH
+    cuts, at, start = [], 0, 0
+    for piece in pieces:
+        cuts.append((at, start, piece.shape[0]))
+        at, start = (at, start + piece.shape[0]) if start + piece.shape[0] < features else (at + 1, 0)
+    vmem = pl.BlockSpec(memory_space=pltpu.VMEM)
+    return pl.pallas_call(
+        functools.partial(project_kernel, cuts=cuts),
+        in_specs=[pl.BlockSpec(memory_space=pltpu.SMEM)] * 4
+        + [pl.BlockSpec(memory_space=pl.ANY)] * (len(pieces) + len(weights))
+        + [vmem] * 2,
+        out_specs=[vmem] * 5,
+        out_shape=[
+            jax.ShapeDtypeStruct((kv_width, blocks // 2 * block), jnp.bfloat16),
+            jax.ShapeDtypeStruct((blocks // 2, width - kv_width, block), jnp.bfloat16),
+            jax.ShapeDtypeStruct((kv_width, WINDOW_KEYS), jnp.bfloat16),
+            *[jax.ShapeDtypeStruct((blocks // 4, width - kv_width, block), jnp.bfloat16)] * 2,
+        ],
+        scratch_shapes=[
+            pltpu.VMEM((blocks // 2, features, 2 * block), jnp.bfloat16),
+            pltpu.VMEM((features, width), jnp.bfloat16),
+            pltpu.VMEM((kv_width, blocks * block), jnp.bfloat16),
+            pltpu.VMEM((blocks, width - kv_width, block), jnp.bfloat16),
+            pltpu.VMEM((blocks // 2 * block + WINDOW_KEYS, HEAD_WIDTH), jnp.bfloat16),
+            pltpu.VMEM((HEAD_WIDTH, blocks // 2 * block + WINDOW_KEYS), jnp.bfloat16),
+            pltpu.SemaphoreType.DMA((len(pieces) + len(weights),)),
+        ],
+        compiler_params=pltpu.CompilerParams(vmem_limit_bytes=wide_vmem_bytes),
+        cost_estimate=small_cost,
+        name="project",
+    )(zs, order, first, sinks, *pieces, *weights, cosine, sine)
 
 
 def first_part(weights):
@@ -387,10 +399,10 @@
     own_out = by(row, near_out, by(core, *far_out))
     own_out_late, weights_in[-1] = tie(own_out, weights_in[-1])
     weights_out = [own_out, turn(own_out_late)]
-    kv, q, kv_tail = project(slabs_held, order, pieces, weights_in, cosine, sine)
+    kv, q, kv_tail, *later = project(slabs_held, order, first_row, head_sinks, pieces, weights_in, cosine, sine)
     kv_tail = shift(kv_tail, "seq", SLICES)
-    mixed = [None, list(attend(first_row, head_sinks, q, kv, 1))]
-    mixed[1][1], kv_tail, weights_out[1] = tie(mixed[1][1], kv_tail, weights_out[1])
+    kv_tail, weights_out[1] = tie(kv_tail, weights_out[1])
+    mixed = [None, later]
     mixed[0] = attend(first_row, head_sinks, q, kv, 0, (kv_tail,))
     came = [swap(give, 1, 0) for give, _ in mixed]
     kept = [keep for _, keep in mixed]

time: 194 us -> 193 us (level)
  waiting for transfers between devices: 85.4 us -> 90.1 us
  local copies, waits for them, and re-layouts: 13.5 us -> 11.4 us
    pallas_call x2 -> x1, Pallas kernels: 7.02 us -> 3.5 us  [attend(): pl.pallas_call(functools.partial(attend_kernel, low=half * 4 * block), gr...]
    unnamed x102 -> x96, local copies, waits for them, and re-layouts: 10 us -> 7.52 us
    pallas_call x1, Pallas kernels: 14.8 us -> 17.4 us  [project(): pl.pallas_call(functools.partial(project_kernel, cuts=cuts), in_specs=[pl...]
    ppermute x49, waiting for transfers between devices: 41 us -> 43.2 us  [swap(): return lax.ppermute(value, both, pairs)]
  transfers between devices with their start and end apart: 58 -> 58, of which waited for: 25 -> 27; matrix products, arithmetic and copies ran while one was open for 8% -> 8% of each run, Pallas kernels for 19% -> 18%
where the time goes in v4:
time: 193 us; the launch traced here: 192 us
  waiting for transfers between devices  90.1 us (47%)
  starting transfers between devices  40.7 us (21%)
  Pallas kernels  34.9 us (18%)
  other arithmetic  14.5 us (8%)
  local copies, waits for them, and re-layouts  11.4 us (6%)
    ppermute x8, waiting for transfers between devices, turn(): return lax.ppermute(value, 'seq', pairs)  45.4 us
    ppermute x49, waiting for transfers between devices, swap(): return lax.ppermute(value, both, pairs)  43.2 us
    ppermute x49, starting transfers between devices, swap(): return lax.ppermute(value, both, pairs)  35.3 us
    pallas_call x1, Pallas kernels, project(): pl.pallas_call(functools.partial(project_kernel, cuts=cuts), in_specs=[pl...  17.4 us
    pallas_call x6, Pallas kernels, output_sums(): pl.pallas_call(functools.partial(sums_kernel, count=len(w_near), crossing...  14.1 us
    unnamed x96, local copies, waits for them, and re-layouts  7.52 us
    ppermute x8, starting transfers between devices, turn(): return lax.ppermute(value, 'seq', pairs)  3.96 us
  transfers between devices with their start and end apart: 58, of which 27 were waited for; matrix products, arithmetic and copies ran while one was open for 8% of the time, Pallas kernels for 18%

profile of v4, /device:TPU:0, one launch (start us, length us, event | category | flops | bytes accessed | tf_op | source)
XLA Modules:
  0.0 192.4 jit_solution(9724377460797236857)
XLA Ops:
  4.4 2.9 %collective-permute-start.4 = (bf16[960,256]{1,0:T(8,128)(2,1)S(1)}, bf16[960,256]{1,0:T(8,128)(2,1)}, u32[]{:S(2)}, u32[]{:S(2)}) collective-permute-start(bf16[960,256]{1,0:T(8,128)(2,1)S(1)} %get-tuple-element.139), channel_id=1, source_target_pairs={{0,1},{1,0},{2,3},{3,2},{4,5},{5,4},{6,7},{7,6},{8,9},{9,8},{10,11... | collective-permute-start | bytes 1474568 | tf_op jit(solution)/shard_map/ppermute | solution.py:320
  7.3 1.6 collective-permute-start.2
  11.1 4.8 %collective-permute-done.2 = bf16[180,640]{1,0:T(8,128)(2,1)S(1)} collective-permute-done((bf16[180,640]{1,0:T(8,128)(2,1)S(1)}, bf16[180,640]{1,0:T(8,128)(2,1)S(1)}, u32[]{:S(2)}, u32[]{:S(2)}) %collective-permute-start.2) | collective-permute-done | bytes 230432 | tf_op jit(solution)/shard_map/ppermute | solution.py:320
  15.9 3.0 %collective-permute-done.3 = bf16[180,640]{1,0:T(8,128)(2,1)S(1)} collective-permute-done((bf16[180,640]{1,0:T(8,128)(2,1)S(1)}, bf16[180,640]{1,0:T(8,128)(2,1)S(1)}, u32[]{:S(2)}, u32[]{:S(2)}) %collective-permute-start.3) | collective-permute-done | bytes 230432 | tf_op jit(solution)/shard_map/ppermute | solution.py:320
  19.1 3.8 %collective-permute-done.1 = bf16[360,640]{1,0:T(8,128)(2,1)} collective-permute-done((bf16[360,640]{1,0:T(8,128)(2,1)S(1)}, bf16[360,640]{1,0:T(8,128)(2,1)}, u32[]{:S(2)}, u32[]{:S(2)}) %collective-permute-start.1) | collective-permute-done | bytes 460832 | tf_op jit(solution)/shard_map/ppermute | solution.py:324
  26.6 10.1 %collective-permute-done.5 = bf16[360,640]{1,0:T(8,128)(2,1)} collective-permute-done((bf16[360,640]{1,0:T(8,128)(2,1)S(1)}, bf16[360,640]{1,0:T(8,128)(2,1)}, u32[]{:S(2)}, u32[]{:S(2)}) %collective-permute-start.5) | collective-permute-done | bytes 460832 | tf_op jit(solution)/shard_map/ppermute | solution.py:324
  39.5 1.7 maximum_select_fusion.1.refs_21_
  41.3 1.8 multiply_sine_fusion
  44.3 3.2 %collective-permute-done.8.refs_3_ = bf16[960,256]{1,0:T(8,128)(2,1)S(1)} collective-permute-done((bf16[960,256]{1,0:T(8,128)(2,1)}, bf16[960,256]{1,0:T(8,128)(2,1)S(1)}, u32[]{:S(2)}, u32[]{:S(2)}) %collective-permute-start.8) | collective-permute-done | bytes 491552 | tf_op jit(solution)/shard_map/ppermute | solution.py:320
  47.5 2.0 %collective-permute-done.9.refs_10_ = bf16[960,256]{1,0:T(8,128)(2,1)S(1)} collective-permute-done((bf16[960,256]{1,0:T(8,128)(2,1)}, bf16[960,256]{1,0:T(8,128)(2,1)S(1)}, u32[]{:S(2)}, u32[]{:S(2)}) %collective-permute-start.9) | collective-permute-done | bytes 491552 | tf_op jit(solution)/shard_map/ppermute | solution.py:320
  51.5 10.6 %collective-permute-done.10.refs_22_ = bf16[720,640]{1,0:T(8,128)(2,1)S(1)} collective-permute-done((bf16[720,640]{1,0:T(8,128)(2,1)S(1)}, bf16[720,640]{1,0:T(8,128)(2,1)S(1)}, u32[]{:S(2)}, u32[]{:S(2)}) %collective-permute-start.10) | collective-permute-done | bytes 921632 | tf_op jit(solution)/shard_map/ppermute | solution.py:324
  64.4 12.9 %collective-permute-done.19.refs_23_ = bf16[368,640]{1,0:T(8,128)(2,1)} collective-permute-done((bf16[368,640]{1,0:T(8,128)(2,1)S(1)}, bf16[368,640]{1,0:T(8,128)(2,1)}, u32[]{:S(2)}, u32[]{:S(2)}) %collective-permute-start.19) | collective-permute-done | bytes 471072 | tf_op jit(solution)/shard_map/ppermute | solution.py:324
  82.7 5.5 %collective-permute-done.26 = bf16[180,512]{1,0:T(8,128)(2,1)S(1)} collective-permute-done((bf16[180,512]{1,0:T(8,128)(2,1)S(1)}, bf16[180,512]{1,0:T(8,128)(2,1)S(1)}, u32[]{:S(2)}, u32[]{:S(2)}) %collective-permute-start.26) | collective-permute-done | bytes 184352 | tf_op jit(solution)/shard_map/ppermute | solution.py:320
  88.2 2.4 %collective-permute-done.27 = bf16[180,512]{1,0:T(8,128)(2,1)S(1)} collective-permute-done((bf16[180,512]{1,0:T(8,128)(2,1)S(1)}, bf16[180,512]{1,0:T(8,128)(2,1)S(1)}, u32[]{:S(2)}, u32[]{:S(2)}) %collective-permute-start.27) | collective-permute-done | bytes 184352 | tf_op jit(solution)/shard_map/ppermute | solution.py:320
  91.8 2.3 %collective-permute-done.29.refs_24_ = bf16[352,640]{1,0:T(8,128)(2,1)S(1)} collective-permute-done((bf16[352,640]{1,0:T(8,128)(2,1)S(1)}, bf16[352,640]{1,0:T(8,128)(2,1)S(1)}, u32[]{:S(2)}, u32[]{:S(2)}) %collective-permute-start.29) | collective-permute-done | bytes 450592 | tf_op jit(solution)/shard_map/ppermute | solution.py:324
  94.9 17.4 %project.1 = (bf16[128,1024]{1,0:T(8,128)(2,1)}, bf16[4,512,256]{2,1,0:T(8,128)(2,1)}, bf16[128,128]{1,0:T(8,128)(2,1)}, bf16[2,512,256]{2,1,0:T(8,128)(2,1)}, bf16[2,512,256]{2,1,0:T(8,128)(2,1)}) custom-call(s32[4]{0:T(128)} %pad_add_fusion.zs, s32[8]{0:T(128)} %stack.73.order, s32[2]{0:T(128)} %pad_add_fusion.2.first, f32[8]{0:T(128)} %dynamic_slice.47.sinks, ...), custom_call_target="tpu_custom_call" | custom-call | flops 1000 | bytes 1000 | tf_op jit(solution)/shard_map/project/pallas_call | solution.py:215
  115.6 2.2 %collective-permute-start.36 = (bf16[720,512]{1,0:T(8,128)(2,1)}, bf16[720,512]{1,0:T(8,128)(2,1)S(1)}, u32[]{:S(2)}, u32[]{:S(2)}) collective-permute-start(bf16[720,512]{1,0:T(8,128)(2,1)} %collective-permute-done.31.refs_1_), channel_id=1, source_target_pairs={{0,8},{2,10},{4,12},{6,14},{8,16},{10,18},{12,20},{14,22},{16,24},... | collective-permute-start | bytes 2211848 | tf_op jit(solution)/shard_map/ppermute | solution.py:324
  120.3 3.5 %attend.1 = (bf16[2,512,256]{2,1,0:T(8,128)(2,1)S(1)}, bf16[2,512,256]{2,1,0:T(8,128)(2,1)S(1)}) custom-call(s32[2]{0:T(128)S(1)} %copy-done.15, f32[8]{0:T(128)S(1)} %copy-done.14, bf16[4,512,256]{2,1,0:T(8,128)(2,1)S(1)} %copy-done.4, bf16[128,1024]{1,0:T(8,128)(2,1)S(1)} %copy-done.13, bf16[128,128]{1,0:T(8,128)(2,1)S(1)} %collective-permute-done.30.refs_0_), custom_call_target="tpu_custom_call" | custom-call | flops 1000 | bytes 1000 | tf_op jit(solution)/shard_map/attend/pallas_call | solution.py:132
  124.1 1.6 collective-permute-done.34.refs_6_.refs_4_
  125.8 2.3 %crossing_sums.4 = (bf16[720,256]{1,0:T(8,128)(2,1)S(1)}, bf16[720,256]{1,0:T(8,128)(2,1)S(1)}) custom-call(s32[2]{0:T(128)S(1)} %pad_add_fusion.1.sides, bf16[720,512]{1,0:T(8,128)(2,1)S(1)} %maximum_select_fusion.2.refs_0_, bf16[720,512]{1,0:T(8,128)(2,1)} %collective-permute-done.31.refs_1_, bf16[720,512]{1,0:T(8,128)(2,1)S(1)} %collective-permute-done.32.refs_2_, ...), custom_call_target="tpu_custom_call" | custom-call | flops 1000 | bytes 1000 | tf_op jit(solution)/shard_map/crossing_sums/pallas_call | solution.py:292
  130.4 4.2 %output_sums.3 = (f32[720,256]{1,0:T(8,128)S(1)}, f32[720,256]{1,0:T(8,128)S(1)}, bf16[720,256]{1,0:T(8,128)(2,1)S(1)}, f32[720,256]{1,0:T(8,128)S(1)}, f32[720,...) custom-call(s32[2]{0:T(128)S(1)} %pad_add_fusion.1.sides, bf16[720,512]{1,0:T(8,128)(2,1)} %copy-done.1, ...), custom_call_target="tpu_custom_call" | custom-call | flops 1000 | bytes 1000 | tf_op jit(solution)/shard_map/output_sums/pallas_call | solution.py:292
  135.5 4.1 %collective-permute-done.36.refs_0_ = bf16[720,512]{1,0:T(8,128)(2,1)S(1)} collective-permute-done((bf16[720,512]{1,0:T(8,128)(2,1)}, bf16[720,512]{1,0:T(8,128)(2,1)S(1)}, u32[]{:S(2)}, u32[]{:S(2)}) %collective-permute-start.36) | collective-permute-done | bytes 737312 | tf_op jit(solution)/shard_map/ppermute | solution.py:324
  143.9 6.7 %collective-permute-done.37 = bf16[720,256]{1,0:T(8,128)(2,1)S(1)} collective-permute-done((bf16[720,256]{1,0:T(8,128)(2,1)S(1)}, bf16[720,256]{1,0:T(8,128)(2,1)S(1)}, u32[]{:S(2)}, u32[]{:S(2)}) %collective-permute-start.37) | collective-permute-done | bytes 368672 | tf_op jit(solution)/shard_map/ppermute | solution.py:320
  151.6 2.5 %output_sums.4 = (f32[368,256]{1,0:T(8,128)S(1)}, f32[352,256]{1,0:T(8,128)S(1)}, bf16[368,256]{1,0:T(8,128)(2,1)}, f32[352,256]{1,0:T(8,128)S(1)}, f32[368,256]...) custom-call(s32[2]{0:T(128)S(1)} %pad_add_fusion.1.sides, bf16[720,512]{1,0:T(8,128)(2,1)S(1)} %collective-permute-done.36.refs_0_, ...), custom_call_target="tpu_custom_call" | custom-call | flops 1000 | bytes 1000 | tf_op jit(solution)/shard_map/output_sums/pallas_call | solution.py:292
  156.9 1.8 crossing_sums.3
  158.6 1.7 collective-permute-done.48.refs_0_
  160.8 1.8 collective-permute-done.47
  164.3 2.1 %collective-permute-done.46 = bf16[368,256]{1,0:T(8,128)(2,1)} collective-permute-done((bf16[368,256]{1,0:T(8,128)(2,1)}, bf16[368,256]{1,0:T(8,128)(2,1)}, u32[]{:S(2)}, u32[]{:S(2)}) %collective-permute-start.46) | collective-permute-done | bytes 188448 | tf_op jit(solution)/shard_map/ppermute | solution.py:320
  166.5 3.1 %collective-permute-done.41 = bf16[352,256]{1,0:T(8,128)(2,1)} collective-permute-done((bf16[352,256]{1,0:T(8,128)(2,1)}, bf16[352,256]{1,0:T(8,128)(2,1)}, u32[]{:S(2)}, u32[]{:S(2)}) %collective-permute-start.41) | collective-permute-done | bytes 180256 | tf_op jit(solution)/shard_map/ppermute | solution.py:320
  179.8 1.9 output_sums.5
  185.0 2.1 %collective-permute-start.55 = (bf16[368,256]{1,0:T(8,128)(2,1)S(1)}, bf16[368,256]{1,0:T(8,128)(2,1)S(1)}, u32[]{:S(2)}, u32[]{:S(2)}) collective-permute-start(bf16[368,256]{1,0:T(8,128)(2,1)S(1)} %add_convert_fusion.5), channel_id=1, source_target_pairs={{0,4},{1,5},{2,6},{3,7},{4,0},{5,1},{6,2},{7,3},{8,12},{9,13},{10,... | collective-permute-start | bytes 565256 | tf_op jit(solution)/shard_map/ppermute | solution.py:320
  188.5 2.6 %collective-permute-done.55 = bf16[368,256]{1,0:T(8,128)(2,1)S(1)} collective-permute-done((bf16[368,256]{1,0:T(8,128)(2,1)S(1)}, bf16[368,256]{1,0:T(8,128)(2,1)S(1)}, u32[]{:S(2)}, u32[]{:S(2)}) %collective-permute-start.55) | collective-permute-done | bytes 188448 | tf_op jit(solution)/shard_map/ppermute | solution.py:320
  (225 shorter events, 61.6 us)
Async XLA Ops:
  4.4 14.5 %collective-permute-start.4 = (bf16[960,256]{1,0:T(8,128)(2,1)S(1)}, bf16[960,256]{1,0:T(8,128)(2,1)}, u32[]{:S(2)}, u32[]{:S(2)}) collective-permute-start(bf16[960,256]{1,0:T(8,128)(2,1)S(1)} %get-tuple-element.139), channel_id=1, source_target_pairs={{0,1},{1,0},{2,3},{3,2},{4,5},{5,4},{6,7},{7,6},{8,9},{9,8},{10,11... | collective-permute-start | bytes 1474568 | tf_op jit(solution)/shard_map/ppermute | solution.py:320
  8.8 14.0 %collective-permute-start.1 = (bf16[360,640]{1,0:T(8,128)(2,1)S(1)}, bf16[360,640]{1,0:T(8,128)(2,1)}, u32[]{:S(2)}, u32[]{:S(2)}) collective-permute-start(bf16[360,640]{1,0:T(8,128)(2,1)S(1)} %maximum_select_fusion.3), channel_id=1, source_target_pairs={{0,8},{2,10},{4,12},{6,14},{8,16},{10,18},{12,20},{14,22},{16,24},... | collective-permute-start | bytes 1382408 | tf_op jit(solution)/shard_map/ppermute | solution.py:324
  10.5 52.3 %collective-permute-start.13 = (bf16[2880,256]{1,0:T(8,128)(2,1)S(1)}, bf16[2880,256]{1,0:T(8,128)(2,1)}, u32[]{:S(2)}, u32[]{:S(2)}) collective-permute-start(bf16[2880,256]{1,0:T(8,128)(2,1)S(1)} %bitcast.20), channel_id=1, source_target_pairs={{0,2},{1,3},{2,0},{3,1},{4,6},{5,7},{6,4},{7,5},{8,10},{9,11},{10,... | collective-permute-start | bytes 4423688 | tf_op jit(solution)/shard_map/ppermute | solution.py:320
  22.9 13.8 %collective-permute-start.6 = (bf16[960,256]{1,0:T(8,128)(2,1)}, bf16[960,256]{1,0:T(8,128)(2,1)}, u32[]{:S(2)}, u32[]{:S(2)}) collective-permute-start(bf16[960,256]{1,0:T(8,128)(2,1)} %get-tuple-element.127), channel_id=1, source_target_pairs={{0,1},{1,0},{2,3},{3,2},{4,5},{5,4},{6,7},{7,6},{8,9},{9,8},{10,11... | collective-permute-start | bytes 1474568 | tf_op jit(solution)/shard_map/ppermute | solution.py:320
  23.4 13.3 %collective-permute-start.7 = (bf16[960,256]{1,0:T(8,128)(2,1)}, bf16[960,256]{1,0:T(8,128)(2,1)}, u32[]{:S(2)}, u32[]{:S(2)}) collective-permute-start(bf16[960,256]{1,0:T(8,128)(2,1)} %get-tuple-element.127), channel_id=1, source_target_pairs={{0,4},{1,5},{2,6},{3,7},{4,0},{5,1},{6,2},{7,3},{8,12},{9,13},{10,... | collective-permute-start | bytes 1474568 | tf_op jit(solution)/shard_map/ppermute | solution.py:320
  23.9 12.8 %collective-permute-start.5 = (bf16[360,640]{1,0:T(8,128)(2,1)S(1)}, bf16[360,640]{1,0:T(8,128)(2,1)}, u32[]{:S(2)}, u32[]{:S(2)}) collective-permute-start(bf16[360,640]{1,0:T(8,128)(2,1)S(1)} %maximum_select_fusion.4), channel_id=1, source_target_pairs={{0,8},{2,10},{4,12},{6,14},{8,16},{10,18},{12,20},{14,22},{16,24},... | collective-permute-start | bytes 1382408 | tf_op jit(solution)/shard_map/ppermute | solution.py:324
  36.7 10.8 %collective-permute-start.8 = (bf16[960,256]{1,0:T(8,128)(2,1)}, bf16[960,256]{1,0:T(8,128)(2,1)S(1)}, u32[]{:S(2)}, u32[]{:S(2)}) collective-permute-start(bf16[960,256]{1,0:T(8,128)(2,1)} %get-tuple-element.132), channel_id=1, source_target_pairs={{0,1},{1,0},{2,3},{3,2},{4,5},{5,4},{6,7},{7,6},{8,9},{9,8},{10,11... | collective-permute-start | bytes 1474568 | tf_op jit(solution)/shard_map/ppermute | solution.py:320
  37.9 11.6 %collective-permute-start.9 = (bf16[960,256]{1,0:T(8,128)(2,1)}, bf16[960,256]{1,0:T(8,128)(2,1)S(1)}, u32[]{:S(2)}, u32[]{:S(2)}) collective-permute-start(bf16[960,256]{1,0:T(8,128)(2,1)} %get-tuple-element.132), channel_id=1, source_target_pairs={{0,4},{1,5},{2,6},{3,7},{4,0},{5,1},{6,2},{7,3},{8,12},{9,13},{10,... | collective-permute-start | bytes 1474568 | tf_op jit(solution)/shard_map/ppermute | solution.py:320
  41.2 20.9 %collective-permute-start.10 = (bf16[720,640]{1,0:T(8,128)(2,1)S(1)}, bf16[720,640]{1,0:T(8,128)(2,1)S(1)}, u32[]{:S(2)}, u32[]{:S(2)}) collective-permute-start(bf16[720,640]{1,0:T(8,128)(2,1)S(1)} %maximum_select_fusion.1.refs_21_), channel_id=1, source_target_pairs={{0,8},{2,10},{4,12},{6,14},{8,16},{10,18},{12,20},{14,22},{16,24},... | collective-permute-start | bytes 2764808 | tf_op jit(solution)/shard_map/ppermute | solution.py:324
  49.5 12.6 %collective-permute-start.11 = (bf16[960,256]{1,0:T(8,128)(2,1)S(1)}, bf16[960,256]{1,0:T(8,128)(2,1)S(1)}, u32[]{:S(2)}, u32[]{:S(2)}) collective-permute-start(bf16[960,256]{1,0:T(8,128)(2,1)S(1)} %copy-done.24), channel_id=1, source_target_pairs={{0,4},{1,5},{2,6},{3,7},{4,0},{5,1},{6,2},{7,3},{8,12},{9,13},{10,... | collective-permute-start | bytes 1474568 | tf_op jit(solution)/shard_map/ppermute | solution.py:320
  51.1 11.0 %collective-permute-start.12 = (bf16[960,256]{1,0:T(8,128)(2,1)}, bf16[960,256]{1,0:T(8,128)(2,1)S(1)}, u32[]{:S(2)}, u32[]{:S(2)}) collective-permute-start(bf16[960,256]{1,0:T(8,128)(2,1)} %collective-permute-done.7.refs_9_), channel_id=1, source_target_pairs={{0,1},{1,0},{2,3},{3,2},{4,5},{5,4},{6,7},{7,6},{8,9},{9,8},{10,11... | collective-permute-start | bytes 1474568 | tf_op jit(solution)/shard_map/ppermute | solution.py:320
  51.5 12.4 %collective-permute-start.15 = (bf16[960,256]{1,0:T(8,128)(2,1)}, bf16[960,256]{1,0:T(8,128)(2,1)S(1)}, u32[]{:S(2)}, u32[]{:S(2)}) collective-permute-start(bf16[960,256]{1,0:T(8,128)(2,1)} %collective-permute-done.6.refs_2_), channel_id=1, source_target_pairs={{0,2},{1,3},{2,0},{3,1},{4,6},{5,7},{6,4},{7,5},{8,10},{9,11},{10,... | collective-permute-start | bytes 1474568 | tf_op jit(solution)/shard_map/ppermute | solution.py:320
  62.2 15.1 %collective-permute-start.19 = (bf16[368,640]{1,0:T(8,128)(2,1)S(1)}, bf16[368,640]{1,0:T(8,128)(2,1)}, u32[]{:S(2)}, u32[]{:S(2)}) collective-permute-start(bf16[368,640]{1,0:T(8,128)(2,1)S(1)} %slice.18), channel_id=1, source_target_pairs={{0,8},{2,10},{4,12},{6,14},{8,16},{10,18},{12,20},{14,22},{16,24},... | collective-permute-start | bytes 1413128 | tf_op jit(solution)/shard_map/ppermute | solution.py:324
  62.2 15.1 %collective-permute-start.17 = (bf16[960,256]{1,0:T(8,128)(2,1)}, bf16[960,256]{1,0:T(8,128)(2,1)S(1)}, u32[]{:S(2)}, u32[]{:S(2)}) collective-permute-start(bf16[960,256]{1,0:T(8,128)(2,1)} %collective-permute-done.4.refs_1_), channel_id=1, source_target_pairs={{0,4},{1,5},{2,6},{3,7},{4,0},{5,1},{6,2},{7,3},{8,12},{9,13},{10,... | collective-permute-start | bytes 1474568 | tf_op jit(solution)/shard_map/ppermute | solution.py:320
  62.8 15.0 %collective-permute-start.18 = (bf16[960,256]{1,0:T(8,128)(2,1)S(1)}, bf16[960,256]{1,0:T(8,128)(2,1)S(1)}, u32[]{:S(2)}, u32[]{:S(2)}) collective-permute-start(bf16[960,256]{1,0:T(8,128)(2,1)S(1)} %collective-permute-done.9.refs_10_), channel_id=1, source_target_pairs={{0,1},{1,0},{2,3},{3,2},{4,5},{5,4},{6,7},{7,6},{8,9},{9,8},{10,11... | collective-permute-start | bytes 1474568 | tf_op jit(solution)/shard_map/ppermute | solution.py:320
  63.9 14.1 %collective-permute-start.21 = (bf16[960,256]{1,0:T(8,128)(2,1)}, bf16[960,256]{1,0:T(8,128)(2,1)S(1)}, u32[]{:S(2)}, u32[]{:S(2)}) collective-permute-start(bf16[960,256]{1,0:T(8,128)(2,1)} %collective-permute-done.7.refs_9_), channel_id=1, source_target_pairs={{0,2},{1,3},{2,0},{3,1},{4,6},{5,7},{6,4},{7,5},{8,10},{9,11},{10,... | collective-permute-start | bytes 1474568 | tf_op jit(solution)/shard_map/ppermute | solution.py:320
  63.9 14.5 %collective-permute-start.14 = (bf16[960,256]{1,0:T(8,128)(2,1)}, bf16[960,256]{1,0:T(8,128)(2,1)S(1)}, u32[]{:S(2)}, u32[]{:S(2)}) collective-permute-start(bf16[960,256]{1,0:T(8,128)(2,1)} %collective-permute-done.4.refs_1_), channel_id=1, source_target_pairs={{0,2},{1,3},{2,0},{3,1},{4,6},{5,7},{6,4},{7,5},{8,10},{9,11},{10,... | collective-permute-start | bytes 1474568 | tf_op jit(solution)/shard_map/ppermute | solution.py:320
  78.0 12.6 %collective-permute-start.23 = (bf16[960,256]{1,0:T(8,128)(2,1)S(1)}, bf16[960,256]{1,0:T(8,128)(2,1)S(1)}, u32[]{:S(2)}, u32[]{:S(2)}) collective-permute-start(bf16[960,256]{1,0:T(8,128)(2,1)S(1)} %collective-permute-done.17.refs_11_), channel_id=1, source_target_pairs={{0,2},{1,3},{2,0},{3,1},{4,6},{5,7},{6,4},{7,5},{8,10},{9,11},{10,... | collective-permute-start | bytes 1474568 | tf_op jit(solution)/shard_map/ppermute | solution.py:320
  78.8 11.8 %collective-permute-start.25 = (bf16[960,256]{1,0:T(8,128)(2,1)S(1)}, bf16[960,256]{1,0:T(8,128)(2,1)}, u32[]{:S(2)}, u32[]{:S(2)}) collective-permute-start(bf16[960,256]{1,0:T(8,128)(2,1)S(1)} %collective-permute-done.18.refs_13_), channel_id=1, source_target_pairs={{0,2},{1,3},{2,0},{3,1},{4,6},{5,7},{6,4},{7,5},{8,10},{9,11},{10,... | collective-permute-start | bytes 1474568 | tf_op jit(solution)/shard_map/ppermute | solution.py:320
  79.9 14.2 %collective-permute-start.29 = (bf16[352,640]{1,0:T(8,128)(2,1)S(1)}, bf16[352,640]{1,0:T(8,128)(2,1)S(1)}, u32[]{:S(2)}, u32[]{:S(2)}) collective-permute-start(bf16[352,640]{1,0:T(8,128)(2,1)S(1)} %slice.19), channel_id=1, source_target_pairs={{0,8},{2,10},{4,12},{6,14},{8,16},{10,18},{12,20},{14,22},{16,24},... | collective-permute-start | bytes 1351688 | tf_op jit(solution)/shard_map/ppermute | solution.py:324
  94.9 20.8 %collective-permute-start.31 = (bf16[720,512]{1,0:T(8,128)(2,1)S(1)}, bf16[720,512]{1,0:T(8,128)(2,1)}, u32[]{:S(2)}, u32[]{:S(2)}) collective-permute-start(bf16[720,512]{1,0:T(8,128)(2,1)S(1)} %maximum_select_fusion.2.refs_0_), channel_id=1, source_target_pairs={{0,8},{2,10},{4,12},{6,14},{8,16},{10,18},{12,20},{14,22},{16,24},... | collective-permute-start | bytes 2211848 | tf_op jit(solution)/shard_map/ppermute | solution.py:324
  115.6 24.0 %collective-permute-start.36 = (bf16[720,512]{1,0:T(8,128)(2,1)}, bf16[720,512]{1,0:T(8,128)(2,1)S(1)}, u32[]{:S(2)}, u32[]{:S(2)}) collective-permute-start(bf16[720,512]{1,0:T(8,128)(2,1)} %collective-permute-done.31.refs_1_), channel_id=1, source_target_pairs={{0,8},{2,10},{4,12},{6,14},{8,16},{10,18},{12,20},{14,22},{16,24},... | collective-permute-start | bytes 2211848 | tf_op jit(solution)/shard_map/ppermute | solution.py:324
  128.1 12.0 %collective-permute-start.42 = (bf16[720,256]{1,0:T(8,128)(2,1)S(1)}, bf16[720,256]{1,0:T(8,128)(2,1)S(1)}, u32[]{:S(2)}, u32[]{:S(2)}) collective-permute-start(bf16[720,256]{1,0:T(8,128)(2,1)S(1)} %get-tuple-element.205), channel_id=1, source_target_pairs={{0,1},{1,0},{2,3},{3,2},{4,5},{5,4},{6,7},{7,6},{8,9},{9,8},{10,11... | collective-permute-start | bytes 1105928 | tf_op jit(solution)/shard_map/ppermute | solution.py:320
  129.4 11.8 %collective-permute-start.43 = (bf16[720,256]{1,0:T(8,128)(2,1)S(1)}, bf16[720,256]{1,0:T(8,128)(2,1)S(1)}, u32[]{:S(2)}, u32[]{:S(2)}) collective-permute-start(bf16[720,256]{1,0:T(8,128)(2,1)S(1)} %get-tuple-element.206), channel_id=1, source_target_pairs={{0,4},{1,5},{2,6},{3,7},{4,0},{5,1},{6,2},{7,3},{8,12},{9,13},{10,... | collective-permute-start | bytes 1105928 | tf_op jit(solution)/shard_map/ppermute | solution.py:320
  139.6 12.0 %collective-permute-start.39 = (bf16[720,512]{1,0:T(8,128)(2,1)S(1)}, bf16[720,512]{1,0:T(8,128)(2,1)S(1)}, u32[]{:S(2)}, u32[]{:S(2)}) collective-permute-start(bf16[720,512]{1,0:T(8,128)(2,1)S(1)} %collective-permute-done.36.refs_0_), channel_id=1, source_target_pairs={{0,2},{1,3},{2,0},{3,1},{4,6},{5,7},{6,4},{7,5},{8,10},{9,11},{10,... | collective-permute-start | bytes 2211848 | tf_op jit(solution)/shard_map/ppermute | solution.py:320
  139.6 20.7 %collective-permute-start.48 = (bf16[720,512]{1,0:T(8,128)(2,1)S(1)}, bf16[720,512]{1,0:T(8,128)(2,1)S(1)}, u32[]{:S(2)}, u32[]{:S(2)}) collective-permute-start(bf16[720,512]{1,0:T(8,128)(2,1)S(1)} %collective-permute-done.36.refs_0_), channel_id=1, source_target_pairs={{0,8},{2,10},{4,12},{6,14},{8,16},{10,18},{12,20},{14,22},{16,24},... | collective-permute-start | bytes 2211848 | tf_op jit(solution)/shard_map/ppermute | solution.py:324
  139.6 11.0 %collective-permute-start.37 = (bf16[720,256]{1,0:T(8,128)(2,1)S(1)}, bf16[720,256]{1,0:T(8,128)(2,1)S(1)}, u32[]{:S(2)}, u32[]{:S(2)}) collective-permute-start(bf16[720,256]{1,0:T(8,128)(2,1)S(1)} %get-tuple-element.197), channel_id=1, source_target_pairs={{0,1},{1,0},{2,3},{3,2},{4,5},{5,4},{6,7},{7,6},{8,9},{9,8},{10,11... | collective-permute-start | bytes 1105928 | tf_op jit(solution)/shard_map/ppermute | solution.py:320
  140.1 11.4 %collective-permute-start.38 = (bf16[720,256]{1,0:T(8,128)(2,1)S(1)}, bf16[720,256]{1,0:T(8,128)(2,1)S(1)}, u32[]{:S(2)}, u32[]{:S(2)}) collective-permute-start(bf16[720,256]{1,0:T(8,128)(2,1)S(1)} %get-tuple-element.198), channel_id=1, source_target_pairs={{0,4},{1,5},{2,6},{3,7},{4,0},{5,1},{6,2},{7,3},{8,12},{9,13},{10,... | collective-permute-start | bytes 1105928 | tf_op jit(solution)/shard_map/ppermute | solution.py:320
  142.0 24.4 %collective-permute-start.45 = (bf16[720,256]{1,0:T(8,128)(2,1)}, bf16[720,256]{1,0:T(8,128)(2,1)}, u32[]{:S(2)}, u32[]{:S(2)}) collective-permute-start(bf16[720,256]{1,0:T(8,128)(2,1)} %add_convert_fusion.2), channel_id=1, source_target_pairs={{0,4},{1,5},{2,6},{3,7},{4,0},{5,1},{6,2},{7,3},{8,12},{9,13},{10,... | collective-permute-start | bytes 1105928 | tf_op jit(solution)/shard_map/ppermute | solution.py:320
  150.6 15.9 %collective-permute-start.44 = (bf16[720,256]{1,0:T(8,128)(2,1)}, bf16[720,256]{1,0:T(8,128)(2,1)}, u32[]{:S(2)}, u32[]{:S(2)}) collective-permute-start(bf16[720,256]{1,0:T(8,128)(2,1)} %add_convert_fusion.3), channel_id=1, source_target_pairs={{0,1},{1,0},{2,3},{3,2},{4,5},{5,4},{6,7},{7,6},{8,9},{9,8},{10,11... | collective-permute-start | bytes 1105928 | tf_op jit(solution)/shard_map/ppermute | solution.py:320
  155.9 10.6 %collective-permute-start.46 = (bf16[368,256]{1,0:T(8,128)(2,1)}, bf16[368,256]{1,0:T(8,128)(2,1)}, u32[]{:S(2)}, u32[]{:S(2)}) collective-permute-start(bf16[368,256]{1,0:T(8,128)(2,1)} %get-tuple-element.215), channel_id=1, source_target_pairs={{0,1},{1,0},{2,3},{3,2},{4,5},{5,4},{6,7},{7,6},{8,9},{9,8},{10,11... | collective-permute-start | bytes 565256 | tf_op jit(solution)/shard_map/ppermute | solution.py:320
  170.8 13.0 %collective-permute-start.53 = (bf16[368,256]{1,0:T(8,128)(2,1)S(1)}, bf16[368,256]{1,0:T(8,128)(2,1)S(1)}, u32[]{:S(2)}, u32[]{:S(2)}) collective-permute-start(bf16[368,256]{1,0:T(8,128)(2,1)S(1)} %add_convert_fusion.7), channel_id=1, source_target_pairs={{0,4},{1,5},{2,6},{3,7},{4,0},{5,1},{6,2},{7,3},{8,12},{9,13},{10,... | collective-permute-start | bytes 565256 | tf_op jit(solution)/shard_map/ppermute | solution.py:320
  (74 other events, 650.8 us)

commit v5 on v4

--- a/solution.py
+++ b/solution.py
@@ -14,7 +14,7 @@
 
 rope_base = 150000.0
 vmem_bytes = 48 * 1024 * 1024
-wide_vmem_bytes = 62 * 1024 * 1024
+wide_vmem_bytes = 60 * 1024 * 1024
 log2e = math.log2(math.e)
 small_cost = pl.CostEstimate(flops=1000, bytes_accessed=1000, transcendentals=0)
 score_scale = HEAD_WIDTH**-0.5 * log2e

time: 193 us -> 192 us (level)
    unnamed x96 -> x100, local copies, waits for them, and re-layouts: 7.52 us -> 8.07 us
  transfers between devices with their start and end apart: 58 -> 58, of which waited for: 27 -> 28; matrix products, arithmetic and copies ran while one was open for 8% -> 8% of each run, Pallas kernels for 18% -> 18%
where the time goes in v5:
time: 192 us; the launch traced here: 191 us
  waiting for transfers between devices  89.2 us (46%)
  starting transfers between devices  40 us (21%)
  Pallas kernels  34.9 us (18%)
  other arithmetic  14.6 us (8%)
  local copies, waits for them, and re-layouts  12 us (6%)
    ppermute x8, waiting for transfers between devices, turn(): return lax.ppermute(value, 'seq', pairs)  44 us
    ppermute x49, waiting for transfers between devices, swap(): return lax.ppermute(value, both, pairs)  43.7 us
    ppermute x49, starting transfers between devices, swap(): return lax.ppermute(value, both, pairs)  34.4 us
    pallas_call x1, Pallas kernels, project(): pl.pallas_call(functools.partial(project_kernel, cuts=cuts), in_specs=[pl...  17.3 us
    pallas_call x6, Pallas kernels, output_sums(): pl.pallas_call(functools.partial(sums_kernel, count=len(w_near), crossing...  14 us
    unnamed x100, local copies, waits for them, and re-layouts  8.07 us
    ppermute x8, starting transfers between devices, turn(): return lax.ppermute(value, 'seq', pairs)  4.02 us
  transfers between devices with their start and end apart: 58, of which 28 were waited for; matrix products, arithmetic and copies ran while one was open for 8% of the time, Pallas kernels for 18%

profile of v5, /device:TPU:0, one launch (start us, length us, event | category | flops | bytes accessed | tf_op | source)
XLA Modules:
  0.0 191.5 jit_solution(5251705642881013121)
XLA Ops:
  4.4 2.9 %collective-permute-start.4 = (bf16[960,256]{1,0:T(8,128)(2,1)S(1)}, bf16[960,256]{1,0:T(8,128)(2,1)}, u32[]{:S(2)}, u32[]{:S(2)}) collective-permute-start(bf16[960,256]{1,0:T(8,128)(2,1)S(1)} %get-tuple-element.139), channel_id=1, source_target_pairs={{0,1},{1,0},{2,3},{3,2},{4,5},{5,4},{6,7},{7,6},{8,9},{9,8},{10,11... | collective-permute-start | bytes 1474568 | tf_op jit(solution)/shard_map/ppermute | solution.py:320
  7.3 1.6 collective-permute-start.2
  11.1 4.8 %collective-permute-done.2 = bf16[180,640]{1,0:T(8,128)(2,1)S(1)} collective-permute-done((bf16[180,640]{1,0:T(8,128)(2,1)S(1)}, bf16[180,640]{1,0:T(8,128)(2,1)S(1)}, u32[]{:S(2)}, u32[]{:S(2)}) %collective-permute-start.2) | collective-permute-done | bytes 230432 | tf_op jit(solution)/shard_map/ppermute | solution.py:320
  15.9 3.0 %collective-permute-done.3 = bf16[180,640]{1,0:T(8,128)(2,1)S(1)} collective-permute-done((bf16[180,640]{1,0:T(8,128)(2,1)S(1)}, bf16[180,640]{1,0:T(8,128)(2,1)S(1)}, u32[]{:S(2)}, u32[]{:S(2)}) %collective-permute-start.3) | collective-permute-done | bytes 230432 | tf_op jit(solution)/shard_map/ppermute | solution.py:320
  19.1 3.8 %collective-permute-done.1 = bf16[360,640]{1,0:T(8,128)(2,1)} collective-permute-done((bf16[360,640]{1,0:T(8,128)(2,1)S(1)}, bf16[360,640]{1,0:T(8,128)(2,1)}, u32[]{:S(2)}, u32[]{:S(2)}) %collective-permute-start.1) | collective-permute-done | bytes 460832 | tf_op jit(solution)/shard_map/ppermute | solution.py:324
  26.7 10.0 %collective-permute-done.5 = bf16[360,640]{1,0:T(8,128)(2,1)} collective-permute-done((bf16[360,640]{1,0:T(8,128)(2,1)S(1)}, bf16[360,640]{1,0:T(8,128)(2,1)}, u32[]{:S(2)}, u32[]{:S(2)}) %collective-permute-start.5) | collective-permute-done | bytes 460832 | tf_op jit(solution)/shard_map/ppermute | solution.py:324
  39.5 1.7 maximum_select_fusion.1.refs_21_
  41.3 1.8 multiply_sine_fusion
  44.3 3.2 %collective-permute-done.8.refs_3_ = bf16[960,256]{1,0:T(8,128)(2,1)S(1)} collective-permute-done((bf16[960,256]{1,0:T(8,128)(2,1)}, bf16[960,256]{1,0:T(8,128)(2,1)S(1)}, u32[]{:S(2)}, u32[]{:S(2)}) %collective-permute-start.8) | collective-permute-done | bytes 491552 | tf_op jit(solution)/shard_map/ppermute | solution.py:320
  47.5 2.0 %collective-permute-done.9.refs_10_ = bf16[960,256]{1,0:T(8,128)(2,1)S(1)} collective-permute-done((bf16[960,256]{1,0:T(8,128)(2,1)}, bf16[960,256]{1,0:T(8,128)(2,1)S(1)}, u32[]{:S(2)}, u32[]{:S(2)}) %collective-permute-start.9) | collective-permute-done | bytes 491552 | tf_op jit(solution)/shard_map/ppermute | solution.py:320
  51.5 10.6 %collective-permute-done.10.refs_22_ = bf16[720,640]{1,0:T(8,128)(2,1)S(1)} collective-permute-done((bf16[720,640]{1,0:T(8,128)(2,1)S(1)}, bf16[720,640]{1,0:T(8,128)(2,1)S(1)}, u32[]{:S(2)}, u32[]{:S(2)}) %collective-permute-start.10) | collective-permute-done | bytes 921632 | tf_op jit(solution)/shard_map/ppermute | solution.py:324
  64.4 12.8 %collective-permute-done.19.refs_23_ = bf16[368,640]{1,0:T(8,128)(2,1)S(1)} collective-permute-done((bf16[368,640]{1,0:T(8,128)(2,1)S(1)}, bf16[368,640]{1,0:T(8,128)(2,1)S(1)}, u32[]{:S(2)}, u32[]{:S(2)}) %collective-permute-start.19) | collective-permute-done | bytes 471072 | tf_op jit(solution)/shard_map/ppermute | solution.py:324
  82.5 5.5 %collective-permute-done.26 = bf16[180,512]{1,0:T(8,128)(2,1)S(1)} collective-permute-done((bf16[180,512]{1,0:T(8,128)(2,1)S(1)}, bf16[180,512]{1,0:T(8,128)(2,1)S(1)}, u32[]{:S(2)}, u32[]{:S(2)}) %collective-permute-start.26) | collective-permute-done | bytes 184352 | tf_op jit(solution)/shard_map/ppermute | solution.py:320
  88.1 2.4 %collective-permute-done.27 = bf16[180,512]{1,0:T(8,128)(2,1)S(1)} collective-permute-done((bf16[180,512]{1,0:T(8,128)(2,1)S(1)}, bf16[180,512]{1,0:T(8,128)(2,1)S(1)}, u32[]{:S(2)}, u32[]{:S(2)}) %collective-permute-start.27) | collective-permute-done | bytes 184352 | tf_op jit(solution)/shard_map/ppermute | solution.py:320
  94.8 17.3 %project.1 = (bf16[128,1024]{1,0:T(8,128)(2,1)}, bf16[4,512,256]{2,1,0:T(8,128)(2,1)}, bf16[128,128]{1,0:T(8,128)(2,1)}, bf16[2,512,256]{2,1,0:T(8,128)(2,1)}, bf16[2,512,256]{2,1,0:T(8,128)(2,1)}) custom-call(s32[4]{0:T(128)} %pad_add_fusion.zs, s32[8]{0:T(128)} %stack.73.order, s32[2]{0:T(128)} %pad_add_fusion.2.first, f32[8]{0:T(128)} %dynamic_slice.47.sinks, ...), custom_call_target="tpu_custom_call" | custom-call | flops 1000 | bytes 1000 | tf_op jit(solution)/shard_map/project/pallas_call | solution.py:215
  112.1 1.6 collective-permute-start.30
  115.6 2.3 %collective-permute-start.36 = (bf16[720,512]{1,0:T(8,128)(2,1)}, bf16[720,512]{1,0:T(8,128)(2,1)S(1)}, u32[]{:S(2)}, u32[]{:S(2)}) collective-permute-start(bf16[720,512]{1,0:T(8,128)(2,1)} %collective-permute-done.31.refs_1_), channel_id=1, source_target_pairs={{0,8},{2,10},{4,12},{6,14},{8,16},{10,18},{12,20},{14,22},{16,24},... | collective-permute-start | bytes 2211848 | tf_op jit(solution)/shard_map/ppermute | solution.py:324
  120.3 3.5 %attend.1 = (bf16[2,512,256]{2,1,0:T(8,128)(2,1)S(1)}, bf16[2,512,256]{2,1,0:T(8,128)(2,1)S(1)}) custom-call(s32[2]{0:T(128)S(1)} %copy-done.15, f32[8]{0:T(128)S(1)} %copy-done.14, bf16[4,512,256]{2,1,0:T(8,128)(2,1)S(1)} %copy-done.4, bf16[128,1024]{1,0:T(8,128)(2,1)S(1)} %copy-done.13, bf16[128,128]{1,0:T(8,128)(2,1)S(1)} %collective-permute-done.30.refs_0_), custom_call_target="tpu_custom_call" | custom-call | flops 1000 | bytes 1000 | tf_op jit(solution)/shard_map/attend/pallas_call | solution.py:132
  124.2 1.6 collective-permute-done.34.refs_6_.refs_4_
  125.8 2.3 %crossing_sums.4 = (bf16[720,256]{1,0:T(8,128)(2,1)S(1)}, bf16[720,256]{1,0:T(8,128)(2,1)S(1)}) custom-call(s32[2]{0:T(128)S(1)} %pad_add_fusion.1.sides, bf16[720,512]{1,0:T(8,128)(2,1)S(1)} %maximum_select_fusion.2.refs_0_, bf16[720,512]{1,0:T(8,128)(2,1)} %collective-permute-done.31.refs_1_, bf16[720,512]{1,0:T(8,128)(2,1)S(1)} %collective-permute-done.32.refs_2_, ...), custom_call_target="tpu_custom_call" | custom-call | flops 1000 | bytes 1000 | tf_op jit(solution)/shard_map/crossing_sums/pallas_call | solution.py:292
  129.8 4.2 %output_sums.3 = (f32[720,256]{1,0:T(8,128)S(1)}, f32[720,256]{1,0:T(8,128)S(1)}, bf16[720,256]{1,0:T(8,128)(2,1)S(1)}, f32[720,256]{1,0:T(8,128)S(1)}, f32[720,...) custom-call(s32[2]{0:T(128)S(1)} %pad_add_fusion.1.sides, bf16[720,512]{1,0:T(8,128)(2,1)} %copy-done.1, ...), custom_call_target="tpu_custom_call" | custom-call | flops 1000 | bytes 1000 | tf_op jit(solution)/shard_map/output_sums/pallas_call | solution.py:292
  135.0 3.7 %collective-permute-done.36.refs_0_ = bf16[720,512]{1,0:T(8,128)(2,1)S(1)} collective-permute-done((bf16[720,512]{1,0:T(8,128)(2,1)}, bf16[720,512]{1,0:T(8,128)(2,1)S(1)}, u32[]{:S(2)}, u32[]{:S(2)}) %collective-permute-start.36) | collective-permute-done | bytes 737312 | tf_op jit(solution)/shard_map/ppermute | solution.py:324
  142.9 6.7 %collective-permute-done.37 = bf16[720,256]{1,0:T(8,128)(2,1)S(1)} collective-permute-done((bf16[720,256]{1,0:T(8,128)(2,1)S(1)}, bf16[720,256]{1,0:T(8,128)(2,1)S(1)}, u32[]{:S(2)}, u32[]{:S(2)}) %collective-permute-start.37) | collective-permute-done | bytes 368672 | tf_op jit(solution)/shard_map/ppermute | solution.py:320
  150.6 2.5 %output_sums.4 = (f32[368,256]{1,0:T(8,128)S(1)}, f32[352,256]{1,0:T(8,128)S(1)}, bf16[368,256]{1,0:T(8,128)(2,1)}, f32[352,256]{1,0:T(8,128)S(1)}, f32[368,256]...) custom-call(s32[2]{0:T(128)S(1)} %pad_add_fusion.1.sides, bf16[720,512]{1,0:T(8,128)(2,1)S(1)} %collective-permute-done.36.refs_0_, ...), custom_call_target="tpu_custom_call" | custom-call | flops 1000 | bytes 1000 | tf_op jit(solution)/shard_map/output_sums/pallas_call | solution.py:292
  156.0 1.7 crossing_sums.3
  157.7 1.7 collective-permute-done.48.refs_0_
  159.9 1.8 collective-permute-done.47
  163.4 2.2 %collective-permute-done.46 = bf16[368,256]{1,0:T(8,128)(2,1)} collective-permute-done((bf16[368,256]{1,0:T(8,128)(2,1)}, bf16[368,256]{1,0:T(8,128)(2,1)}, u32[]{:S(2)}, u32[]{:S(2)}) %collective-permute-start.46) | collective-permute-done | bytes 188448 | tf_op jit(solution)/shard_map/ppermute | solution.py:320
  165.6 3.1 %collective-permute-done.41 = bf16[352,256]{1,0:T(8,128)(2,1)} collective-permute-done((bf16[352,256]{1,0:T(8,128)(2,1)}, bf16[352,256]{1,0:T(8,128)(2,1)}, u32[]{:S(2)}, u32[]{:S(2)}) %collective-permute-start.41) | collective-permute-done | bytes 180256 | tf_op jit(solution)/shard_map/ppermute | solution.py:320
  178.9 1.9 output_sums.5
  184.1 2.1 %collective-permute-start.55 = (bf16[368,256]{1,0:T(8,128)(2,1)S(1)}, bf16[368,256]{1,0:T(8,128)(2,1)S(1)}, u32[]{:S(2)}, u32[]{:S(2)}) collective-permute-start(bf16[368,256]{1,0:T(8,128)(2,1)S(1)} %add_convert_fusion.5), channel_id=1, source_target_pairs={{0,4},{1,5},{2,6},{3,7},{4,0},{5,1},{6,2},{7,3},{8,12},{9,13},{10,... | collective-permute-start | bytes 565256 | tf_op jit(solution)/shard_map/ppermute | solution.py:320
  187.6 2.6 %collective-permute-done.55 = bf16[368,256]{1,0:T(8,128)(2,1)S(1)} collective-permute-done((bf16[368,256]{1,0:T(8,128)(2,1)S(1)}, bf16[368,256]{1,0:T(8,128)(2,1)S(1)}, u32[]{:S(2)}, u32[]{:S(2)}) %collective-permute-start.55) | collective-permute-done | bytes 188448 | tf_op jit(solution)/shard_map/ppermute | solution.py:320
  (229 shorter events, 61.8 us)
Async XLA Ops:
  4.4 14.5 %collective-permute-start.4 = (bf16[960,256]{1,0:T(8,128)(2,1)S(1)}, bf16[960,256]{1,0:T(8,128)(2,1)}, u32[]{:S(2)}, u32[]{:S(2)}) collective-permute-start(bf16[960,256]{1,0:T(8,128)(2,1)S(1)} %get-tuple-element.139), channel_id=1, source_target_pairs={{0,1},{1,0},{2,3},{3,2},{4,5},{5,4},{6,7},{7,6},{8,9},{9,8},{10,11... | collective-permute-start | bytes 1474568 | tf_op jit(solution)/shard_map/ppermute | solution.py:320
  8.8 14.0 %collective-permute-start.1 = (bf16[360,640]{1,0:T(8,128)(2,1)S(1)}, bf16[360,640]{1,0:T(8,128)(2,1)}, u32[]{:S(2)}, u32[]{:S(2)}) collective-permute-start(bf16[360,640]{1,0:T(8,128)(2,1)S(1)} %maximum_select_fusion.3), channel_id=1, source_target_pairs={{0,8},{2,10},{4,12},{6,14},{8,16},{10,18},{12,20},{14,22},{16,24},... | collective-permute-start | bytes 1382408 | tf_op jit(solution)/shard_map/ppermute | solution.py:324
  10.5 52.3 %collective-permute-start.13 = (bf16[2880,256]{1,0:T(8,128)(2,1)S(1)}, bf16[2880,256]{1,0:T(8,128)(2,1)}, u32[]{:S(2)}, u32[]{:S(2)}) collective-permute-start(bf16[2880,256]{1,0:T(8,128)(2,1)S(1)} %bitcast.20), channel_id=1, source_target_pairs={{0,2},{1,3},{2,0},{3,1},{4,6},{5,7},{6,4},{7,5},{8,10},{9,11},{10,... | collective-permute-start | bytes 4423688 | tf_op jit(solution)/shard_map/ppermute | solution.py:320
  22.8 13.8 %collective-permute-start.6 = (bf16[960,256]{1,0:T(8,128)(2,1)}, bf16[960,256]{1,0:T(8,128)(2,1)}, u32[]{:S(2)}, u32[]{:S(2)}) collective-permute-start(bf16[960,256]{1,0:T(8,128)(2,1)} %get-tuple-element.127), channel_id=1, source_target_pairs={{0,1},{1,0},{2,3},{3,2},{4,5},{5,4},{6,7},{7,6},{8,9},{9,8},{10,11... | collective-permute-start | bytes 1474568 | tf_op jit(solution)/shard_map/ppermute | solution.py:320
  23.4 13.3 %collective-permute-start.7 = (bf16[960,256]{1,0:T(8,128)(2,1)}, bf16[960,256]{1,0:T(8,128)(2,1)}, u32[]{:S(2)}, u32[]{:S(2)}) collective-permute-start(bf16[960,256]{1,0:T(8,128)(2,1)} %get-tuple-element.127), channel_id=1, source_target_pairs={{0,4},{1,5},{2,6},{3,7},{4,0},{5,1},{6,2},{7,3},{8,12},{9,13},{10,... | collective-permute-start | bytes 1474568 | tf_op jit(solution)/shard_map/ppermute | solution.py:320
  23.9 12.8 %collective-permute-start.5 = (bf16[360,640]{1,0:T(8,128)(2,1)S(1)}, bf16[360,640]{1,0:T(8,128)(2,1)}, u32[]{:S(2)}, u32[]{:S(2)}) collective-permute-start(bf16[360,640]{1,0:T(8,128)(2,1)S(1)} %maximum_select_fusion.4), channel_id=1, source_target_pairs={{0,8},{2,10},{4,12},{6,14},{8,16},{10,18},{12,20},{14,22},{16,24},... | collective-permute-start | bytes 1382408 | tf_op jit(solution)/shard_map/ppermute | solution.py:324
  36.7 10.8 %collective-permute-start.8 = (bf16[960,256]{1,0:T(8,128)(2,1)}, bf16[960,256]{1,0:T(8,128)(2,1)S(1)}, u32[]{:S(2)}, u32[]{:S(2)}) collective-permute-start(bf16[960,256]{1,0:T(8,128)(2,1)} %get-tuple-element.132), channel_id=1, source_target_pairs={{0,1},{1,0},{2,3},{3,2},{4,5},{5,4},{6,7},{7,6},{8,9},{9,8},{10,11... | collective-permute-start | bytes 1474568 | tf_op jit(solution)/shard_map/ppermute | solution.py:320
  37.9 11.6 %collective-permute-start.9 = (bf16[960,256]{1,0:T(8,128)(2,1)}, bf16[960,256]{1,0:T(8,128)(2,1)S(1)}, u32[]{:S(2)}, u32[]{:S(2)}) collective-permute-start(bf16[960,256]{1,0:T(8,128)(2,1)} %get-tuple-element.132), channel_id=1, source_target_pairs={{0,4},{1,5},{2,6},{3,7},{4,0},{5,1},{6,2},{7,3},{8,12},{9,13},{10,... | collective-permute-start | bytes 1474568 | tf_op jit(solution)/shard_map/ppermute | solution.py:320
  41.2 20.9 %collective-permute-start.10 = (bf16[720,640]{1,0:T(8,128)(2,1)S(1)}, bf16[720,640]{1,0:T(8,128)(2,1)S(1)}, u32[]{:S(2)}, u32[]{:S(2)}) collective-permute-start(bf16[720,640]{1,0:T(8,128)(2,1)S(1)} %maximum_select_fusion.1.refs_21_), channel_id=1, source_target_pairs={{0,8},{2,10},{4,12},{6,14},{8,16},{10,18},{12,20},{14,22},{16,24},... | collective-permute-start | bytes 2764808 | tf_op jit(solution)/shard_map/ppermute | solution.py:324
  49.5 12.6 %collective-permute-start.11 = (bf16[960,256]{1,0:T(8,128)(2,1)S(1)}, bf16[960,256]{1,0:T(8,128)(2,1)S(1)}, u32[]{:S(2)}, u32[]{:S(2)}) collective-permute-start(bf16[960,256]{1,0:T(8,128)(2,1)S(1)} %copy-done.24), channel_id=1, source_target_pairs={{0,4},{1,5},{2,6},{3,7},{4,0},{5,1},{6,2},{7,3},{8,12},{9,13},{10,... | collective-permute-start | bytes 1474568 | tf_op jit(solution)/shard_map/ppermute | solution.py:320
  51.1 11.0 %collective-permute-start.12 = (bf16[960,256]{1,0:T(8,128)(2,1)}, bf16[960,256]{1,0:T(8,128)(2,1)S(1)}, u32[]{:S(2)}, u32[]{:S(2)}) collective-permute-start(bf16[960,256]{1,0:T(8,128)(2,1)} %collective-permute-done.7.refs_9_), channel_id=1, source_target_pairs={{0,1},{1,0},{2,3},{3,2},{4,5},{5,4},{6,7},{7,6},{8,9},{9,8},{10,11... | collective-permute-start | bytes 1474568 | tf_op jit(solution)/shard_map/ppermute | solution.py:320
  51.5 12.4 %collective-permute-start.15 = (bf16[960,256]{1,0:T(8,128)(2,1)}, bf16[960,256]{1,0:T(8,128)(2,1)S(1)}, u32[]{:S(2)}, u32[]{:S(2)}) collective-permute-start(bf16[960,256]{1,0:T(8,128)(2,1)} %collective-permute-done.6.refs_2_), channel_id=1, source_target_pairs={{0,2},{1,3},{2,0},{3,1},{4,6},{5,7},{6,4},{7,5},{8,10},{9,11},{10,... | collective-permute-start | bytes 1474568 | tf_op jit(solution)/shard_map/ppermute | solution.py:320
  62.2 15.0 %collective-permute-start.19 = (bf16[368,640]{1,0:T(8,128)(2,1)S(1)}, bf16[368,640]{1,0:T(8,128)(2,1)S(1)}, u32[]{:S(2)}, u32[]{:S(2)}) collective-permute-start(bf16[368,640]{1,0:T(8,128)(2,1)S(1)} %slice.18), channel_id=1, source_target_pairs={{0,8},{2,10},{4,12},{6,14},{8,16},{10,18},{12,20},{14,22},{16,24},... | collective-permute-start | bytes 1413128 | tf_op jit(solution)/shard_map/ppermute | solution.py:324
  62.2 15.0 %collective-permute-start.17 = (bf16[960,256]{1,0:T(8,128)(2,1)}, bf16[960,256]{1,0:T(8,128)(2,1)S(1)}, u32[]{:S(2)}, u32[]{:S(2)}) collective-permute-start(bf16[960,256]{1,0:T(8,128)(2,1)} %collective-permute-done.4.refs_1_), channel_id=1, source_target_pairs={{0,4},{1,5},{2,6},{3,7},{4,0},{5,1},{6,2},{7,3},{8,12},{9,13},{10,... | collective-permute-start | bytes 1474568 | tf_op jit(solution)/shard_map/ppermute | solution.py:320
  62.8 14.9 %collective-permute-start.18 = (bf16[960,256]{1,0:T(8,128)(2,1)S(1)}, bf16[960,256]{1,0:T(8,128)(2,1)S(1)}, u32[]{:S(2)}, u32[]{:S(2)}) collective-permute-start(bf16[960,256]{1,0:T(8,128)(2,1)S(1)} %collective-permute-done.9.refs_10_), channel_id=1, source_target_pairs={{0,1},{1,0},{2,3},{3,2},{4,5},{5,4},{6,7},{7,6},{8,9},{9,8},{10,11... | collective-permute-start | bytes 1474568 | tf_op jit(solution)/shard_map/ppermute | solution.py:320
  63.9 14.0 %collective-permute-start.21 = (bf16[960,256]{1,0:T(8,128)(2,1)}, bf16[960,256]{1,0:T(8,128)(2,1)S(1)}, u32[]{:S(2)}, u32[]{:S(2)}) collective-permute-start(bf16[960,256]{1,0:T(8,128)(2,1)} %collective-permute-done.7.refs_9_), channel_id=1, source_target_pairs={{0,2},{1,3},{2,0},{3,1},{4,6},{5,7},{6,4},{7,5},{8,10},{9,11},{10,... | collective-permute-start | bytes 1474568 | tf_op jit(solution)/shard_map/ppermute | solution.py:320
  63.9 14.4 %collective-permute-start.14 = (bf16[960,256]{1,0:T(8,128)(2,1)}, bf16[960,256]{1,0:T(8,128)(2,1)S(1)}, u32[]{:S(2)}, u32[]{:S(2)}) collective-permute-start(bf16[960,256]{1,0:T(8,128)(2,1)} %collective-permute-done.4.refs_1_), channel_id=1, source_target_pairs={{0,2},{1,3},{2,0},{3,1},{4,6},{5,7},{6,4},{7,5},{8,10},{9,11},{10,... | collective-permute-start | bytes 1474568 | tf_op jit(solution)/shard_map/ppermute | solution.py:320
  77.9 12.6 %collective-permute-start.23 = (bf16[960,256]{1,0:T(8,128)(2,1)S(1)}, bf16[960,256]{1,0:T(8,128)(2,1)S(1)}, u32[]{:S(2)}, u32[]{:S(2)}) collective-permute-start(bf16[960,256]{1,0:T(8,128)(2,1)S(1)} %collective-permute-done.17.refs_11_), channel_id=1, source_target_pairs={{0,2},{1,3},{2,0},{3,1},{4,6},{5,7},{6,4},{7,5},{8,10},{9,11},{10,... | collective-permute-start | bytes 1474568 | tf_op jit(solution)/shard_map/ppermute | solution.py:320
  78.4 12.1 %collective-permute-start.25 = (bf16[960,256]{1,0:T(8,128)(2,1)S(1)}, bf16[960,256]{1,0:T(8,128)(2,1)S(1)}, u32[]{:S(2)}, u32[]{:S(2)}) collective-permute-start(bf16[960,256]{1,0:T(8,128)(2,1)S(1)} %collective-permute-done.18.refs_13_), channel_id=1, source_target_pairs={{0,2},{1,3},{2,0},{3,1},{4,6},{5,7},{6,4},{7,5},{8,10},{9,11},{10,... | collective-permute-start | bytes 1474568 | tf_op jit(solution)/shard_map/ppermute | solution.py:320
  79.8 14.2 %collective-permute-start.29 = (bf16[352,640]{1,0:T(8,128)(2,1)S(1)}, bf16[352,640]{1,0:T(8,128)(2,1)S(1)}, u32[]{:S(2)}, u32[]{:S(2)}) collective-permute-start(bf16[352,640]{1,0:T(8,128)(2,1)S(1)} %slice.19), channel_id=1, source_target_pairs={{0,8},{2,10},{4,12},{6,14},{8,16},{10,18},{12,20},{14,22},{16,24},... | collective-permute-start | bytes 1351688 | tf_op jit(solution)/shard_map/ppermute | solution.py:324
  94.0 21.7 %collective-permute-start.31 = (bf16[720,512]{1,0:T(8,128)(2,1)S(1)}, bf16[720,512]{1,0:T(8,128)(2,1)}, u32[]{:S(2)}, u32[]{:S(2)}) collective-permute-start(bf16[720,512]{1,0:T(8,128)(2,1)S(1)} %maximum_select_fusion.2.refs_0_), channel_id=1, source_target_pairs={{0,8},{2,10},{4,12},{6,14},{8,16},{10,18},{12,20},{14,22},{16,24},... | collective-permute-start | bytes 2211848 | tf_op jit(solution)/shard_map/ppermute | solution.py:324
  115.6 23.0 %collective-permute-start.36 = (bf16[720,512]{1,0:T(8,128)(2,1)}, bf16[720,512]{1,0:T(8,128)(2,1)S(1)}, u32[]{:S(2)}, u32[]{:S(2)}) collective-permute-start(bf16[720,512]{1,0:T(8,128)(2,1)} %collective-permute-done.31.refs_1_), channel_id=1, source_target_pairs={{0,8},{2,10},{4,12},{6,14},{8,16},{10,18},{12,20},{14,22},{16,24},... | collective-permute-start | bytes 2211848 | tf_op jit(solution)/shard_map/ppermute | solution.py:324
  128.2 11.0 %collective-permute-start.42 = (bf16[720,256]{1,0:T(8,128)(2,1)S(1)}, bf16[720,256]{1,0:T(8,128)(2,1)S(1)}, u32[]{:S(2)}, u32[]{:S(2)}) collective-permute-start(bf16[720,256]{1,0:T(8,128)(2,1)S(1)} %get-tuple-element.205), channel_id=1, source_target_pairs={{0,1},{1,0},{2,3},{3,2},{4,5},{5,4},{6,7},{7,6},{8,9},{9,8},{10,11... | collective-permute-start | bytes 1105928 | tf_op jit(solution)/shard_map/ppermute | solution.py:320
  128.8 11.4 %collective-permute-start.43 = (bf16[720,256]{1,0:T(8,128)(2,1)S(1)}, bf16[720,256]{1,0:T(8,128)(2,1)S(1)}, u32[]{:S(2)}, u32[]{:S(2)}) collective-permute-start(bf16[720,256]{1,0:T(8,128)(2,1)S(1)} %get-tuple-element.206), channel_id=1, source_target_pairs={{0,4},{1,5},{2,6},{3,7},{4,0},{5,1},{6,2},{7,3},{8,12},{9,13},{10,... | collective-permute-start | bytes 1105928 | tf_op jit(solution)/shard_map/ppermute | solution.py:320
  138.7 12.0 %collective-permute-start.39 = (bf16[720,512]{1,0:T(8,128)(2,1)S(1)}, bf16[720,512]{1,0:T(8,128)(2,1)S(1)}, u32[]{:S(2)}, u32[]{:S(2)}) collective-permute-start(bf16[720,512]{1,0:T(8,128)(2,1)S(1)} %collective-permute-done.36.refs_0_), channel_id=1, source_target_pairs={{0,2},{1,3},{2,0},{3,1},{4,6},{5,7},{6,4},{7,5},{8,10},{9,11},{10,... | collective-permute-start | bytes 2211848 | tf_op jit(solution)/shard_map/ppermute | solution.py:320
  138.7 20.7 %collective-permute-start.48 = (bf16[720,512]{1,0:T(8,128)(2,1)S(1)}, bf16[720,512]{1,0:T(8,128)(2,1)S(1)}, u32[]{:S(2)}, u32[]{:S(2)}) collective-permute-start(bf16[720,512]{1,0:T(8,128)(2,1)S(1)} %collective-permute-done.36.refs_0_), channel_id=1, source_target_pairs={{0,8},{2,10},{4,12},{6,14},{8,16},{10,18},{12,20},{14,22},{16,24},... | collective-permute-start | bytes 2211848 | tf_op jit(solution)/shard_map/ppermute | solution.py:324
  138.7 11.0 %collective-permute-start.37 = (bf16[720,256]{1,0:T(8,128)(2,1)S(1)}, bf16[720,256]{1,0:T(8,128)(2,1)S(1)}, u32[]{:S(2)}, u32[]{:S(2)}) collective-permute-start(bf16[720,256]{1,0:T(8,128)(2,1)S(1)} %get-tuple-element.197), channel_id=1, source_target_pairs={{0,1},{1,0},{2,3},{3,2},{4,5},{5,4},{6,7},{7,6},{8,9},{9,8},{10,11... | collective-permute-start | bytes 1105928 | tf_op jit(solution)/shard_map/ppermute | solution.py:320
  139.2 11.4 %collective-permute-start.38 = (bf16[720,256]{1,0:T(8,128)(2,1)S(1)}, bf16[720,256]{1,0:T(8,128)(2,1)S(1)}, u32[]{:S(2)}, u32[]{:S(2)}) collective-permute-start(bf16[720,256]{1,0:T(8,128)(2,1)S(1)} %get-tuple-element.198), channel_id=1, source_target_pairs={{0,4},{1,5},{2,6},{3,7},{4,0},{5,1},{6,2},{7,3},{8,12},{9,13},{10,... | collective-permute-start | bytes 1105928 | tf_op jit(solution)/shard_map/ppermute | solution.py:320
  141.1 24.4 %collective-permute-start.45 = (bf16[720,256]{1,0:T(8,128)(2,1)}, bf16[720,256]{1,0:T(8,128)(2,1)}, u32[]{:S(2)}, u32[]{:S(2)}) collective-permute-start(bf16[720,256]{1,0:T(8,128)(2,1)} %add_convert_fusion.2), channel_id=1, source_target_pairs={{0,4},{1,5},{2,6},{3,7},{4,0},{5,1},{6,2},{7,3},{8,12},{9,13},{10,... | collective-permute-start | bytes 1105928 | tf_op jit(solution)/shard_map/ppermute | solution.py:320
  149.7 15.9 %collective-permute-start.44 = (bf16[720,256]{1,0:T(8,128)(2,1)}, bf16[720,256]{1,0:T(8,128)(2,1)}, u32[]{:S(2)}, u32[]{:S(2)}) collective-permute-start(bf16[720,256]{1,0:T(8,128)(2,1)} %add_convert_fusion.3), channel_id=1, source_target_pairs={{0,1},{1,0},{2,3},{3,2},{4,5},{5,4},{6,7},{7,6},{8,9},{9,8},{10,11... | collective-permute-start | bytes 1105928 | tf_op jit(solution)/shard_map/ppermute | solution.py:320
  155.0 10.6 %collective-permute-start.46 = (bf16[368,256]{1,0:T(8,128)(2,1)}, bf16[368,256]{1,0:T(8,128)(2,1)}, u32[]{:S(2)}, u32[]{:S(2)}) collective-permute-start(bf16[368,256]{1,0:T(8,128)(2,1)} %get-tuple-element.215), channel_id=1, source_target_pairs={{0,1},{1,0},{2,3},{3,2},{4,5},{5,4},{6,7},{7,6},{8,9},{9,8},{10,11... | collective-permute-start | bytes 565256 | tf_op jit(solution)/shard_map/ppermute | solution.py:320
  169.8 13.0 %collective-permute-start.53 = (bf16[368,256]{1,0:T(8,128)(2,1)S(1)}, bf16[368,256]{1,0:T(8,128)(2,1)S(1)}, u32[]{:S(2)}, u32[]{:S(2)}) collective-permute-start(bf16[368,256]{1,0:T(8,128)(2,1)S(1)} %add_convert_fusion.7), channel_id=1, source_target_pairs={{0,4},{1,5},{2,6},{3,7},{4,0},{5,1},{6,2},{7,3},{8,12},{9,13},{10,... | collective-permute-start | bytes 565256 | tf_op jit(solution)/shard_map/ppermute | solution.py:320
  (76 other events, 664.5 us)
